TPU v7x, 32 devices: a whole 2x2x4 slice. The times are simulated.
32 devices in a mesh: groups: 2 (over y), seq: 4 (over z), head: 4 (over x, core).
Axes of the slice: x: 2, y: 2, z: 4, core: 2. Of those that a mesh axis runs over, the one named last changes fastest.
Arguments:
- queries: bfloat16 [1024, 2048], P(('groups', 'seq', 'head')), parts along dimension 0, may hold values from -6 to 6
- keys: bfloat16 [1024, 2048], P(('groups', 'seq', 'head')), parts along dimension 0, may hold values from -6 to 6
- values: bfloat16 [1024, 4096], P(('groups', 'seq', 'head')), parts along dimension 0, may hold values from -6 to 6
- cotangent: bfloat16 [1024, 4096], P(('groups', 'seq', 'head')), parts along dimension 0, may hold values from -6 to 6
- igate: float32 [8, 1024], P('head', ('groups', 'seq')), parts along dimension 1, may hold values from -3 to 1
- fgate: float32 [8, 1024], P('head', ('groups', 'seq')), parts along dimension 1, may hold values from 0 to 10
- lengths: int32 [8], P(('groups', 'seq')), parts along dimension 0, may hold values from 1 to 128, 256 in all
Outputs:
- hidden_out: bfloat16 [1024, 4096], P(('groups', 'seq', 'head')), parts along dimension 0
- grad_queries: bfloat16 [1024, 2048], P(('groups', 'seq', 'head')), parts along dimension 0
- grad_keys: bfloat16 [1024, 2048], P(('groups', 'seq', 'head')), parts along dimension 0
- grad_values: bfloat16 [1024, 4096], P(('groups', 'seq', 'head')), parts along dimension 0
- grad_igate: float32 [8, 1024], P('head', ('groups', 'seq')), parts along dimension 1
- grad_fgate: float32 [8, 1024], P('head', ('groups', 'seq')), parts along dimension 1
There are 2 independent parts, one for each index of `groups`. A program takes and returns all parts, laid end to end along the dimension named above; each array names one. Nothing has to cross between parts.
All inputs are finite; a program needn't handle non-finite values. No bound on the sum of `lengths` on one device may be relied on, other than what follows from the above.
Results may differ from a plain program's by a relative error of at most 0.001.
Values may be sent and summed in bfloat16 or wider, within the bound.
No kernel may reach another device: no remote copies, remote signals or barrier semaphores. Data moves between devices by JAX's collectives and lax.ppermute only.
A program may use at most 128 MiB of HBM per device.

v0:
```python
import jax
import jax.numpy as jnp
from jax import lax
from jax.sharding import PartitionSpec as P

BLOCK_ROWS = 64


HIGHEST_PRECISION = lax.Precision.HIGHEST


def swapped(value, axis, distance):
    mask = 2**distance
    pairs = [(source, source ^ mask) for source in range(lax.axis_size(axis))]
    return lax.ppermute(value, axis, pairs)


def product(left, right):
    return jnp.dot(left, right, precision=HIGHEST_PRECISION, preferred_element_type=jnp.float32)


def block_step(carried, block_data):

    def active(operand):
        (memory, norm_state), (q_rows, k_rows, v_rows, in_gate, forget_gate, live_mask) = operand
        block_rows = q_rows.shape[0]
        scaled_keys = k_rows * k_rows.shape[1] ** (-0.5)
        cumulative = jnp.cumsum(jax.nn.log_sigmoid(forget_gate) * live_mask)
        inflow = jnp.exp(in_gate) * live_mask
        causal_mask = jnp.arange(block_rows)[:, None] >= jnp.arange(block_rows)[None, :]
        spread_log = cumulative[:, None] - cumulative[None, :]
        decay_table = jnp.where(causal_mask, jnp.exp(jnp.where(causal_mask, spread_log, 0.0)), 0.0)
        scores = product(q_rows, scaled_keys.T) * decay_table * inflow[None, :]
        front_decay = jnp.exp(cumulative)
        numerator = front_decay[:, None] * product(q_rows, memory) + product(scores, v_rows)
        denominator = front_decay * product(q_rows, norm_state) + jnp.sum(scores, axis=1)
        hidden = numerator / jnp.maximum(jnp.abs(denominator), 1.0)[:, None] * live_mask[:, None]
        tail_weight = jnp.exp(cumulative[-1] - cumulative) * inflow
        memory = front_decay[-1] * memory + product((scaled_keys * tail_weight[:, None]).T, v_rows)
        norm_state = front_decay[-1] * norm_state + product(tail_weight, scaled_keys)
        return ((memory, norm_state), hidden)

    def skipped(operand):
        state_pair, pieces = operand
        return (state_pair, jnp.zeros((pieces[0].shape[0], pieces[2].shape[1]), jnp.float32))

    return lax.cond(block_data[5][0] > 0, active, skipped, (carried, block_data))


def run_scan(q_rows, k_rows, v_rows, in_gate, forget_gate, live_mask, memory, norm_state):
    block_count = q_rows.shape[0] // BLOCK_ROWS

    def to_blocks(tensor):
        return tensor.reshape((block_count, BLOCK_ROWS) + tensor.shape[1:])

    pieces = tuple(
        (to_blocks(tensor) for tensor in (q_rows, k_rows, v_rows, in_gate, forget_gate, live_mask))
    )
    final_state, hidden = lax.scan(block_step, (memory, norm_state), pieces)
    return (hidden.reshape(q_rows.shape[0], v_rows.shape[1]), final_state)


def columns(tensor, head_index, width, offset):
    return tensor[:, offset + head_index * width : offset + (head_index + 1) * width].astype(
        jnp.float32
    )


def place_after(full, piece, axis, start):
    total = full.shape[axis]
    before_shape = full.shape[:axis] + (total,) + full.shape[axis + 1 :]
    after_shape = full.shape[:axis] + (total - piece.shape[axis],) + full.shape[axis + 1 :]
    widened = jnp.concatenate(
        [jnp.zeros(before_shape, piece.dtype), piece, jnp.zeros(after_shape, piece.dtype)],
        axis=axis,
    )
    return full + lax.dynamic_slice_in_dim(widened, total - start, total, axis)


def shards(queries, keys, values, cotangent, igate, fgate, lengths):
    q_all, k_all, v_all, g_all = (
        lax.all_to_all(queries, "head", split_axis=1, concat_axis=0, tiled=True),
        lax.all_to_all(keys, "head", split_axis=1, concat_axis=0, tiled=True),
        lax.all_to_all(values, "head", split_axis=1, concat_axis=0, tiled=True),
        lax.all_to_all(cotangent, "head", split_axis=1, concat_axis=0, tiled=True),
    )
    heads_here = igate.shape[0]
    total_rows = q_all.shape[0]
    slot_rows = total_rows // 2
    qk_width = q_all.shape[1] // heads_here
    v_width = v_all.shape[1] // heads_here
    qk_cols = q_all.shape[1]
    v_cols = v_all.shape[1]
    my_length = lengths[0]
    positions = jnp.arange(total_rows, dtype=jnp.int32)
    slot_positions = jnp.arange(slot_rows, dtype=jnp.int32)
    zero_memory = jnp.zeros((qk_width, v_width), jnp.float32)
    zero_norm = jnp.zeros((qk_width,), jnp.float32)

    def own_forward(kept_rows):
        live_mask = (positions < kept_rows).astype(jnp.float32)

        def forward(q_rows, k_rows, v_rows, in_gate, forget_gate):
            return run_scan(
                q_rows, k_rows, v_rows, in_gate, forget_gate, live_mask, zero_memory, zero_norm
            )

        outputs = []
        for head_index in range(heads_here):
            outputs.append(
                jax.vjp(
                    forward,
                    columns(q_all, head_index, qk_width, 0),
                    columns(k_all, head_index, qk_width, 0),
                    columns(v_all, head_index, v_width, 0),
                    igate[head_index],
                    fgate[head_index],
                )
            )
        return outputs

    swap_bit = lax.axis_size("seq").bit_length() - 2
    peer_length = swapped(lengths, "seq", swap_bit)[0]
    halfway = (my_length + peer_length + 1) // 2
    kept_rows = jnp.where(my_length > peer_length, halfway, my_length)
    incoming = peer_length - jnp.where(peer_length > my_length, halfway, peer_length)
    joined = jnp.concatenate([q_all, k_all, v_all, g_all], axis=1)
    padded = jnp.concatenate(
        [joined, jnp.zeros((slot_rows, joined.shape[1]), joined.dtype)], axis=0
    )
    outgoing = lax.dynamic_slice_in_dim(padded, kept_rows, slot_rows, 0)
    gate_pair = jnp.stack([igate, fgate], axis=0)
    gate_padded = jnp.concatenate(
        [gate_pair, jnp.zeros((2, heads_here, slot_rows), gate_pair.dtype)], axis=2
    )
    gate_out = lax.dynamic_slice_in_dim(gate_padded, kept_rows, slot_rows, 2)
    sent_rows = swapped(outgoing, "seq", swap_bit)
    outputs = own_forward(kept_rows)
    memories = jnp.stack([out[0][1][0] for out in outputs], axis=0)
    norms = jnp.stack([out[0][1][1] for out in outputs], axis=0)
    in_memory, in_norm, in_gates = swapped((memories, norms, gate_out), "seq", swap_bit)
    slot_live = (slot_positions < incoming).astype(jnp.float32)

    def guest_forward(q_rows, k_rows, v_rows, in_gate, forget_gate, memory, norm_state):
        return run_scan(
            q_rows, k_rows, v_rows, in_gate, forget_gate, slot_live, memory, norm_state
        )[0]

    guest_results = []
    for head_index in range(heads_here):
        guest_hidden, guest_pull = jax.vjp(
            guest_forward,
            columns(sent_rows, head_index, qk_width, 0),
            columns(sent_rows, head_index, qk_width, qk_cols),
            columns(sent_rows, head_index, v_width, 2 * qk_cols),
            in_gates[0, head_index],
            in_gates[1, head_index],
            in_memory[head_index],
            in_norm[head_index],
        )
        guest_results.append(
            (guest_hidden,)
            + tuple(guest_pull(columns(sent_rows, head_index, v_width, 2 * qk_cols + v_cols)))
        )
    back_rows = jnp.concatenate(
        [res[0] for res in guest_results]
        + [res[1] for res in guest_results]
        + [res[2] for res in guest_results]
        + [res[3] for res in guest_results],
        axis=1,
    ).astype(jnp.bfloat16)
    back_memory = jnp.stack([res[6] for res in guest_results], axis=0)
    back_norm = jnp.stack([res[7] for res in guest_results], axis=0)
    back_gates = jnp.stack(
        [
            jnp.stack([res[4] for res in guest_results], axis=0),
            jnp.stack([res[5] for res in guest_results], axis=0),
        ],
        axis=0,
    )
    slot_rows_back = swapped(back_rows, "seq", swap_bit)
    memory_grads, norm_grads, slot_gates = swapped(
        (back_memory, back_norm, back_gates), "seq", swap_bit
    )
    pulled = []
    for head_index in range(heads_here):
        grad_rows = columns(g_all, head_index, v_width, 0)
        pulled.append(
            outputs[head_index][1]((grad_rows, (memory_grads[head_index], norm_grads[head_index])))
        )
    hidden_all = jnp.concatenate([out[0][0] for out in outputs], axis=1)
    grad_q = jnp.concatenate([grads[0] for grads in pulled], axis=1)
    grad_k = jnp.concatenate([grads[1] for grads in pulled], axis=1)
    grad_v = jnp.concatenate([grads[2] for grads in pulled], axis=1)
    grad_in = jnp.stack([grads[3] for grads in pulled], axis=0)
    grad_forget = jnp.stack([grads[4] for grads in pulled], axis=0)
    hidden_all, grad_q, grad_k, grad_v, grad_in, grad_forget = (
        hidden_all,
        grad_q,
        grad_k,
        grad_v,
        grad_in,
        grad_forget,
    )
    own_rows = jnp.concatenate([hidden_all, grad_q, grad_k, grad_v], axis=1)
    placed = place_after(own_rows, slot_rows_back.astype(jnp.float32), 0, kept_rows).astype(
        jnp.bfloat16
    )
    hidden_all = placed[:, :v_cols]
    grad_q = placed[:, v_cols : v_cols + qk_cols]
    grad_k = placed[:, v_cols + qk_cols : v_cols + 2 * qk_cols]
    grad_v = placed[:, v_cols + 2 * qk_cols :]
    gates_placed = place_after(jnp.stack([grad_in, grad_forget], axis=0), slot_gates, 2, kept_rows)
    grad_in = gates_placed[0]
    grad_forget = gates_placed[1]
    hidden_rows, grad_q_rows, grad_k_rows, grad_v_rows = (
        lax.all_to_all(hidden_all, "head", split_axis=0, concat_axis=1, tiled=True),
        lax.all_to_all(grad_q, "head", split_axis=0, concat_axis=1, tiled=True),
        lax.all_to_all(grad_k, "head", split_axis=0, concat_axis=1, tiled=True),
        lax.all_to_all(grad_v, "head", split_axis=0, concat_axis=1, tiled=True),
    )
    return (hidden_rows, grad_q_rows, grad_k_rows, grad_v_rows, grad_in, grad_forget)


def solution(mesh):
    return jax.shard_map(
        shards,
        mesh=mesh,
        in_specs=(
            P(("groups", "seq", "head"), None),
            P(("groups", "seq", "head"), None),
            P(("groups", "seq", "head"), None),
            P(("groups", "seq", "head"), None),
            P("head", ("groups", "seq")),
            P("head", ("groups", "seq")),
            P(("groups", "seq")),
        ),
        out_specs=(
            P(("groups", "seq", "head"), None),
            P(("groups", "seq", "head"), None),
            P(("groups", "seq", "head"), None),
            P(("groups", "seq", "head"), None),
            P("head", ("groups", "seq")),
            P("head", ("groups", "seq")),
        ),
        check_vma=False,
    )
```

profile of v0, /device:TPU:8, one launch (start us, length us, event | category | flops | bytes accessed | tf_op | source)
XLA Modules:
  0.0 623.6 jit_solution(12326078671940859908)
XLA Ops:
  26.8 4.6 all-to-all-done.2
  31.3 3.4 all-to-all-start.1
  36.8 4.0 all-to-all-done.1
  40.7 4.0 all-to-all-start.3
  61.6 98.7 %while.21 = (s32[]{:T(128)}, f32[256,512]{1,0:T(8,128)S(1)}, f32[256]{0:T(256)S(1)}, f32[2,64,512]{2,1,0:T(8,128)}, s32[2]{0:T(128)}, /*index=5*/f32[2,64,512]{2...) while((s32[]{:T(128)}, f32[256,512]{1,0:T(8,128)S(1)}, ...), condition=%wide.region_11.13_spmd, body=%wide.region_6.12_spmd.sunk | while | flops 240003776 | bytes 13353463 | solution.py:59
  62.3 26.4 %conditional.17 = (f32[256,512]{1,0:T(8,128)S(1)}, f32[256]{0:T(256)S(1)}, f32[]{:T(128)}, f32[1,64,512]{2,1,0:T(8,128)S(1)}, f32[1,64,512]{2,1,0:T(8,128)}, /*i...) conditional(s32[]{:T(128)} %bitcast.888, ...), branch_computations={%region_7.8_spmd, %region_8.11_spmd} | conditional | flops 240003776 | bytes 5844656 | solution.py:47
  111.7 26.4 %conditional.17 = (f32[256,512]{1,0:T(8,128)S(1)}, f32[256]{0:T(256)S(1)}, f32[]{:T(128)}, f32[1,64,512]{2,1,0:T(8,128)S(1)}, f32[1,64,512]{2,1,0:T(8,128)}, /*i...) conditional(s32[]{:T(128)} %bitcast.888, ...), branch_computations={%region_7.8_spmd, %region_8.11_spmd} | conditional | flops 240003776 | bytes 5844656 | solution.py:47
  181.8 133.7 %while.20 = (s32[]{:T(128)}, f32[256,512]{1,0:T(8,128)S(1)}, f32[256]{0:T(256)S(1)}, f32[2,64,512]{2,1,0:T(8,128)}, s32[2]{0:T(128)}, /*index=5*/f32[2,64,512]{2...) while((s32[]{:T(128)}, f32[256,512]{1,0:T(8,128)S(1)}, ...), condition=%wide.region_5.7_spmd, body=%wide.region_0.6_spmd.sunk | while | flops 240003776 | bytes 13961975 | solution.py:59
  182.5 29.6 %conditional.16 = (f32[256,512]{1,0:T(8,128)S(1)}, f32[256]{0:T(256)S(1)}, f32[]{:T(128)}, f32[1,64,512]{2,1,0:T(8,128)S(1)}, f32[1,64,512]{2,1,0:T(8,128)}, /*i...) conditional(s32[]{:T(128)} %bitcast.884, ...), branch_computations={%region_1.1_spmd, %region_2.5_spmd} | conditional | flops 240003776 | bytes 6370024 | solution.py:47
  249.4 29.6 %conditional.16 = (f32[256,512]{1,0:T(8,128)S(1)}, f32[256]{0:T(256)S(1)}, f32[]{:T(128)}, f32[1,64,512]{2,1,0:T(8,128)S(1)}, f32[1,64,512]{2,1,0:T(8,128)}, /*i...) conditional(s32[]{:T(128)} %bitcast.884, ...), branch_computations={%region_1.1_spmd, %region_2.5_spmd} | conditional | flops 240003776 | bytes 6370024 | solution.py:47
  328.3 23.6 %collective-permute-done.3 = bf16[64,3072]{1,0:T(8,128)(2,1)} collective-permute-done((bf16[64,3072]{1,0:T(8,128)(2,1)}, bf16[64,3072]{1,0:T(8,128)(2,1)}, u32[]{:S(2)}, u32[]{:S(2)}) %collective-permute-start.3) | collective-permute-done | bytes 393248 | tf_op jit(solution)/shard_map/ppermute | solution.py:15
  354.3 4.8 conditional.8
  362.7 4.6 conditional.10
  371.5 60.3 %collective-permute-start.6 = (f32[2,256]{1,0:T(2,128)S(1)}, f32[2,256]{1,0:T(2,128)S(1)}, u32[]{:S(2)}, u32[]{:S(2)}) collective-permute-start(f32[2,256]{1,0:T(2,128)S(1)} %pad_maximum_fusion.3), channel_id=1, source_target_pairs={{0,8},{4,12},{8,0},{12,4},{1,9},{5,13},{9,1},{13,5},{2,10},{6,14},... | collective-permute-start | bytes 6152 | tf_op jit(solution)/shard_map/ppermute | solution.py:15
  441.0 25.5 %collective-permute-done.7 = bf16[64,3072]{1,0:T(8,128)(2,1)S(1)} collective-permute-done((bf16[64,3072]{1,0:T(8,128)(2,1)S(1)}, bf16[64,3072]{1,0:T(8,128)(2,1)S(1)}, u32[]{:S(2)}, u32[]{:S(2)}) %collective-permute-start.7) | collective-permute-done | bytes 393248 | tf_op jit(solution)/shard_map/ppermute | solution.py:15
  470.7 55.7 %while.23 = (s32[]{:T(128)}, f32[256,512]{1,0:T(8,128)S(1)}, f32[256]{0:T(256)S(1)}, f32[2,64,256]{2,1,0:T(8,128)}, f32[2,64,256]{2,1,0:T(8,128)}, /*index=5*/f3...) while((s32[]{:T(128)}, f32[256,512]{1,0:T(8,128)S(1)}, ...), condition=%wide.region_71.73_spmd, body=%wide.region_58.72_spmd.sunk | while | flops 479886144 | bytes 12494605 | solution.py:59
  472.0 21.9 %conditional.19 = (f32[256,512]{1,0:T(8,128)S(1)}, f32[256]{0:T(256)S(1)}, f32[1,64,256]{2,1,0:T(8,128)S(1)}, f32[1,64,256]{2,1,0:T(8,128)}, f32[1,64,512]{2,1,0...) conditional(s32[]{:T(128)} %bitcast.891, (f32[256,512]{1,0:T(8,128)S(1)}, f32[256]{0:T(256)S(1)}) %tuple.646, ...), branch_computations={%region_59.60_spmd, %region_60.71_spmd} | conditional | flops 479886144 | bytes 11967560 | solution.py:47
  499.9 21.9 %conditional.19 = (f32[256,512]{1,0:T(8,128)S(1)}, f32[256]{0:T(256)S(1)}, f32[1,64,256]{2,1,0:T(8,128)S(1)}, f32[1,64,256]{2,1,0:T(8,128)}, f32[1,64,512]{2,1,0...) conditional(s32[]{:T(128)} %bitcast.891, (f32[256,512]{1,0:T(8,128)S(1)}, f32[256]{0:T(256)S(1)}) %tuple.646, ...), branch_computations={%region_59.60_spmd, %region_60.71_spmd} | conditional | flops 479886144 | bytes 11967560 | solution.py:47
  529.6 46.0 %while.22 = (s32[]{:T(128)}, f32[256,512]{1,0:T(8,128)S(1)}, f32[256]{0:T(256)S(1)}, f32[2,64,256]{2,1,0:T(8,128)}, f32[2,64,256]{2,1,0:T(8,128)}, /*index=5*/f3...) while((s32[]{:T(128)}, f32[256,512]{1,0:T(8,128)S(1)}, ...), condition=%wide.region_57.59_spmd, body=%wide.region_44.58_spmd.sunk | while | flops 479886144 | bytes 12946077 | solution.py:59
  530.8 17.9 %conditional.18 = (f32[256,512]{1,0:T(8,128)S(1)}, f32[256]{0:T(256)S(1)}, f32[1,64,256]{2,1,0:T(8,128)S(1)}, f32[1,64,256]{2,1,0:T(8,128)S(1)}, f32[1,64,512]{2...) conditional(s32[]{:T(128)} %bitcast.890, (f32[256,512]{1,0:T(8,128)S(1)}, f32[256]{0:T(256)S(1)}) %tuple.642, ...), branch_computations={%region_45.46_spmd, %region_46.57_spmd} | conditional | flops 479886144 | bytes 12419032 | solution.py:47
  553.8 18.0 %conditional.18 = (f32[256,512]{1,0:T(8,128)S(1)}, f32[256]{0:T(256)S(1)}, f32[1,64,256]{2,1,0:T(8,128)S(1)}, f32[1,64,256]{2,1,0:T(8,128)S(1)}, f32[1,64,512]{2...) conditional(s32[]{:T(128)} %bitcast.890, (f32[256,512]{1,0:T(8,128)S(1)}, f32[256]{0:T(256)S(1)}) %tuple.642, ...), branch_computations={%region_45.46_spmd, %region_46.57_spmd} | conditional | flops 479886144 | bytes 12419032 | solution.py:47
  591.6 4.6 all-to-all-done.5
  599.5 4.6 all-to-all-done.6
  608.3 5.2 all-to-all-done.4
  (1053 shorter events, 476.9 us)
Async XLA Ops:
  0.6 18.8 %copy-start.129 = (f32[2,128]{1,0:T(2,128)S(1)}, f32[2,128]{1,0:T(2,128)}, u32[]{:S(2)}) copy-start(f32[2,128]{1,0:T(2,128)} %param.36) | copy-start | bytes 3076
  0.6 18.8 %copy-start.130 = (f32[2,128]{1,0:T(2,128)S(1)}, f32[2,128]{1,0:T(2,128)}, u32[]{:S(2)}) copy-start(f32[2,128]{1,0:T(2,128)} %param.37) | copy-start | bytes 3076
  0.7 17.0 %collective-permute-start = (s32[1]{0:T(128)}, s32[1]{0:T(128)}, u32[]{:S(2)}, u32[]{:S(2)}) collective-permute-start(s32[1]{0:T(128)} %param.38), channel_id=1, source_target_pairs={{0,8},{4,12},{8,0},{12,4},{1,9},{5,13},{9,1},{13,5},{2,10},{6,14},... | collective-permute-start | bytes 20 | tf_op jit(solution)/shard_map/ppermute | solution.py:15
  4.9 18.5 %all-to-all-start = ((bf16[32,4,512]{2,0,1:T(8,128)(2,1)}), bf16[32,4,512]{2,0,1:T(8,128)(2,1)S(1)}, u32[]{:S(2)}, u32[]{:S(2)}) async-start(bf16[32,4,512]{2,0,1:T(8,128)(2,1)} %bitcast.868), calls=%async_computation | async-start | bytes 262144 | tf_op jit(solution)/shard_map/all_to_all | solution.py:83
  20.1 333.6 %collective-permute-start.1 = (f32[2,2,64]{2,1,0:T(2,128)}, f32[2,2,64]{2,1,0:T(2,128)}, u32[]{:S(2)}, u32[]{:S(2)}) collective-permute-start(f32[2,2,64]{2,1,0:T(2,128)} %fusion.275), channel_id=1, source_target_pairs={{0,8},{4,12},{8,0},{12,4},{1,9},{5,13},{9,1},{13,5},{2,10},{6,14},... | collective-permute-start | bytes 3080 | tf_op jit(solution)/shard_map/ppermute | solution.py:15
  23.4 22.1 %copy-start.29 = (bf16[32,4,512]{2,0,1:T(8,128)(2,1)}, bf16[32,4,512]{2,0,1:T(8,128)(2,1)S(1)}, u32[]{:S(2)}) copy-start(bf16[32,4,512]{2,0,1:T(8,128)(2,1)S(1)} %all-to-all-done) | copy-start | bytes 393220
  23.4 7.9 %all-to-all-start.2 = ((bf16[32,4,512]{2,0,1:T(8,128)(2,1)}), bf16[32,4,512]{2,0,1:T(8,128)(2,1)S(1)}, u32[]{:S(2)}, u32[]{:S(2)}) async-start(bf16[32,4,512]{2,0,1:T(8,128)(2,1)} %bitcast.867), calls=%async_computation.2 | async-start | bytes 262144 | tf_op jit(solution)/shard_map/all_to_all | solution.py:82
  31.3 9.4 %all-to-all-start.1 = ((bf16[32,4,1024]{2,0,1:T(8,128)(2,1)}), bf16[32,4,1024]{2,0,1:T(8,128)(2,1)S(1)}, u32[]{:S(2)}, u32[]{:S(2)}) async-start(bf16[32,4,1024]{2,0,1:T(8,128)(2,1)} %bitcast.866), calls=%async_computation.1 | async-start | bytes 524288 | tf_op jit(solution)/shard_map/all_to_all | solution.py:84
  40.7 278.9 %all-to-all-start.3 = ((bf16[32,4,1024]{2,0,1:T(8,128)(2,1)}), bf16[32,4,1024]{2,0,1:T(8,128)(2,1)}, u32[]{:S(2)}, u32[]{:S(2)}) async-start(bf16[32,4,1024]{2,0,1:T(8,128)(2,1)} %bitcast.865), calls=%async_computation.3 | async-start | bytes 524288 | tf_op jit(solution)/shard_map/all_to_all | solution.py:85
  92.4 15.9 %copy-start.103 = (pred[1,64]{1,0:T(4,128)(4,1)S(1)}, pred[1,64]{1,0:T(4,128)(4,1)}, u32[]{:S(2)}) copy-start(pred[1,64]{1,0:T(4,128)(4,1)} %copy-done.102) | copy-start | bytes 196 | tf_op jit(solution)/shard_map/jvp()/while
  141.8 16.0 %copy-start.103 = (pred[1,64]{1,0:T(4,128)(4,1)S(1)}, pred[1,64]{1,0:T(4,128)(4,1)}, u32[]{:S(2)}) copy-start(pred[1,64]{1,0:T(4,128)(4,1)} %copy-done.102) | copy-start | bytes 196 | tf_op jit(solution)/shard_map/jvp()/while
  316.6 37.1 %collective-permute-start.2 = (f32[2,256,512]{2,1,0:T(8,128)}, f32[2,256,512]{2,1,0:T(8,128)}, u32[]{:S(2)}, u32[]{:S(2)}) collective-permute-start(f32[2,256,512]{2,1,0:T(8,128)} %pad_maximum_fusion), channel_id=1, source_target_pairs={{0,8},{4,12},{8,0},{12,4},{1,9},{5,13},{9,1},{13,5},{2,10},{6,14},... | collective-permute-start | bytes 3145736 | tf_op jit(solution)/shard_map/ppermute | solution.py:15
  316.7 37.0 %collective-permute-start.4 = (f32[2,256]{1,0:T(2,128)S(1)}, f32[2,256]{1,0:T(2,128)S(1)}, u32[]{:S(2)}, u32[]{:S(2)}) collective-permute-start(f32[2,256]{1,0:T(2,128)S(1)} %pad_maximum_fusion.2), channel_id=1, source_target_pairs={{0,8},{4,12},{8,0},{12,4},{1,9},{5,13},{9,1},{13,5},{2,10},{6,14},... | collective-permute-start | bytes 6152 | tf_op jit(solution)/shard_map/ppermute | solution.py:15
  322.3 29.6 %collective-permute-start.3 = (bf16[64,3072]{1,0:T(8,128)(2,1)}, bf16[64,3072]{1,0:T(8,128)(2,1)}, u32[]{:S(2)}, u32[]{:S(2)}) collective-permute-start(bf16[64,3072]{1,0:T(8,128)(2,1)} %fusion.270), channel_id=1, source_target_pairs={{0,8},{4,12},{8,0},{12,4},{1,9},{5,13},{9,1},{13,5},{2,10},{6,14},... | collective-permute-start | bytes 1179656 | tf_op jit(solution)/shard_map/ppermute | solution.py:15
  326.6 27.7 %copy-start.86 = (f32[64]{0:T(128)S(1)}, f32[64]{0:T(128)}, u32[]{:S(2)}) copy-start(f32[64]{0:T(128)} %copy-done.85) | copy-start | bytes 772
  328.3 23.6 %copy-start.28 = (f32[128,3072]{1,0:T(8,128)}, f32[128,3072]{1,0:T(8,128)S(1)}, u32[]{:S(2)}) copy-start(f32[128,3072]{1,0:T(8,128)S(1)} %constant_dynamic-update-slice_fusion.54) | copy-start | bytes 4718596
  371.5 69.4 %collective-permute-start.6 = (f32[2,256]{1,0:T(2,128)S(1)}, f32[2,256]{1,0:T(2,128)S(1)}, u32[]{:S(2)}, u32[]{:S(2)}) collective-permute-start(f32[2,256]{1,0:T(2,128)S(1)} %pad_maximum_fusion.3), channel_id=1, source_target_pairs={{0,8},{4,12},{8,0},{12,4},{1,9},{5,13},{9,1},{13,5},{2,10},{6,14},... | collective-permute-start | bytes 6152 | tf_op jit(solution)/shard_map/ppermute | solution.py:15
  432.4 35.1 %collective-permute-start.5 = (f32[2,256,512]{2,1,0:T(8,128)S(1)}, f32[2,256,512]{2,1,0:T(8,128)S(1)}, u32[]{:S(2)}, u32[]{:S(2)}) collective-permute-start(f32[2,256,512]{2,1,0:T(8,128)S(1)} %pad_maximum_fusion.1), channel_id=1, source_target_pairs={{0,8},{4,12},{8,0},{12,4},{1,9},{5,13},{9,1},{13,5},{2,10},{6,14},... | collective-permute-start | bytes 3145736 | tf_op jit(solution)/shard_map/ppermute | solution.py:15
  436.0 30.5 %collective-permute-start.7 = (bf16[64,3072]{1,0:T(8,128)(2,1)S(1)}, bf16[64,3072]{1,0:T(8,128)(2,1)S(1)}, u32[]{:S(2)}, u32[]{:S(2)}) collective-permute-start(bf16[64,3072]{1,0:T(8,128)(2,1)S(1)} %constant_dynamic-update-slice_fusion.56), channel_id=1, source_target_pairs={{0,8},{4,12},{8,0},{12,4},{1,9},{5,13},{9,1},{13,5},{2,10},{6,14},... | collective-permute-start | bytes 1179656 | tf_op jit(solution)/shard_map/ppermute | solution.py:15
  440.5 167.0 %collective-permute-start.8 = (f32[2,2,64]{2,1,0:T(2,128)}, f32[2,2,64]{2,1,0:T(2,128)}, u32[]{:S(2)}, u32[]{:S(2)}) collective-permute-start(f32[2,2,64]{2,1,0:T(2,128)} %pad_maximum_fusion.4), channel_id=1, source_target_pairs={{0,8},{4,12},{8,0},{12,4},{1,9},{5,13},{9,1},{13,5},{2,10},{6,14},... | collective-permute-start | bytes 3080 | tf_op jit(solution)/shard_map/ppermute | solution.py:15
  588.2 7.9 %all-to-all-start.5 = ((bf16[4,32,512]{2,1,0:T(8,128)(2,1)}), bf16[4,32,512]{2,1,0:T(8,128)(2,1)S(1)}, u32[]{:S(2)}, u32[]{:S(2)}) async-start(bf16[4,32,512]{2,1,0:T(8,128)(2,1)} %bitcast.291), calls=%async_computation.5 | async-start | bytes 262144 | tf_op jit(solution)/shard_map/all_to_all | solution.py:218
  596.1 7.9 %all-to-all-start.6 = ((bf16[4,32,512]{2,1,0:T(8,128)(2,1)}), bf16[4,32,512]{2,1,0:T(8,128)(2,1)S(1)}, u32[]{:S(2)}, u32[]{:S(2)}) async-start(bf16[4,32,512]{2,1,0:T(8,128)(2,1)} %bitcast.293), calls=%async_computation.6 | async-start | bytes 262144 | tf_op jit(solution)/shard_map/all_to_all | solution.py:219
  604.1 9.4 %all-to-all-start.4 = ((bf16[4,32,1024]{2,1,0:T(8,128)(2,1)}), bf16[4,32,1024]{2,1,0:T(8,128)(2,1)S(1)}, u32[]{:S(2)}, u32[]{:S(2)}) async-start(bf16[4,32,1024]{2,1,0:T(8,128)(2,1)} %bitcast.289), calls=%async_computation.4 | async-start | bytes 524288 | tf_op jit(solution)/shard_map/all_to_all | solution.py:217
  613.5 9.4 %all-to-all-start.7 = ((bf16[4,32,1024]{2,1,0:T(8,128)(2,1)}), bf16[4,32,1024]{2,1,0:T(8,128)(2,1)S(1)}, u32[]{:S(2)}, u32[]{:S(2)}) async-start(bf16[4,32,1024]{2,1,0:T(8,128)(2,1)} %bitcast.295), calls=%async_computation.7 | async-start | bytes 524288 | tf_op jit(solution)/shard_map/all_to_all | solution.py:220
  (199 other events, 972.7 us)
where the time goes:
time: 632 us; the launch traced here: 624 us
  local copies, waits for them, and re-layouts  260 us (41%)
  starting transfers between devices  97 us (15%)
  other arithmetic  96.6 us (15%)
  matrix products  82.1 us (13%)
  waiting for transfers between devices  75.4 us (12%)
  loops' own time  8.06 us (1%)
    dynamic_update_slice x132, local copies, waits for them, and re-layouts, run_scan(): final_state, hidden = lax.scan(block_step, (memory, norm_state), pieces)  127 us
    dot_general x64, matrix products, product(): jnp.dot(left, right, precision=HIGHEST_PRECISION, preferred_element_type=...  82.1 us
    ppermute x9, starting transfers between devices, swapped(): return lax.ppermute(value, axis, pairs)  69.4 us
    another operation x158, local copies, waits for them, and re-layouts  53.7 us
    ppermute x9, waiting for transfers between devices, swapped(): return lax.ppermute(value, axis, pairs)  49.1 us
    broadcast_in_dim x28, other arithmetic, run_scan(): final_state, hidden = lax.scan(block_step, (memory, norm_state), pieces)  19.8 us
    unnamed x98, local copies, waits for them, and re-layouts  14.2 us
    dynamic_slice x20, local copies, waits for them, and re-layouts, run_scan(): final_state, hidden = lax.scan(block_step, (memory, norm_state), pieces)  13.1 us
  transfers between devices with their start and end apart: 17, of which 8 were waited for; matrix products, arithmetic and copies ran while one was open for 66% of the time, Pallas kernels for 0%

commit v1 on v0

v1 whole, which is shorter than its diff:
```python
import functools

import jax
import jax.numpy as jnp
from jax import lax
from jax.experimental import pallas as pl
from jax.experimental.pallas import tpu as pltpu
from jax.sharding import PartitionSpec as P

FAR = -1e30


def dot(left, right, contract):
    return lax.dot_general(left, right, (contract, ((), ())), preferred_element_type=jnp.float32)


def halves(value):
    high = value.astype(jnp.bfloat16)
    return high, (value - high.astype(jnp.float32)).astype(jnp.bfloat16)


def wide_dot(left, right, contract):
    high, low = halves(left)
    return dot(high, right, contract) + dot(low, right, contract)


NN = ((1,), (0,))
NT = ((1,), (1,))
TN = ((0,), (0,))


def log_sigmoid(value):
    return jnp.minimum(value, 0.0) - jnp.log(1.0 + jnp.exp(-jnp.abs(value)))


def decay(in_gate, forget_gate, length, scale):
    size = in_gate.shape[1]
    rows = lax.broadcasted_iota(jnp.int32, (size, size), 0)
    cols = lax.broadcasted_iota(jnp.int32, (size, size), 1)
    logs = jnp.where(cols[:1] < length, log_sigmoid(forget_gate), 0.0)
    total_col = jnp.sum(jnp.where(cols <= rows, logs, 0.0), axis=1, keepdims=True)
    total_row = jnp.sum(jnp.where(cols == rows, total_col, 0.0), axis=0, keepdims=True)
    mask = (cols <= rows) & (rows < length)
    return jnp.exp(jnp.where(mask, total_col - total_row, FAR)) * (jnp.exp(in_gate) * scale)


def whole_kernel(heads, qk, vw, length_ref, x_ref, ig_ref, fg_ref, out_ref, gi_ref, gf_ref):
    length = length_ref[0]
    size = x_ref.shape[0]
    rows = lax.broadcasted_iota(jnp.int32, (size, size), 0)
    cols = lax.broadcasted_iota(jnp.int32, (size, size), 1)
    for head in range(heads):
        q = x_ref[:, head * qk : (head + 1) * qk]
        k = x_ref[:, (heads + head) * qk : (heads + head + 1) * qk]
        v0 = 2 * heads * qk + head * vw
        g0 = v0 + heads * vw
        v = x_ref[:, v0 : v0 + vw]
        g = x_ref[:, g0 : g0 + vw]
        forget = fg_ref[head : head + 1, :]
        weight = decay(ig_ref[head : head + 1, :], forget, length, qk**-0.5)
        scores = dot(q, k, NT) * weight
        pulled = dot(g, v, NT)
        norm = jnp.sum(scores, axis=1, keepdims=True)
        along = jnp.sum(scores * pulled, axis=1, keepdims=True)
        size_of = jnp.abs(norm)
        inverse = 1.0 / jnp.maximum(size_of, 1.0)
        share = jnp.where(size_of > 1.0, 1.0, jnp.where(size_of == 1.0, 0.5, 0.0))
        grad_norm = -along * inverse * inverse * share * jnp.where(norm < 0.0, -1.0, 1.0)
        grad_scores = pulled * inverse + grad_norm
        hidden = wide_dot(scores * inverse, v, NN)
        grad_raw = grad_scores * weight
        gq = wide_dot(grad_raw, k, NN)
        gk = wide_dot(grad_raw.T, q, NN)
        gv = wide_dot((scores * inverse).T, g, NN)
        out_ref[:, head * qk : (head + 1) * qk] = gq.astype(jnp.bfloat16)
        out_ref[:, (heads + head) * qk : (heads + head + 1) * qk] = gk.astype(jnp.bfloat16)
        out_ref[:, v0 : v0 + vw] = gv.astype(jnp.bfloat16)
        out_ref[:, g0 : g0 + vw] = hidden.astype(jnp.bfloat16)
        by_column = jnp.sum(grad_scores * scores, axis=0, keepdims=True)
        by_row = along * inverse * (1.0 - share)
        moved = by_row - jnp.sum(jnp.where(rows == cols, by_column, 0.0), axis=1, keepdims=True)
        grad_log = jnp.sum(jnp.where(rows >= cols, moved, 0.0), axis=0, keepdims=True)
        gi_ref[head : head + 1, :] = by_column
        gf_ref[head : head + 1, :] = jnp.where(
            cols[:1] < length, grad_log / (1.0 + jnp.exp(forget)), 0.0
        )


def shards(queries, keys, values, cotangent, igate, fgate, lengths):
    devices = lax.axis_size("head")
    rows = queries.shape[0]
    heads = igate.shape[0]
    qk = queries.shape[1] // (devices * heads)
    vw = values.shape[1] // (devices * heads)
    parts = [a.reshape(rows, devices, -1) for a in (queries, keys, values, cotangent)]
    joined = jnp.concatenate(parts, axis=2)
    here = lax.all_to_all(joined, "head", split_axis=1, concat_axis=0, tiled=True)
    here = here.reshape(rows * devices, -1)
    vmem = pl.BlockSpec(memory_space=pltpu.VMEM)
    out, grad_in, grad_forget = pl.pallas_call(
        functools.partial(whole_kernel, heads, qk, vw),
        out_shape=(
            jax.ShapeDtypeStruct(here.shape, jnp.bfloat16),
            jax.ShapeDtypeStruct(igate.shape, jnp.float32),
            jax.ShapeDtypeStruct(igate.shape, jnp.float32),
        ),
        in_specs=[pl.BlockSpec(memory_space=pltpu.SMEM), vmem, vmem, vmem],
        out_specs=(vmem, vmem, vmem),
        compiler_params=pltpu.CompilerParams(vmem_limit_bytes=32 * 1024 * 1024),
    )(lengths, here, igate, fgate)
    back = lax.all_to_all(
        out.reshape(devices, rows, -1), "head", split_axis=0, concat_axis=0, tiled=True
    )
    back = back.transpose(1, 0, 2)
    ends = [0, heads * qk, 2 * heads * qk, 2 * heads * qk + heads * vw, back.shape[2]]
    gq, gk, gv, hidden = [
        back[:, :, a:b].reshape(rows, -1) for a, b in zip(ends[:-1], ends[1:])
    ]
    return hidden, gq, gk, gv, grad_in, grad_forget


def solution(mesh):
    rows = P(("groups", "seq", "head"), None)
    gates = P("head", ("groups", "seq"))
    return jax.shard_map(
        shards,
        mesh=mesh,
        in_specs=(rows, rows, rows, rows, gates, gates, P(("groups", "seq"))),
        out_specs=(rows, rows, rows, rows, gates, gates),
        check_vma=False,
    )
```

time: 632 us -> 38.3 us (0.06)
  the two profiles are of different devices: /device:TPU:8 before, /device:TPU:0 now
where the time goes in v1:
time: 38.3 us; the launch traced here: 38 us
  blocking collectives  14.1 us (37%)
  waiting for transfers between devices  11 us (29%)
  local copies, waits for them, and re-layouts  4.88 us (13%)
  starting transfers between devices  4.34 us (11%)
  Pallas kernels  1.48 us (4%)
  between operations  1.31 us (3%)
  other arithmetic  0.95 us (2%)
    all_to_all x1, blocking collectives, shards(): lax.all_to_all(out.reshape(devices, rows, -1), 'head', split_axis=0, conc...  14.1 us
    all_to_all x1, waiting for transfers between devices, shards(): lax.all_to_all(joined, 'head', split_axis=1, concat_axis=0, tiled=True)  11 us
    all_to_all x1, starting transfers between devices, shards(): lax.all_to_all(joined, 'head', split_axis=1, concat_axis=0, tiled=True)  4.34 us
    reshape x4, local copies, waits for them, and re-layouts, shards(): back[:, :, a:b].reshape(rows, -1)  2.77 us
    reshape x2, local copies, waits for them, and re-layouts, shards(): a.reshape(rows, devices, -1)  2.05 us
    pallas_call x1, Pallas kernels, shards(): pl.pallas_call(functools.partial(whole_kernel, heads, qk, vw), out_shape=...  1.48 us
    concatenate x1, other arithmetic, shards(): joined = jnp.concatenate(parts, axis=2)  0.95 us
  transfers between devices with their start and end apart: 1, of which 1 were waited for; matrix products, arithmetic and copies ran while one was open for 0% of the time, Pallas kernels for 0%

profile of v1, /device:TPU:0, one launch (start us, length us, event | category | flops | bytes accessed | tf_op | source)
XLA Modules:
  0.0 38.0 jit_solution(7820230762065522673)
XLA Ops:
  0.6 1.0 %copy_bitcast_fusion.2 = (bf16[32,4,512]{2,0,1:T(8,128)(2,1)S(1)}, bf16[32,4,512]{2,0,1:T(8,128)(2,1)S(1)}) fusion(bf16[4,4,8,512]{3,2,1,0:T(8,128)(2,1)} %bitcast.41, bf16[4,4,8,512]{3,2,1,0:T(8,128)(2,1)} %bitcast.42), kind=kLoop, calls=%fused_computation.5 | loop fusion | bytes 524288 | tf_op jit(solution)/shard_map/reshape | solution.py:95
  1.6 1.1 %copy_bitcast_fusion = (bf16[32,4,1024]{2,0,1:T(8,128)(2,1)S(1)}, bf16[32,4,1024]{2,0,1:T(8,128)(2,1)S(1)}) fusion(bf16[4,4,8,1024]{3,2,1,0:T(8,128)(2,1)} %bitcast.37, bf16[4,4,8,1024]{3,2,1,0:T(8,128)(2,1)} %bitcast.38), kind=kLoop, calls=%fused_computation.1 | loop fusion | bytes 1048576 | tf_op jit(solution)/shard_map/reshape | solution.py:95
  2.7 1.0 %pad_maximum_fusion = bf16[32,4,3072]{2,0,1:T(8,128)(2,1)} fusion(bf16[32,4,1024]{2,0,1:T(8,128)(2,1)S(1)} %get-tuple-element.16, bf16[32,4,1024]{2,0,1:T(8,128)(2,1)S(1)} %get-tuple-element.17, bf16[32,4,512]{2,0,1:T(8,128)(2,1)S(1)} %get-tuple-element.18, bf16[32,4,512]{2,0,1:T(8,128)(2,1)S(1)} %get-tuple-element.19), kind=kLoop, calls=%fused_computation | loop fusion | flops 3145728 | bytes 1572864 | tf_op jit(solution)/shard_map/concatenate | solution.py:96
  3.6 0.0 copy-start
  3.7 0.0 copy-start.1
  3.7 4.3 %all-to-all-start = ((bf16[32,4,3072]{2,0,1:T(8,128)(2,1)}), bf16[32,4,3072]{2,0,1:T(8,128)(2,1)S(1)}, u32[]{:S(2)}, u32[]{:S(2)}) async-start(bf16[32,4,3072]{2,0,1:T(8,128)(2,1)} %pad_maximum_fusion), calls=%async_computation | async-start | bytes 1572864 | tf_op jit(solution)/shard_map/all_to_all | solution.py:97
  8.6 11.0 %all-to-all-done = bf16[32,4,3072]{2,0,1:T(8,128)(2,1)S(1)} async-done(((bf16[32,4,3072]{2,0,1:T(8,128)(2,1)}), bf16[32,4,3072]{2,0,1:T(8,128)(2,1)S(1)}, u32[]{:S(2)}, u32[]{:S(2)}) %all-to-all-start) | async-done | bytes 786464 | tf_op jit(solution)/shard_map/all_to_all | solution.py:97
  19.6 0.0 copy-done
  19.7 0.0 copy-done.1
  19.7 1.5 %shard_map.118 = (bf16[128,3072]{1,0:T(8,128)(2,1)S(1)}, f32[2,128]{1,0:T(2,128)}, f32[2,128]{1,0:T(2,128)}) custom-call(s32[1]{0:T(128)S(6)} %copy.33.length_ref, bf16[128,3072]{1,0:T(8,128)(2,1)S(1)} %bitcast.31, f32[2,128]{1,0:T(2,128)S(1)} %copy-done, f32[2,128]{1,0:T(2,128)S(1)} %copy-done.1), custom_call_target="tpu_custom_call" | custom-call | tf_op jit(solution)/shard_map/pallas_call | solution.py:100
  21.1 14.1 %all_to_all.20 = bf16[4,32,3072]{2,1,0:T(8,128)(2,1)S(1)} all-to-all(bf16[4,32,3072]{2,1,0:T(8,128)(2,1)S(1)} %bitcast.32), channel_id=1, replica_groups=mesh['groups'=2,'seq'=4,'head'=4] {'head'}, dimensions={0} | all-to-all | bytes 1572864 | tf_op jit(solution)/shard_map/all_to_all | solution.py:111
  35.3 0.7 %copy.28 = bf16[4,4,8,1024]{3,2,0,1:T(8,128)(2,1)} copy(bf16[4,4,8,1024]{3,2,1,0:T(8,128)(2,1)S(1)} %get-tuple-element.12) | data formatting | bytes 524288 | tf_op jit(solution)/shard_map/reshape | solution.py:117
  36.0 0.7 %copy.27 = bf16[4,4,8,512]{3,2,0,1:T(8,128)(2,1)} copy(bf16[4,4,8,512]{3,2,1,0:T(8,128)(2,1)S(1)} %get-tuple-element.14) | data formatting | bytes 262144 | tf_op jit(solution)/shard_map/reshape | solution.py:117
  36.6 0.7 %copy.26 = bf16[4,4,8,512]{3,2,0,1:T(8,128)(2,1)} copy(bf16[4,4,8,512]{3,2,1,0:T(8,128)(2,1)S(1)} %get-tuple-element.15) | data formatting | bytes 262144 | tf_op jit(solution)/shard_map/reshape | solution.py:117
  37.3 0.7 %copy.25 = bf16[4,4,8,1024]{3,2,0,1:T(8,128)(2,1)} copy(bf16[4,4,8,1024]{3,2,1,0:T(8,128)(2,1)S(1)} %get-tuple-element.13) | data formatting | bytes 524288 | tf_op jit(solution)/shard_map/reshape | solution.py:117
  (2 shorter events, 0.1 us)
Async XLA Ops:
  3.6 16.0 %copy-start = (f32[2,128]{1,0:T(2,128)S(1)}, f32[2,128]{1,0:T(2,128)}, u32[]{:S(2)}) copy-start(f32[2,128]{1,0:T(2,128)} %ig_ref.1) | copy-start | bytes 3076
  3.7 16.0 %copy-start.1 = (f32[2,128]{1,0:T(2,128)S(1)}, f32[2,128]{1,0:T(2,128)}, u32[]{:S(2)}) copy-start(f32[2,128]{1,0:T(2,128)} %fg_ref.1) | copy-start | bytes 3076
  3.7 16.0 %all-to-all-start = ((bf16[32,4,3072]{2,0,1:T(8,128)(2,1)}), bf16[32,4,3072]{2,0,1:T(8,128)(2,1)S(1)}, u32[]{:S(2)}, u32[]{:S(2)}) async-start(bf16[32,4,3072]{2,0,1:T(8,128)(2,1)} %pad_maximum_fusion), calls=%async_computation | async-start | bytes 1572864 | tf_op jit(solution)/shard_map/all_to_all | solution.py:97

commit v2 on v1

--- a/solution.py
+++ b/solution.py
@@ -86,7 +86,7 @@
         )
 
 
-def shards(queries, keys, values, cotangent, igate, fgate, lengths):
+def swapped_shards(queries, keys, values, cotangent, igate, fgate, lengths):
     devices = lax.axis_size("head")
     rows = queries.shape[0]
     heads = igate.shape[0]
@@ -119,6 +119,353 @@
     return hidden, gq, gk, gv, grad_in, grad_forget
 
 
+def backward_terms(norm, along):
+    size = jnp.abs(norm)
+    inverse = 1.0 / jnp.maximum(size, 1.0)
+    share = jnp.where(size > 1.0, 1.0, jnp.where(size == 1.0, 0.5, 0.0))
+    grad_norm = -along * inverse * inverse * share * jnp.where(norm < 0.0, -1.0, 1.0)
+    return inverse, grad_norm, along * inverse * (1.0 - share)
+
+
+def place():
+    me = lax.axis_index("head")
+    return me // 2, lax.rem(me, 2)
+
+
+def run_copies(pairs, sems):
+    copies = [pltpu.make_async_copy(a, b, sems.at[i]) for i, (a, b) in enumerate(pairs)]
+    for copy in copies:
+        copy.start()
+    return copies
+
+
+def pack_kernel(q_ref, k_ref, v_ref, g_ref, ig_ref, fg_ref, m1_ref, a2_ref, a3_ref, b2_ref, b3_ref, gates_ref, sems):
+    chip, core = place()
+    wq, wv = q_ref.shape[1] // 4, v_ref.shape[1] // 4
+    heads = ig_ref.shape[0]
+
+    def block(ref, owner, width):
+        return ref.at[:, pl.ds(pl.multiple_of(owner * width, width), width)]
+
+    def cross(first, second):
+        pairs = []
+        for chunk, (same, other) in enumerate(((a2_ref, a3_ref), (b2_ref, b3_ref))):
+            for target, to in ((same, core), (other, 1 - core)):
+                pairs.append((block(first, 2 * chunk + to, wq), target.at[:, :wq]))
+                pairs.append((block(second, 2 * chunk + to, wv), target.at[:, wq:]))
+        return pairs
+
+    @pl.when(chip == 0)
+    def _():
+        run_copies(cross(k_ref, v_ref), sems)
+
+    @pl.when(chip != 0)
+    def _():
+        run_copies(cross(q_ref, g_ref), sems)
+
+    pairs = []
+    for chunk in range(2):
+        start = chunk * 2 * (wq + wv)
+        for ref, width in ((q_ref, wq), (g_ref, wv), (k_ref, wq), (v_ref, wv)):
+            pairs.append((block(ref, 2 * chunk + 1 - core, width), m1_ref.at[:, start : start + width]))
+            start += width
+    copies = run_copies(pairs, sems.at[pl.ds(8, 8)])
+    gates_ref[:heads, :] = ig_ref[...]
+    gates_ref[heads:, :] = fg_ref[...]
+    for i, (source, target) in enumerate(cross(k_ref, v_ref)):
+        pltpu.make_async_copy(source, target, sems.at[i]).wait()
+    for copy in copies:
+        copy.wait()
+
+
+def local_kernel(qk, vw, length_ref, q_ref, k_ref, v_ref, g_ref, m1_ref, own_ref, got_ref, qg_ref, kv_ref, stats_ref, sems):
+    chip, core = place()
+    rows = q_ref.shape[0]
+    heads = own_ref.shape[0] // 2
+    wq, wv = heads * qk, heads * vw
+    pairs = []
+    mine = pl.ds(pl.multiple_of(core * rows, rows), rows)
+    theirs = pl.ds(pl.multiple_of((1 - core) * rows, rows), rows)
+    for chunk in range(2):
+        start = chunk * 2 * (wq + wv)
+        owner = 2 * chunk + core
+        for first, second, target in ((q_ref, g_ref, qg_ref), (k_ref, v_ref, kv_ref)):
+            pairs.append((first.at[:, pl.ds(pl.multiple_of(owner * wq, wq), wq)], target.at[chunk, mine, :wq]))
+            pairs.append((second.at[:, pl.ds(pl.multiple_of(owner * wv, wv), wv)], target.at[chunk, mine, wq:]))
+            pairs.append((m1_ref.at[:, start : start + wq + wv], target.at[chunk, theirs, :]))
+            start += wq + wv
+    copies = run_copies(pairs, sems)
+    stats_ref[...] = jnp.zeros_like(stats_ref)
+    for copy in copies:
+        copy.wait()
+    length = length_ref[0]
+
+    def part(side, chunk):
+        gates = own_ref if side == chunk else got_ref
+        size = 2 * rows
+        low = side * size
+        for head in range(heads):
+            q = qg_ref[chunk, :, head * qk : (head + 1) * qk]
+            k = kv_ref[chunk, :, head * qk : (head + 1) * qk]
+            g = qg_ref[chunk, :, wq + head * vw : wq + (head + 1) * vw]
+            v = kv_ref[chunk, :, wq + head * vw : wq + (head + 1) * vw]
+            weight = decay(gates[head : head + 1, :], gates[heads + head : heads + head + 1, :], length, qk**-0.5)
+            weight = weight[low : low + size, low : low + size]
+            scores = dot(q, k, NT) * weight
+            pulled = dot(g, v, NT)
+            norm = jnp.sum(scores, axis=1, keepdims=True)
+            along = jnp.sum(scores * pulled, axis=1, keepdims=True)
+            on = lax.broadcasted_iota(jnp.int32, (size, 2 * size), 0) + low == lax.broadcasted_iota(
+                jnp.int32, (size, 2 * size), 1
+            )
+
+            def as_row(column):
+                return jnp.sum(jnp.where(on, column, 0.0), axis=0, keepdims=True)
+
+            if side == 1:
+                at = chunk * heads + head
+                stats_ref[at : at + 1, :] = as_row(norm)
+                stats_ref[2 * heads + at : 2 * heads + at + 1, :] = as_row(along)
+            else:
+                inverse, grad_norm, by_row = backward_terms(norm, along)
+                by_column = jnp.sum((pulled * inverse + grad_norm) * scores, axis=0, keepdims=True)
+                stats_ref[head : head + 1, :size] = by_column
+                stats_ref[heads + head : heads + head + 1, :] = as_row(by_row)
+
+    @pl.when(chip == 0)
+    def _():
+        part(0, 1)
+
+    @pl.when(chip != 0)
+    def _():
+        part(1, 0)
+        part(1, 1)
+
+
+def cross_kernel(
+    chunk, qk, vw, length_ref, qg_ref, kv_ref, same_ref, other_ref, own_ref, got_ref, stats_ref,
+    mine_ref, theirs_ref, gates_ref, wide_ref, thin_ref, result_ref, sems,
+):
+    chip, core = place()
+    rows = same_ref.shape[0]
+    size = 2 * rows
+    heads = own_ref.shape[0] // 2
+    wq, wv = heads * qk, heads * vw
+
+    def gather(side, wide, thin):
+        base = 0 if side else size
+        at_same = pl.ds(pl.multiple_of(base + core * rows, rows), rows)
+        at_other = pl.ds(pl.multiple_of(base + (1 - core) * rows, rows), rows)
+        local = wide_ref.at[side * size : (side + 1) * size, :]
+        return [
+            (wide.at[chunk], local),
+            (thin.at[chunk], thin_ref),
+            (same_ref, wide_ref.at[at_same, :]),
+            (other_ref, wide_ref.at[at_other, :]),
+        ]
+
+    length = length_ref[0]
+    gates_ref[...] = jnp.zeros_like(gates_ref)
+
+    def part(side):
+        copies = run_copies(gather(side, *((kv_ref, qg_ref) if side else (qg_ref, kv_ref))), sems)
+        gates = own_ref if side == chunk else got_ref
+        full = 2 * size
+        rows_at = lax.broadcasted_iota(jnp.int32, (full, full), 0)
+        cols_at = lax.broadcasted_iota(jnp.int32, (full, full), 1)
+
+        def as_column(row):
+            return jnp.sum(jnp.where(rows_at == cols_at, row, 0.0), axis=1, keepdims=True)
+
+        weights = [
+            decay(gates[head : head + 1, :], gates[heads + head : heads + head + 1, :], length, qk**-0.5)
+            for head in range(heads)
+        ]
+        for copy in copies:
+            copy.wait()
+        for head in range(heads):
+            first = slice(head * qk, (head + 1) * qk)
+            second = slice(wq + head * vw, wq + (head + 1) * vw)
+            if side == 0:
+                q, g, k, v = wide_ref[:, first], wide_ref[:, second], thin_ref[:, first], thin_ref[:, second]
+                weight = weights[head][:, :size]
+            else:
+                k, v, q, g = wide_ref[:, first], wide_ref[:, second], thin_ref[:, first], thin_ref[:, second]
+                weight = weights[head][size:, :]
+            scores = dot(q, k, NT) * weight
+            pulled = dot(g, v, NT)
+            norm = jnp.sum(scores, axis=1, keepdims=True)
+            along = jnp.sum(scores * pulled, axis=1, keepdims=True)
+            if side == 0:
+                at = chunk * heads + head
+                norm = norm + as_column(stats_ref[at : at + 1, :])
+                along = along + as_column(stats_ref[2 * heads + at : 2 * heads + at + 1, :])
+            inverse, grad_norm, by_row = backward_terms(norm, along)
+            grad_scores = pulled * inverse + grad_norm
+            scaled = scores * inverse
+            grad_raw = grad_scores * weight
+            if side == 0:
+                hidden = wide_dot(scaled[:size], v, NN)
+                gq = wide_dot(grad_raw[:size], k, NN)
+                gk = wide_dot(grad_raw.T, q, NN)
+                gv = wide_dot(scaled.T, g, NN)
+            else:
+                hidden = wide_dot(scaled, v, NN)
+                gq = wide_dot(grad_raw, k, NN)
+                gk = wide_dot(grad_raw.T[size:], q, NN)
+                gv = wide_dot(scaled.T[size:], g, NN)
+            result_ref[:, head * qk : (head + 1) * qk] = gq.astype(jnp.bfloat16)
+            result_ref[:, wq + head * qk : wq + (head + 1) * qk] = gk.astype(jnp.bfloat16)
+            result_ref[:, 2 * wq + head * vw : 2 * wq + (head + 1) * vw] = gv.astype(jnp.bfloat16)
+            result_ref[:, 2 * wq + wv + head * vw : 2 * wq + wv + (head + 1) * vw] = hidden.astype(jnp.bfloat16)
+            by_column = jnp.sum(grad_scores * scores, axis=0, keepdims=True)
+            forget = gates[heads + head : heads + head + 1, :]
+            live = cols_at[:1] < length
+            slope = jnp.where(live, 1.0 / (1.0 + jnp.exp(forget)), 0.0)
+            if side == 0 and chunk == 0:
+                small_rows, small_cols = rows_at[:size, :size], cols_at[:size, :size]
+                column = jnp.sum(jnp.where(small_rows == small_cols, by_column, 0.0), axis=1, keepdims=True)
+                before = jnp.where(small_rows < small_cols, column - by_row[:size], 0.0)
+                grad_log = jnp.sum(before, axis=0, keepdims=True)
+                gates_ref[head : head + 1, :size] = by_column
+                gates_ref[heads + head : heads + head + 1, :size] = grad_log * slope[:, :size]
+            if side == 1:
+                row = jnp.sum(jnp.where(rows_at[size:] == cols_at[size:], by_row, 0.0), axis=0, keepdims=True)
+                if chunk == 1:
+                    by_column = by_column + stats_ref[head : head + 1, :]
+                    row = row + stats_ref[heads + head : heads + head + 1, :]
+                    seen = jnp.full((1, full), True)
+                else:
+                    seen = cols_at[:1] >= size
+                by_column = jnp.where(seen, by_column, 0.0)
+                moved = as_column(row - by_column)
+                grad_log = jnp.sum(jnp.where(rows_at >= cols_at, moved, 0.0), axis=0, keepdims=True)
+                gates_ref[head : head + 1, :] = by_column
+                gates_ref[heads + head : heads + head + 1, :] = jnp.where(seen, grad_log * slope, 0.0)
+        out = run_copies(
+            [
+                (result_ref.at[pl.ds(pl.multiple_of(core * rows, rows), rows), :], mine_ref),
+                (result_ref.at[pl.ds(pl.multiple_of((1 - core) * rows, rows), rows), :], theirs_ref),
+            ],
+            sems.at[pl.ds(4, 2)],
+        )
+        for copy in out:
+            copy.wait()
+
+    @pl.when(chip == 0)
+    def _():
+        part(0)
+
+    @pl.when(chip != 0)
+    def _():
+        part(1)
+
+
+def merge_kernel(
+    mine_a, mine_b, got_a, got_b, gates_a, gates_got, gates_b, hidden_ref, gq_ref, gk_ref, gv_ref, gi_ref, gf_ref, sems
+):
+    chip, core = place()
+    heads = gi_ref.shape[0]
+    wq, wv = gq_ref.shape[1] // 4, gv_ref.shape[1] // 4
+    pairs = []
+    for chunk, sources in enumerate(((mine_a, got_a), (mine_b, got_b))):
+        for source, by in zip(sources, (core, 1 - core)):
+            start = 0
+            for target, width in ((gq_ref, wq), (gk_ref, wq), (gv_ref, wv), (hidden_ref, wv)):
+                at = pl.ds(pl.multiple_of((2 * chunk + by) * width, width), width)
+                pairs.append((source.at[:, start : start + width], target.at[:, at]))
+                start += width
+    copies = run_copies(pairs, sems)
+    gates = jnp.where(chip == 0, gates_a[...] + gates_got[...], gates_b[...])
+    gi_ref[...] = gates[:heads]
+    gf_ref[...] = gates[heads:]
+    for copy in copies:
+        copy.wait()
+
+
+def split_shards(queries, keys, values, cotangent, igate, fgate, lengths):
+    rows = queries.shape[0]
+    heads = igate.shape[0]
+    qk = queries.shape[1] // (4 * heads)
+    vw = values.shape[1] // (4 * heads)
+    width = heads * (qk + vw)
+    bf16, f32 = jnp.bfloat16, jnp.float32
+    shape = jax.ShapeDtypeStruct
+    vmem = pl.BlockSpec(memory_space=pltpu.VMEM)
+    smem = pl.BlockSpec(memory_space=pltpu.SMEM)
+    hbm = pl.BlockSpec(memory_space=pl.ANY)
+    params = pltpu.CompilerParams(vmem_limit_bytes=32 * 1024 * 1024)
+    dma = pltpu.SemaphoreType.DMA
+
+    def swap(value, mask):
+        return lax.ppermute(value, "head", [(s, s ^ mask) for s in range(4)])
+
+    cross_shape = shape((rows, width), bf16)
+    to_core, a2, a3, b2, b3, gates = pl.pallas_call(
+        pack_kernel,
+        out_shape=(shape((rows, 4 * width), bf16),) + (cross_shape,) * 4 + (shape((2 * heads, igate.shape[1]), f32),),
+        in_specs=[hbm] * 4 + [vmem] * 2,
+        out_specs=(hbm,) * 5 + (vmem,),
+        scratch_shapes=[dma((16,))],
+        compiler_params=params,
+    )(queries, keys, values, cotangent, igate, fgate)
+    gates_got = swap(gates, 2)
+    a2, a3 = swap(a2, 2), swap(a3, 3)
+    from_core = swap(to_core, 1)
+    b2, b3 = swap(b2, 2), swap(b3, 3)
+    both = shape((2, 2 * rows, width), bf16)
+    stats_shape = shape((4 * heads, igate.shape[1]), f32)
+    qg, kv, stats = pl.pallas_call(
+        functools.partial(local_kernel, qk, vw),
+        out_shape=(both, both, stats_shape),
+        in_specs=[smem] + [hbm] * 5 + [vmem] * 2,
+        out_specs=(vmem,) * 3,
+        scratch_shapes=[dma((12,))],
+        compiler_params=params,
+    )(lengths, queries, keys, values, cotangent, from_core, gates, gates_got)
+    stats = swap(stats, 2)
+
+    def cross(chunk, same, other):
+        out_shape = shape((rows, 2 * width), bf16)
+        return pl.pallas_call(
+            functools.partial(cross_kernel, chunk, qk, vw),
+            out_shape=(out_shape, out_shape, shape(gates.shape, f32)),
+            in_specs=[smem] + [hbm] * 4 + [vmem] * 3,
+            out_specs=(hbm, hbm, vmem),
+            scratch_shapes=[
+                pltpu.VMEM((4 * rows, width), bf16),
+                pltpu.VMEM((2 * rows, width), bf16),
+                pltpu.VMEM((2 * rows, 2 * width), bf16),
+                dma((6,)),
+            ],
+            compiler_params=params,
+        )(lengths, qg, kv, same, other, gates, gates_got, stats)
+
+    mine_a, theirs_a, gates_a = cross(0, a2, a3)
+    gates_back = swap(gates_a, 2)
+    got_a = swap(theirs_a, 1)
+    mine_b, theirs_b, gates_b = cross(1, b2, b3)
+    got_b = swap(theirs_b, 1)
+    gate_shape = shape(igate.shape, f32)
+    return pl.pallas_call(
+        merge_kernel,
+        out_shape=(
+            shape(values.shape, bf16), shape(queries.shape, bf16), shape(keys.shape, bf16), shape(values.shape, bf16),
+            gate_shape, gate_shape,
+        ),
+        in_specs=[hbm] * 4 + [vmem] * 3,
+        out_specs=(hbm,) * 4 + (vmem,) * 2,
+        scratch_shapes=[dma((16,))],
+        compiler_params=params,
+    )(mine_a, mine_b, got_a, got_b, gates_a, gates_back, gates_b)
+
+
+def shards(*arrays):
+    if lax.axis_size("head") == 4:
+        return split_shards(*arrays)
+    return swapped_shards(*arrays)
+
+
 def solution(mesh):
     rows = P(("groups", "seq", "head"), None)
     gates = P("head", ("groups", "seq"))

time: 38.3 us -> 31.4 us (0.82)
  blocking collectives: 14.1 us -> 0 us
  Pallas kernels: 1.48 us -> 7.54 us
  starting transfers between devices: 4.34 us -> 8.05 us
  waiting for transfers between devices: 11 us -> 9.1 us
  other arithmetic: 0.95 us -> 0 us
    all_to_all x1 -> x0, blocking collectives: 14.1 us -> none  [shards(): lax.all_to_all(out.reshape(devices, rows, -1), 'head', split_axis=0, conc...]
    all_to_all x1 -> x0, waiting for transfers between devices: 11 us -> none  [shards(): lax.all_to_all(joined, 'head', split_axis=1, concat_axis=0, tiled=True)]
    ppermute x0 -> x10, waiting for transfers between devices: none -> 9.1 us  [swap(): return lax.ppermute(value, 'head', [(s, s ^ mask) for s in range(4)])]
    ppermute x0 -> x10, starting transfers between devices: none -> 8.05 us  [swap(): return lax.ppermute(value, 'head', [(s, s ^ mask) for s in range(4)])]
    pallas_call x1 -> x5, Pallas kernels: 1.48 us -> 7.54 us  [the longest x2 4.81 us: cross(): pl.pallas_call(functools.partial(cross_kernel, chunk, qk, vw), out_shape=...]
    unnamed x6 -> x12, local copies, waits for them, and re-layouts: 0.06 us -> 5.06 us
    reshape x6 -> x0, local copies, waits for them, and re-layouts: 4.82 us -> none  [the longest x4 2.77 us: shards(): back[:, :, a:b].reshape(rows, -1)]
    all_to_all x1 -> x0, starting transfers between devices: 4.34 us -> none  [shards(): lax.all_to_all(joined, 'head', split_axis=1, concat_axis=0, tiled=True)]
  transfers between devices with their start and end apart: 1 -> 10, of which waited for: 1 -> 4; matrix products, arithmetic and copies ran while one was open for 0% -> 0% of each run, Pallas kernels for 0% -> 18%
where the time goes in v2:
time: 31.4 us; the launch traced here: 31.1 us
  waiting for transfers between devices  9.1 us (29%)
  starting transfers between devices  8.05 us (26%)
  Pallas kernels  7.54 us (24%)
  local copies, waits for them, and re-layouts  5.06 us (16%)
  between operations  1.37 us (4%)
    ppermute x10, waiting for transfers between devices, swap(): return lax.ppermute(value, 'head', [(s, s ^ mask) for s in range(4)])  9.1 us
    ppermute x10, starting transfers between devices, swap(): return lax.ppermute(value, 'head', [(s, s ^ mask) for s in range(4)])  8.05 us
    unnamed x12, local copies, waits for them, and re-layouts  5.06 us
    pallas_call x2, Pallas kernels, cross(): pl.pallas_call(functools.partial(cross_kernel, chunk, qk, vw), out_shape=...  4.81 us
    pallas_call x1, Pallas kernels, split_shards(): pl.pallas_call(merge_kernel, out_shape=(shape(values.shape, bf16), shape(...  1.58 us
    pallas_call x1, Pallas kernels, split_shards(): pl.pallas_call(functools.partial(local_kernel, qk, vw), out_shape=(both,...  0.72 us
  transfers between devices with their start and end apart: 10, of which 4 were waited for; matrix products, arithmetic and copies ran while one was open for 0% of the time, Pallas kernels for 18%

profile of v2, /device:TPU:0, one launch (start us, length us, event | category | flops | bytes accessed | tf_op | source)
XLA Modules:
  0.0 31.1 jit_solution(16778732972525828508)
XLA Ops:
  0.6 0.9 %copy-done = bf16[32,4096]{1,0:T(8,128)(2,1)S(1)} copy-done((bf16[32,4096]{1,0:T(8,128)(2,1)S(1)}, bf16[32,4096]{1,0:T(8,128)(2,1)}, u32[]{:S(2)}) %copy-start) | copy-done | bytes 262168
  1.6 0.9 %copy-done.1 = bf16[32,4096]{1,0:T(8,128)(2,1)S(1)} copy-done((bf16[32,4096]{1,0:T(8,128)(2,1)S(1)}, bf16[32,4096]{1,0:T(8,128)(2,1)}, u32[]{:S(2)}) %copy-start.1) | copy-done | bytes 262168
  2.5 0.9 %copy-done.2 = bf16[32,2048]{1,0:T(8,128)(2,1)S(1)} copy-done((bf16[32,2048]{1,0:T(8,128)(2,1)S(1)}, bf16[32,2048]{1,0:T(8,128)(2,1)}, u32[]{:S(2)}) %copy-start.2) | copy-done | bytes 131096
  3.4 0.9 %copy-done.3 = bf16[32,2048]{1,0:T(8,128)(2,1)S(1)} copy-done((bf16[32,2048]{1,0:T(8,128)(2,1)S(1)}, bf16[32,2048]{1,0:T(8,128)(2,1)}, u32[]{:S(2)}) %copy-start.3) | copy-done | bytes 131096
  4.3 0.7 %copy-done.4 = f32[2,128]{1,0:T(2,128)S(1)} copy-done((f32[2,128]{1,0:T(2,128)S(1)}, f32[2,128]{1,0:T(2,128)}, u32[]{:S(2)}) %copy-start.4) | copy-done | bytes 1048
  5.0 0.7 %copy-done.5 = f32[2,128]{1,0:T(2,128)S(1)} copy-done((f32[2,128]{1,0:T(2,128)S(1)}, f32[2,128]{1,0:T(2,128)}, u32[]{:S(2)}) %copy-start.5) | copy-done | bytes 1048
  5.7 0.4 %shard_map.118 = (bf16[32,6144]{1,0:T(8,128)(2,1)S(1)}, bf16[32,1536]{1,0:T(8,128)(2,1)S(1)}, bf16[32,1536]{1,0:T(8,128)(2,1)S(1)}, bf16[32,1536]{1,0:T(8,128)(2...) custom-call(bf16[32,2048]{1,0:T(8,128)(2,1)S(1)} %copy-done.2, bf16[32,2048]{1,0:T(8,128)(2,1)S(1)} %copy-done.3, ...), custom_call_target="tpu_custom_call" | custom-call | tf_op jit(solution)/shard_map/pallas_call | solution.py:404
  6.1 0.5 %collective-permute-start = (bf16[32,6144]{1,0:T(8,128)(2,1)S(1)}, bf16[32,6144]{1,0:T(8,128)(2,1)S(1)}, u32[]{:S(2)}, u32[]{:S(2)}) collective-permute-start(bf16[32,6144]{1,0:T(8,128)(2,1)S(1)} %get-tuple-element.21), channel_id=1, source_target_pairs={{0,1},{1,0},{2,3},{3,2},{4,5},{5,4},{6,7},{7,6},{8,9},{9,8},{10,11... | collective-permute-start | bytes 1179656 | tf_op jit(solution)/shard_map/ppermute | solution.py:401
  6.7 2.6 %collective-permute-start.1 = (f32[4,128]{1,0:T(4,128)S(1)}, f32[4,128]{1,0:T(4,128)S(1)}, u32[]{:S(2)}, u32[]{:S(2)}) collective-permute-start(f32[4,128]{1,0:T(4,128)S(1)} %get-tuple-element.22.own_ref), channel_id=1, source_target_pairs={{0,2},{1,3},{2,0},{3,1},{4,6},{5,7},{6,4},{7,5},{8,10},{9,11},{10,... | collective-permute-start | bytes 6152 | tf_op jit(solution)/shard_map/ppermute | solution.py:401
  9.2 0.1 collective-permute-start.5
  9.3 1.4 %collective-permute-start.6 = (bf16[32,1536]{1,0:T(8,128)(2,1)S(1)}, bf16[32,1536]{1,0:T(8,128)(2,1)S(1)}, u32[]{:S(2)}, u32[]{:S(2)}) collective-permute-start(bf16[32,1536]{1,0:T(8,128)(2,1)S(1)} %get-tuple-element.30), channel_id=1, source_target_pairs={{0,3},{1,2},{2,1},{3,0},{4,7},{5,6},{6,5},{7,4},{8,11},{9,10},{10,... | collective-permute-start | bytes 294920 | tf_op jit(solution)/shard_map/ppermute | solution.py:401
  10.7 0.5 %collective-permute-start.2 = (bf16[32,1536]{1,0:T(8,128)(2,1)S(1)}, bf16[32,1536]{1,0:T(8,128)(2,1)S(1)}, u32[]{:S(2)}, u32[]{:S(2)}) collective-permute-start(bf16[32,1536]{1,0:T(8,128)(2,1)S(1)} %get-tuple-element.25), channel_id=1, source_target_pairs={{0,2},{1,3},{2,0},{3,1},{4,6},{5,7},{6,4},{7,5},{8,10},{9,11},{10,... | collective-permute-start | bytes 294920 | tf_op jit(solution)/shard_map/ppermute | solution.py:401
  11.3 1.4 %collective-permute-start.3 = (bf16[32,1536]{1,0:T(8,128)(2,1)S(1)}, bf16[32,1536]{1,0:T(8,128)(2,1)S(1)}, u32[]{:S(2)}, u32[]{:S(2)}) collective-permute-start(bf16[32,1536]{1,0:T(8,128)(2,1)S(1)} %get-tuple-element.26), channel_id=1, source_target_pairs={{0,3},{1,2},{2,1},{3,0},{4,7},{5,6},{6,5},{7,4},{8,11},{9,10},{10,... | collective-permute-start | bytes 294920 | tf_op jit(solution)/shard_map/ppermute | solution.py:401
  13.4 0.7 %shard_map.119 = (bf16[2,64,1536]{2,1,0:T(8,128)(2,1)S(1)}, bf16[2,64,1536]{2,1,0:T(8,128)(2,1)S(1)}, f32[8,128]{1,0:T(8,128)S(1)}) custom-call(s32[1]{0:T(128)S(6)} %copy.13.length_ref, bf16[32,2048]{1,0:T(8,128)(2,1)S(1)} %copy-done.2, bf16[32,2048]{1,0:T(8,128)(2,1)S(1)} %copy-done.3, bf16[32,4096]{1,0:T(8,128)(2,1)S(1)} %copy-done, ...), custom_call_target="tpu_custom_call" | custom-call | tf_op jit(solution)/shard_map/pallas_call | solution.py:418
  14.1 0.5 %collective-permute-start.4 = (f32[8,128]{1,0:T(8,128)S(1)}, f32[8,128]{1,0:T(8,128)S(1)}, u32[]{:S(2)}, u32[]{:S(2)}) collective-permute-start(f32[8,128]{1,0:T(8,128)S(1)} %get-tuple-element.27), channel_id=1, source_target_pairs={{0,2},{1,3},{2,0},{3,1},{4,6},{5,7},{6,4},{7,5},{8,10},{9,11},{10,... | collective-permute-start | bytes 12296 | tf_op jit(solution)/shard_map/ppermute | solution.py:401
  14.6 0.3 collective-permute-done.5.same_ref
  14.9 0.6 %collective-permute-done.6.other_ref = bf16[32,1536]{1,0:T(8,128)(2,1)S(1)} collective-permute-done((bf16[32,1536]{1,0:T(8,128)(2,1)S(1)}, bf16[32,1536]{1,0:T(8,128)(2,1)S(1)}, u32[]{:S(2)}, u32[]{:S(2)}) %collective-permute-start.6) | collective-permute-done | bytes 98336 | tf_op jit(solution)/shard_map/ppermute | solution.py:401
  15.4 5.1 %collective-permute-done.4.stats_ref = f32[8,128]{1,0:T(8,128)S(1)} collective-permute-done((f32[8,128]{1,0:T(8,128)S(1)}, f32[8,128]{1,0:T(8,128)S(1)}, u32[]{:S(2)}, u32[]{:S(2)}) %collective-permute-start.4) | collective-permute-done | bytes 4128 | tf_op jit(solution)/shard_map/ppermute | solution.py:401
  20.5 2.4 %shard_map.121 = (bf16[32,3072]{1,0:T(8,128)(2,1)S(1)}, bf16[32,3072]{1,0:T(8,128)(2,1)S(1)}, f32[4,128]{1,0:T(4,128)S(1)}) custom-call(s32[1]{0:T(128)S(6)} %copy.13.length_ref, bf16[2,64,1536]{2,1,0:T(8,128)(2,1)S(1)} %get-tuple-element.23.qg_ref, bf16[2,64,1536]{2,1,0:T(8,128)(2,1)S(1)} %get-tuple-element.24.kv_ref, ...), custom_call_target="tpu_custom_call" | custom-call | tf_op jit(solution)/shard_map/pallas_call | solution.py:430
  23.0 2.4 %shard_map.120 = (bf16[32,3072]{1,0:T(8,128)(2,1)S(1)}, bf16[32,3072]{1,0:T(8,128)(2,1)S(1)}, f32[4,128]{1,0:T(4,128)S(1)}) custom-call(s32[1]{0:T(128)S(6)} %copy.13.length_ref, bf16[2,64,1536]{2,1,0:T(8,128)(2,1)S(1)} %get-tuple-element.23.qg_ref, bf16[2,64,1536]{2,1,0:T(8,128)(2,1)S(1)} %get-tuple-element.24.kv_ref, ...), custom_call_target="tpu_custom_call" | custom-call | tf_op jit(solution)/shard_map/pallas_call | solution.py:430
  25.4 0.5 %collective-permute-start.7 = (bf16[32,3072]{1,0:T(8,128)(2,1)S(1)}, bf16[32,3072]{1,0:T(8,128)(2,1)S(1)}, u32[]{:S(2)}, u32[]{:S(2)}) collective-permute-start(bf16[32,3072]{1,0:T(8,128)(2,1)S(1)} %get-tuple-element.32), channel_id=1, source_target_pairs={{0,1},{1,0},{2,3},{3,2},{4,5},{5,4},{6,7},{7,6},{8,9},{9,8},{10,11... | collective-permute-start | bytes 589832 | tf_op jit(solution)/shard_map/ppermute | solution.py:401
  26.0 0.4 %collective-permute-start.9 = (f32[4,128]{1,0:T(4,128)S(1)}, f32[4,128]{1,0:T(4,128)S(1)}, u32[]{:S(2)}, u32[]{:S(2)}) collective-permute-start(f32[4,128]{1,0:T(4,128)S(1)} %get-tuple-element.34.gates_a), channel_id=1, source_target_pairs={{0,2},{1,3},{2,0},{3,1},{4,6},{5,7},{6,4},{7,5},{8,10},{9,11},{10,... | collective-permute-start | bytes 6152 | tf_op jit(solution)/shard_map/ppermute | solution.py:401
  26.4 3.2 %collective-permute-done.9.gates_got = f32[4,128]{1,0:T(4,128)S(1)} collective-permute-done((f32[4,128]{1,0:T(4,128)S(1)}, f32[4,128]{1,0:T(4,128)S(1)}, u32[]{:S(2)}, u32[]{:S(2)}) %collective-permute-start.9) | collective-permute-done | bytes 2080 | tf_op jit(solution)/shard_map/ppermute | solution.py:401
  29.5 1.6 %shard_map.122 = (bf16[32,4096]{1,0:T(8,128)(2,1)}, bf16[32,2048]{1,0:T(8,128)(2,1)}, bf16[32,2048]{1,0:T(8,128)(2,1)}, bf16[32,4096]{1,0:T(8,128)(2,1)}, f32[2,128]{1,0:T(2,128)}, /*index=5*/f32[2,128]{1,0:T(2,128)}) custom-call(bf16[32,3072]{1,0:T(8,128)(2,1)S(1)} %get-tuple-element.28.mine_a, bf16[32,3072]{1,0:T(8,128)(2,1)S(1)} %get-tuple-element.31.mine_b, ...), custom_call_target="tpu_custom_call" | custom-call | tf_op jit(solution)/shard_map/pallas_call | solution.py:450
  (13 shorter events, 0.1 us)
Async XLA Ops:
  0.6 1.0 %copy-start = (bf16[32,4096]{1,0:T(8,128)(2,1)S(1)}, bf16[32,4096]{1,0:T(8,128)(2,1)}, u32[]{:S(2)}) copy-start(bf16[32,4096]{1,0:T(8,128)(2,1)} %v_ref.3) | copy-start | bytes 786436
  1.6 0.9 %copy-start.1 = (bf16[32,4096]{1,0:T(8,128)(2,1)S(1)}, bf16[32,4096]{1,0:T(8,128)(2,1)}, u32[]{:S(2)}) copy-start(bf16[32,4096]{1,0:T(8,128)(2,1)} %g_ref.3) | copy-start | bytes 786436
  2.5 0.9 %copy-start.2 = (bf16[32,2048]{1,0:T(8,128)(2,1)S(1)}, bf16[32,2048]{1,0:T(8,128)(2,1)}, u32[]{:S(2)}) copy-start(bf16[32,2048]{1,0:T(8,128)(2,1)} %q_ref.3) | copy-start | bytes 393220
  3.4 0.9 %copy-start.3 = (bf16[32,2048]{1,0:T(8,128)(2,1)S(1)}, bf16[32,2048]{1,0:T(8,128)(2,1)}, u32[]{:S(2)}) copy-start(bf16[32,2048]{1,0:T(8,128)(2,1)} %k_ref.3) | copy-start | bytes 393220
  4.3 0.7 %copy-start.4 = (f32[2,128]{1,0:T(2,128)S(1)}, f32[2,128]{1,0:T(2,128)}, u32[]{:S(2)}) copy-start(f32[2,128]{1,0:T(2,128)} %ig_ref.1) | copy-start | bytes 3076
  5.0 0.7 %copy-start.5 = (f32[2,128]{1,0:T(2,128)S(1)}, f32[2,128]{1,0:T(2,128)}, u32[]{:S(2)}) copy-start(f32[2,128]{1,0:T(2,128)} %fg_ref.1) | copy-start | bytes 3076
  6.1 7.2 %collective-permute-start = (bf16[32,6144]{1,0:T(8,128)(2,1)S(1)}, bf16[32,6144]{1,0:T(8,128)(2,1)S(1)}, u32[]{:S(2)}, u32[]{:S(2)}) collective-permute-start(bf16[32,6144]{1,0:T(8,128)(2,1)S(1)} %get-tuple-element.21), channel_id=1, source_target_pairs={{0,1},{1,0},{2,3},{3,2},{4,5},{5,4},{6,7},{7,6},{8,9},{9,8},{10,11... | collective-permute-start | bytes 1179656 | tf_op jit(solution)/shard_map/ppermute | solution.py:401
  6.7 4.6 %collective-permute-start.1 = (f32[4,128]{1,0:T(4,128)S(1)}, f32[4,128]{1,0:T(4,128)S(1)}, u32[]{:S(2)}, u32[]{:S(2)}) collective-permute-start(f32[4,128]{1,0:T(4,128)S(1)} %get-tuple-element.22.own_ref), channel_id=1, source_target_pairs={{0,2},{1,3},{2,0},{3,1},{4,6},{5,7},{6,4},{7,5},{8,10},{9,11},{10,... | collective-permute-start | bytes 6152 | tf_op jit(solution)/shard_map/ppermute | solution.py:401
  9.2 5.6 %collective-permute-start.5 = (bf16[32,1536]{1,0:T(8,128)(2,1)S(1)}, bf16[32,1536]{1,0:T(8,128)(2,1)S(1)}, u32[]{:S(2)}, u32[]{:S(2)}) collective-permute-start(bf16[32,1536]{1,0:T(8,128)(2,1)S(1)} %get-tuple-element.29), channel_id=1, source_target_pairs={{0,2},{1,3},{2,0},{3,1},{4,6},{5,7},{6,4},{7,5},{8,10},{9,11},{10,... | collective-permute-start | bytes 294920 | tf_op jit(solution)/shard_map/ppermute | solution.py:401
  9.3 6.1 %collective-permute-start.6 = (bf16[32,1536]{1,0:T(8,128)(2,1)S(1)}, bf16[32,1536]{1,0:T(8,128)(2,1)S(1)}, u32[]{:S(2)}, u32[]{:S(2)}) collective-permute-start(bf16[32,1536]{1,0:T(8,128)(2,1)S(1)} %get-tuple-element.30), channel_id=1, source_target_pairs={{0,3},{1,2},{2,1},{3,0},{4,7},{5,6},{6,5},{7,4},{8,11},{9,10},{10,... | collective-permute-start | bytes 294920 | tf_op jit(solution)/shard_map/ppermute | solution.py:401
  10.7 12.2 %collective-permute-start.2 = (bf16[32,1536]{1,0:T(8,128)(2,1)S(1)}, bf16[32,1536]{1,0:T(8,128)(2,1)S(1)}, u32[]{:S(2)}, u32[]{:S(2)}) collective-permute-start(bf16[32,1536]{1,0:T(8,128)(2,1)S(1)} %get-tuple-element.25), channel_id=1, source_target_pairs={{0,2},{1,3},{2,0},{3,1},{4,6},{5,7},{6,4},{7,5},{8,10},{9,11},{10,... | collective-permute-start | bytes 294920 | tf_op jit(solution)/shard_map/ppermute | solution.py:401
  11.3 11.7 %collective-permute-start.3 = (bf16[32,1536]{1,0:T(8,128)(2,1)S(1)}, bf16[32,1536]{1,0:T(8,128)(2,1)S(1)}, u32[]{:S(2)}, u32[]{:S(2)}) collective-permute-start(bf16[32,1536]{1,0:T(8,128)(2,1)S(1)} %get-tuple-element.26), channel_id=1, source_target_pairs={{0,3},{1,2},{2,1},{3,0},{4,7},{5,6},{6,5},{7,4},{8,11},{9,10},{10,... | collective-permute-start | bytes 294920 | tf_op jit(solution)/shard_map/ppermute | solution.py:401
  14.1 6.4 %collective-permute-start.4 = (f32[8,128]{1,0:T(8,128)S(1)}, f32[8,128]{1,0:T(8,128)S(1)}, u32[]{:S(2)}, u32[]{:S(2)}) collective-permute-start(f32[8,128]{1,0:T(8,128)S(1)} %get-tuple-element.27), channel_id=1, source_target_pairs={{0,2},{1,3},{2,0},{3,1},{4,6},{5,7},{6,4},{7,5},{8,10},{9,11},{10,... | collective-permute-start | bytes 12296 | tf_op jit(solution)/shard_map/ppermute | solution.py:401
  22.9 6.7 %collective-permute-start.8 = (bf16[32,3072]{1,0:T(8,128)(2,1)S(1)}, bf16[32,3072]{1,0:T(8,128)(2,1)S(1)}, u32[]{:S(2)}, u32[]{:S(2)}) collective-permute-start(bf16[32,3072]{1,0:T(8,128)(2,1)S(1)} %get-tuple-element.33), channel_id=1, source_target_pairs={{0,1},{1,0},{2,3},{3,2},{4,5},{5,4},{6,7},{7,6},{8,9},{9,8},{10,11... | collective-permute-start | bytes 589832 | tf_op jit(solution)/shard_map/ppermute | solution.py:401
  25.4 4.1 %collective-permute-start.7 = (bf16[32,3072]{1,0:T(8,128)(2,1)S(1)}, bf16[32,3072]{1,0:T(8,128)(2,1)S(1)}, u32[]{:S(2)}, u32[]{:S(2)}) collective-permute-start(bf16[32,3072]{1,0:T(8,128)(2,1)S(1)} %get-tuple-element.32), channel_id=1, source_target_pairs={{0,1},{1,0},{2,3},{3,2},{4,5},{5,4},{6,7},{7,6},{8,9},{9,8},{10,11... | collective-permute-start | bytes 589832 | tf_op jit(solution)/shard_map/ppermute | solution.py:401
  26.0 3.6 %collective-permute-start.9 = (f32[4,128]{1,0:T(4,128)S(1)}, f32[4,128]{1,0:T(4,128)S(1)}, u32[]{:S(2)}, u32[]{:S(2)}) collective-permute-start(f32[4,128]{1,0:T(4,128)S(1)} %get-tuple-element.34.gates_a), channel_id=1, source_target_pairs={{0,2},{1,3},{2,0},{3,1},{4,6},{5,7},{6,4},{7,5},{8,10},{9,11},{10,... | collective-permute-start | bytes 6152 | tf_op jit(solution)/shard_map/ppermute | solution.py:401

commit v3 on v2

--- a/solution.py
+++ b/solution.py
@@ -20,8 +20,9 @@
 
 
 def wide_dot(left, right, contract):
-    high, low = halves(left)
-    return dot(high, right, contract) + dot(low, right, contract)
+    rows = left.shape[0]
+    both = dot(jnp.concatenate(halves(left), axis=0), right, contract)
+    return both[:rows] + both[rows:]
 
 
 NN = ((1,), (0,))
@@ -139,7 +140,9 @@
     return copies
 
 
-def pack_kernel(q_ref, k_ref, v_ref, g_ref, ig_ref, fg_ref, m1_ref, a2_ref, a3_ref, b2_ref, b3_ref, gates_ref, sems):
+def pack_kernel(
+    q_ref, k_ref, v_ref, g_ref, ig_ref, fg_ref, m1_ref, a2_ref, a3_ref, qg_ref, kv_ref, gates_ref, in_ref, out_ref, sems
+):
     chip, core = place()
     wq, wv = q_ref.shape[1] // 4, v_ref.shape[1] // 4
     heads = ig_ref.shape[0]
@@ -149,10 +152,9 @@
 
     def cross(first, second):
         pairs = []
-        for chunk, (same, other) in enumerate(((a2_ref, a3_ref), (b2_ref, b3_ref))):
-            for target, to in ((same, core), (other, 1 - core)):
-                pairs.append((block(first, 2 * chunk + to, wq), target.at[:, :wq]))
-                pairs.append((block(second, 2 * chunk + to, wv), target.at[:, wq:]))
+        for target, to in ((a2_ref, core), (a3_ref, 1 - core)):
+            pairs.append((block(first, to, wq), target.at[:, :wq]))
+            pairs.append((block(second, to, wv), target.at[:, wq:]))
         return pairs
 
     @pl.when(chip == 0)
@@ -163,41 +165,40 @@
     def _():
         run_copies(cross(q_ref, g_ref), sems)
 
-    pairs = []
+    pairs = [(ig_ref, in_ref), (fg_ref, out_ref)]
     for chunk in range(2):
         start = chunk * 2 * (wq + wv)
-        for ref, width in ((q_ref, wq), (g_ref, wv), (k_ref, wq), (v_ref, wv)):
-            pairs.append((block(ref, 2 * chunk + 1 - core, width), m1_ref.at[:, start : start + width]))
-            start += width
-    copies = run_copies(pairs, sems.at[pl.ds(8, 8)])
-    gates_ref[:heads, :] = ig_ref[...]
-    gates_ref[heads:, :] = fg_ref[...]
+        for first, second, own in ((q_ref, g_ref, qg_ref), (k_ref, v_ref, kv_ref)):
+            for ref, width, at in ((first, wq, slice(0, wq)), (second, wv, slice(wq, wq + wv))):
+                pairs.append((block(ref, 2 * chunk + 1 - core, width), m1_ref.at[:, start : start + width]))
+                pairs.append((block(ref, 2 * chunk + core, width), own.at[chunk, :, at]))
+                start += width
+    copies = run_copies(pairs, sems.at[pl.ds(4, 18)])
+    for copy in copies[:2]:
+        copy.wait()
+    gates_ref[:heads, :] = in_ref[...]
+    gates_ref[heads:, :] = out_ref[...]
     for i, (source, target) in enumerate(cross(k_ref, v_ref)):
         pltpu.make_async_copy(source, target, sems.at[i]).wait()
-    for copy in copies:
+    for copy in copies[2:]:
         copy.wait()
 
 
-def local_kernel(qk, vw, length_ref, q_ref, k_ref, v_ref, g_ref, m1_ref, own_ref, got_ref, qg_ref, kv_ref, stats_ref, sems):
+def local_kernel(qk, vw, length_ref, own_qg, own_kv, m1_ref, own_ref, got_ref, qg_ref, kv_ref, send_ref, stats_ref):
     chip, core = place()
-    rows = q_ref.shape[0]
+    rows = m1_ref.shape[0]
     heads = own_ref.shape[0] // 2
     wq, wv = heads * qk, heads * vw
-    pairs = []
+    width = wq + wv
     mine = pl.ds(pl.multiple_of(core * rows, rows), rows)
     theirs = pl.ds(pl.multiple_of((1 - core) * rows, rows), rows)
     for chunk in range(2):
-        start = chunk * 2 * (wq + wv)
-        owner = 2 * chunk + core
-        for first, second, target in ((q_ref, g_ref, qg_ref), (k_ref, v_ref, kv_ref)):
-            pairs.append((first.at[:, pl.ds(pl.multiple_of(owner * wq, wq), wq)], target.at[chunk, mine, :wq]))
-            pairs.append((second.at[:, pl.ds(pl.multiple_of(owner * wv, wv), wv)], target.at[chunk, mine, wq:]))
-            pairs.append((m1_ref.at[:, start : start + wq + wv], target.at[chunk, theirs, :]))
-            start += wq + wv
-    copies = run_copies(pairs, sems)
+        start = chunk * 2 * width
+        qg_ref[chunk, mine, :] = own_qg[chunk]
+        qg_ref[chunk, theirs, :] = m1_ref[:, start : start + width]
+        kv_ref[chunk, mine, :] = own_kv[chunk]
+        kv_ref[chunk, theirs, :] = m1_ref[:, start + width : start + 2 * width]
     stats_ref[...] = jnp.zeros_like(stats_ref)
-    for copy in copies:
-        copy.wait()
     length = length_ref[0]
 
     def part(side, chunk):
@@ -234,41 +235,41 @@
 
     @pl.when(chip == 0)
     def _():
+        send_ref[...] = kv_ref[1]
         part(0, 1)
 
     @pl.when(chip != 0)
     def _():
+        send_ref[...] = qg_ref[1]
         part(1, 0)
         part(1, 1)
 
 
 def cross_kernel(
-    chunk, qk, vw, length_ref, qg_ref, kv_ref, same_ref, other_ref, own_ref, got_ref, stats_ref,
-    mine_ref, theirs_ref, gates_ref, wide_ref, thin_ref, result_ref, sems,
+    chunk, qk, vw, length_ref, qg_ref, kv_ref, own_ref, got_ref, stats_ref, *refs
 ):
+    *cross_refs, result_ref, theirs_ref, gates_ref, wide_ref = refs
     chip, core = place()
-    rows = same_ref.shape[0]
+    rows = theirs_ref.shape[0]
     size = 2 * rows
     heads = own_ref.shape[0] // 2
     wq, wv = heads * qk, heads * vw
 
-    def gather(side, wide, thin):
+    def gather(side, local):
         base = 0 if side else size
-        at_same = pl.ds(pl.multiple_of(base + core * rows, rows), rows)
-        at_other = pl.ds(pl.multiple_of(base + (1 - core) * rows, rows), rows)
-        local = wide_ref.at[side * size : (side + 1) * size, :]
-        return [
-            (wide.at[chunk], local),
-            (thin.at[chunk], thin_ref),
-            (same_ref, wide_ref.at[at_same, :]),
-            (other_ref, wide_ref.at[at_other, :]),
-        ]
+        wide_ref[side * size : (side + 1) * size, :] = local[chunk]
+        if len(cross_refs) == 1:
+            wide_ref[base : base + size, :] = cross_refs[0][...]
+        else:
+            for ref, by in zip(cross_refs, (core, 1 - core)):
+                wide_ref[pl.ds(pl.multiple_of(base + by * rows, rows), rows), :] = ref[...]
 
     length = length_ref[0]
     gates_ref[...] = jnp.zeros_like(gates_ref)
 
     def part(side):
-        copies = run_copies(gather(side, *((kv_ref, qg_ref) if side else (qg_ref, kv_ref))), sems)
+        gather(side, kv_ref if side else qg_ref)
+        thin = (qg_ref if side else kv_ref).at[chunk]
         gates = own_ref if side == chunk else got_ref
         full = 2 * size
         rows_at = lax.broadcasted_iota(jnp.int32, (full, full), 0)
@@ -281,16 +282,14 @@
             decay(gates[head : head + 1, :], gates[heads + head : heads + head + 1, :], length, qk**-0.5)
             for head in range(heads)
         ]
-        for copy in copies:
-            copy.wait()
         for head in range(heads):
             first = slice(head * qk, (head + 1) * qk)
             second = slice(wq + head * vw, wq + (head + 1) * vw)
             if side == 0:
-                q, g, k, v = wide_ref[:, first], wide_ref[:, second], thin_ref[:, first], thin_ref[:, second]
+                q, g, k, v = wide_ref[:, first], wide_ref[:, second], thin[:, first], thin[:, second]
                 weight = weights[head][:, :size]
             else:
-                k, v, q, g = wide_ref[:, first], wide_ref[:, second], thin_ref[:, first], thin_ref[:, second]
+                k, v, q, g = wide_ref[:, first], wide_ref[:, second], thin[:, first], thin[:, second]
                 weight = weights[head][size:, :]
             scores = dot(q, k, NT) * weight
             pulled = dot(g, v, NT)
@@ -342,15 +341,7 @@
                 grad_log = jnp.sum(jnp.where(rows_at >= cols_at, moved, 0.0), axis=0, keepdims=True)
                 gates_ref[head : head + 1, :] = by_column
                 gates_ref[heads + head : heads + head + 1, :] = jnp.where(seen, grad_log * slope, 0.0)
-        out = run_copies(
-            [
-                (result_ref.at[pl.ds(pl.multiple_of(core * rows, rows), rows), :], mine_ref),
-                (result_ref.at[pl.ds(pl.multiple_of((1 - core) * rows, rows), rows), :], theirs_ref),
-            ],
-            sems.at[pl.ds(4, 2)],
-        )
-        for copy in out:
-            copy.wait()
+        theirs_ref[...] = result_ref[pl.ds(pl.multiple_of((1 - core) * rows, rows), rows), :]
 
     @pl.when(chip == 0)
     def _():
@@ -361,25 +352,39 @@
         part(1)
 
 
+def placed(source, targets, chunk, by):
+    pairs = []
+    start = 0
+    for target in targets:
+        width = target.shape[1] // 4
+        at = pl.ds(pl.multiple_of((2 * chunk + by) * width, width), width)
+        pairs.append((source.at[:, start : start + width], target.at[:, at]))
+        start += width
+    return pairs
+
+
 def merge_kernel(
-    mine_a, mine_b, got_a, got_b, gates_a, gates_got, gates_b, hidden_ref, gq_ref, gk_ref, gv_ref, gi_ref, gf_ref, sems
+    result_a, result_b, got_a, gates_a, gates_got, gates_b, hidden_ref, gq_ref, gk_ref, gv_ref, gi_ref, gf_ref, sems
 ):
     chip, core = place()
+    rows = got_a.shape[0]
     heads = gi_ref.shape[0]
-    wq, wv = gq_ref.shape[1] // 4, gv_ref.shape[1] // 4
-    pairs = []
-    for chunk, sources in enumerate(((mine_a, got_a), (mine_b, got_b))):
-        for source, by in zip(sources, (core, 1 - core)):
-            start = 0
-            for target, width in ((gq_ref, wq), (gk_ref, wq), (gv_ref, wv), (hidden_ref, wv)):
-                at = pl.ds(pl.multiple_of((2 * chunk + by) * width, width), width)
-                pairs.append((source.at[:, start : start + width], target.at[:, at]))
-                start += width
+    targets = (gq_ref, gk_ref, gv_ref, hidden_ref)
+    mine = pl.ds(pl.multiple_of(core * rows, rows), rows)
+    pairs = placed(result_a.at[mine, :], targets, 0, core)
+    pairs += placed(result_b.at[mine, :], targets, 1, core)
+    pairs += placed(got_a, targets, 0, 1 - core)
     copies = run_copies(pairs, sems)
     gates = jnp.where(chip == 0, gates_a[...] + gates_got[...], gates_b[...])
     gi_ref[...] = gates[:heads]
     gf_ref[...] = gates[heads:]
     for copy in copies:
+        copy.wait()
+
+
+def last_kernel(got_b, h_in, q_in, k_in, v_in, hidden_ref, gq_ref, gk_ref, gv_ref, sems):
+    core = place()[1]
+    for copy in run_copies(placed(got_b, (gq_ref, gk_ref, gv_ref, hidden_ref), 1, 1 - core), sems):
         copy.wait()
 
 
@@ -393,71 +398,78 @@
     shape = jax.ShapeDtypeStruct
     vmem = pl.BlockSpec(memory_space=pltpu.VMEM)
     smem = pl.BlockSpec(memory_space=pltpu.SMEM)
-    hbm = pl.BlockSpec(memory_space=pl.ANY)
+    hbm = pl.BlockSpec(memory_space=pltpu.HBM)
     params = pltpu.CompilerParams(vmem_limit_bytes=32 * 1024 * 1024)
+    costly = pl.CostEstimate(flops=4 * 10**10, bytes_accessed=0, transcendentals=0)
     dma = pltpu.SemaphoreType.DMA
 
     def swap(value, mask):
         return lax.ppermute(value, "head", [(s, s ^ mask) for s in range(4)])
 
     cross_shape = shape((rows, width), bf16)
-    to_core, a2, a3, b2, b3, gates = pl.pallas_call(
+    own_shape = shape((2, rows, width), bf16)
+    slots = igate.shape[1]
+    to_core, a2, a3, own_qg, own_kv, gates = pl.pallas_call(
         pack_kernel,
-        out_shape=(shape((rows, 4 * width), bf16),) + (cross_shape,) * 4 + (shape((2 * heads, igate.shape[1]), f32),),
-        in_specs=[hbm] * 4 + [vmem] * 2,
-        out_specs=(hbm,) * 5 + (vmem,),
-        scratch_shapes=[dma((16,))],
+        out_shape=(shape((rows, 4 * width), bf16), cross_shape, cross_shape, own_shape, own_shape)
+        + (shape((2 * heads, slots), f32),),
+        in_specs=[hbm] * 6,
+        out_specs=(vmem,) * 6,
+        scratch_shapes=[pltpu.VMEM(igate.shape, f32), pltpu.VMEM(igate.shape, f32), dma((22,))],
         compiler_params=params,
-    )(queries, keys, values, cotangent, igate, fgate)
+    )(*(pltpu.with_memory_space_constraint(a, pltpu.HBM) for a in (queries, keys, values, cotangent, igate, fgate)))
+    from_core = swap(to_core, 1)
     gates_got = swap(gates, 2)
     a2, a3 = swap(a2, 2), swap(a3, 3)
-    from_core = swap(to_core, 1)
-    b2, b3 = swap(b2, 2), swap(b3, 3)
     both = shape((2, 2 * rows, width), bf16)
-    stats_shape = shape((4 * heads, igate.shape[1]), f32)
-    qg, kv, stats = pl.pallas_call(
+    qg, kv, send, stats = pl.pallas_call(
         functools.partial(local_kernel, qk, vw),
-        out_shape=(both, both, stats_shape),
-        in_specs=[smem] + [hbm] * 5 + [vmem] * 2,
-        out_specs=(vmem,) * 3,
+        out_shape=(both, both, shape((2 * rows, width), bf16), shape((4 * heads, slots), f32)),
+        in_specs=[smem] + [vmem] * 5,
+        out_specs=(vmem,) * 4,
+        cost_estimate=costly,
+        compiler_params=params,
+    )(lengths, own_qg, own_kv, from_core, gates, gates_got)
+    stats = swap(stats, 2)
+    chunk_b = swap(send, 2)
+
+    def cross(chunk, *received):
+        return pl.pallas_call(
+            functools.partial(cross_kernel, chunk, qk, vw),
+            out_shape=(shape((2 * rows, 2 * width), bf16), shape((rows, 2 * width), bf16), shape(gates.shape, f32)),
+            in_specs=[smem] + [vmem] * (5 + len(received)),
+            out_specs=(vmem,) * 3,
+            cost_estimate=costly,
+            scratch_shapes=[pltpu.VMEM((4 * rows, width), bf16)],
+            compiler_params=params,
+        )(lengths, qg, kv, gates, gates_got, stats, *received)
+
+    result_a, theirs_a, gates_a = cross(0, a2, a3)
+    gates_back = swap(gates_a, 2)
+    got_a = swap(theirs_a, 1)
+    result_b, theirs_b, gates_b = cross(1, chunk_b)
+    theirs_b, gates_back = lax.optimization_barrier((theirs_b, gates_back))
+    got_b = swap(theirs_b, 1)
+    out_shape = tuple(shape(a.shape, bf16) for a in (values, queries, keys, values))
+    gate_shape = shape(igate.shape, f32)
+    *outputs, grad_in, grad_forget = pl.pallas_call(
+        merge_kernel,
+        out_shape=out_shape + (gate_shape, gate_shape),
+        in_specs=[vmem] * 6,
+        out_specs=(hbm,) * 4 + (vmem,) * 2,
         scratch_shapes=[dma((12,))],
         compiler_params=params,
-    )(lengths, queries, keys, values, cotangent, from_core, gates, gates_got)
-    stats = swap(stats, 2)
-
-    def cross(chunk, same, other):
-        out_shape = shape((rows, 2 * width), bf16)
-        return pl.pallas_call(
-            functools.partial(cross_kernel, chunk, qk, vw),
-            out_shape=(out_shape, out_shape, shape(gates.shape, f32)),
-            in_specs=[smem] + [hbm] * 4 + [vmem] * 3,
-            out_specs=(hbm, hbm, vmem),
-            scratch_shapes=[
-                pltpu.VMEM((4 * rows, width), bf16),
-                pltpu.VMEM((2 * rows, width), bf16),
-                pltpu.VMEM((2 * rows, 2 * width), bf16),
-                dma((6,)),
-            ],
-            compiler_params=params,
-        )(lengths, qg, kv, same, other, gates, gates_got, stats)
-
-    mine_a, theirs_a, gates_a = cross(0, a2, a3)
-    gates_back = swap(gates_a, 2)
-    got_a = swap(theirs_a, 1)
-    mine_b, theirs_b, gates_b = cross(1, b2, b3)
-    got_b = swap(theirs_b, 1)
-    gate_shape = shape(igate.shape, f32)
-    return pl.pallas_call(
-        merge_kernel,
-        out_shape=(
-            shape(values.shape, bf16), shape(queries.shape, bf16), shape(keys.shape, bf16), shape(values.shape, bf16),
-            gate_shape, gate_shape,
-        ),
-        in_specs=[hbm] * 4 + [vmem] * 3,
-        out_specs=(hbm,) * 4 + (vmem,) * 2,
-        scratch_shapes=[dma((16,))],
+    )(result_a, result_b, got_a, gates_a, gates_back, gates_b)
+    outputs = pl.pallas_call(
+        last_kernel,
+        out_shape=out_shape,
+        in_specs=[vmem] + [hbm] * 4,
+        out_specs=(hbm,) * 4,
+        scratch_shapes=[dma((4,))],
+        input_output_aliases={1: 0, 2: 1, 3: 2, 4: 3},
         compiler_params=params,
-    )(mine_a, mine_b, got_a, got_b, gates_a, gates_back, gates_b)
+    )(got_b, *outputs)
+    return (*outputs, grad_in, grad_forget)
 
 
 def shards(*arrays):

time: 31.4 us -> 20.1 us (0.64)
  local copies, waits for them, and re-layouts: 5.06 us -> 0 us
  waiting for transfers between devices: 9.1 us -> 5.72 us
  Pallas kernels: 7.54 us -> 5.91 us
  starting transfers between devices: 8.05 us -> 6.85 us
    unnamed x12 -> x0, local copies, waits for them, and re-layouts: 5.06 us -> none
    ppermute x10 -> x9, waiting for transfers between devices: 9.1 us -> 5.72 us  [swap(): return lax.ppermute(value, 'head', [(s, s ^ mask) for s in range(4)])]
    pallas_call x2, Pallas kernels: 4.81 us -> 1.85 us  [cross(): pl.pallas_call(functools.partial(cross_kernel, chunk, qk, vw), out_shape=...]
    pallas_call x2 -> x3, Pallas kernels: 2.01 us -> 3.67 us  [the longest x1 1.48 us: split_shards(): pl.pallas_call(merge_kernel, out_shape=out_shape + (gate_shape, gate_shap...]
    ppermute x10 -> x9, starting transfers between devices: 8.05 us -> 6.85 us  [swap(): return lax.ppermute(value, 'head', [(s, s ^ mask) for s in range(4)])]
    pallas_call x1, Pallas kernels: 0.72 us -> 0.39 us  [split_shards(): pl.pallas_call(functools.partial(local_kernel, qk, vw), out_shape=(both,...]
  transfers between devices with their start and end apart: 10 -> 9, of which waited for: 4 -> 5; matrix products, arithmetic and copies ran while one was open for 0% -> 0% of each run, Pallas kernels for 18% -> 19%
where the time goes in v3:
time: 20.1 us; the launch traced here: 19.8 us
  starting transfers between devices  6.85 us (34%)
  Pallas kernels  5.91 us (29%)
  waiting for transfers between devices  5.72 us (28%)
  between operations  1.37 us (7%)
    ppermute x9, starting transfers between devices, swap(): return lax.ppermute(value, 'head', [(s, s ^ mask) for s in range(4)])  6.85 us
    ppermute x9, waiting for transfers between devices, swap(): return lax.ppermute(value, 'head', [(s, s ^ mask) for s in range(4)])  5.72 us
    pallas_call x2, Pallas kernels, cross(): pl.pallas_call(functools.partial(cross_kernel, chunk, qk, vw), out_shape=...  1.85 us
    pallas_call x1, Pallas kernels, split_shards(): pl.pallas_call(merge_kernel, out_shape=out_shape + (gate_shape, gate_shap...  1.48 us
    pallas_call x1, Pallas kernels, split_shards(): pl.pallas_call(pack_kernel, out_shape=(shape((rows, 4 * width), bf16), cr...  1.47 us
    pallas_call x1, Pallas kernels, split_shards(): pl.pallas_call(last_kernel, out_shape=out_shape, in_specs=[vmem] + [hbm]...  0.72 us
  transfers between devices with their start and end apart: 9, of which 5 were waited for; matrix products, arithmetic and copies ran while one was open for 0% of the time, Pallas kernels for 19%

profile of v3, /device:TPU:0, one launch (start us, length us, event | category | flops | bytes accessed | tf_op | source)
XLA Modules:
  0.0 19.8 jit_solution(8027974860762340068)
XLA Ops:
  0.6 1.5 %shard_map.118 = (bf16[32,6144]{1,0:T(8,128)(2,1)S(1)}, bf16[32,1536]{1,0:T(8,128)(2,1)S(1)}, bf16[32,1536]{1,0:T(8,128)(2,1)S(1)}, bf16[2,32,1536]{2,1,0:T(8,12...) custom-call(bf16[32,2048]{1,0:T(8,128)(2,1)} %q_ref.1, bf16[32,2048]{1,0:T(8,128)(2,1)} %k_ref.1, ...), custom_call_target="tpu_custom_call" | custom-call | tf_op jit(solution)/shard_map/pallas_call | solution.py:412
  2.1 0.5 %collective-permute-start = (bf16[32,6144]{1,0:T(8,128)(2,1)S(1)}, bf16[32,6144]{1,0:T(8,128)(2,1)S(1)}, u32[]{:S(2)}, u32[]{:S(2)}) collective-permute-start(bf16[32,6144]{1,0:T(8,128)(2,1)S(1)} %get-tuple-element.36), channel_id=1, source_target_pairs={{0,1},{1,0},{2,3},{3,2},{4,5},{5,4},{6,7},{7,6},{8,9},{9,8},{10,11... | collective-permute-start | bytes 1179656 | tf_op jit(solution)/shard_map/ppermute | solution.py:407
  2.6 2.6 %collective-permute-start.1 = (f32[4,128]{1,0:T(4,128)S(1)}, f32[4,128]{1,0:T(4,128)S(1)}, u32[]{:S(2)}, u32[]{:S(2)}) collective-permute-start(f32[4,128]{1,0:T(4,128)S(1)} %get-tuple-element.37.own_ref), channel_id=1, source_target_pairs={{0,2},{1,3},{2,0},{3,1},{4,6},{5,7},{6,4},{7,5},{8,10},{9,11},{10,... | collective-permute-start | bytes 6152 | tf_op jit(solution)/shard_map/ppermute | solution.py:407
  5.2 0.1 collective-permute-start.4
  5.3 1.4 %collective-permute-start.5 = (bf16[32,1536]{1,0:T(8,128)(2,1)S(1)}, bf16[32,1536]{1,0:T(8,128)(2,1)S(1)}, u32[]{:S(2)}, u32[]{:S(2)}) collective-permute-start(bf16[32,1536]{1,0:T(8,128)(2,1)S(1)} %get-tuple-element.44), channel_id=1, source_target_pairs={{0,3},{1,2},{2,1},{3,0},{4,7},{5,6},{6,5},{7,4},{8,11},{9,10},{10,... | collective-permute-start | bytes 294920 | tf_op jit(solution)/shard_map/ppermute | solution.py:407
  7.4 0.0 collective-permute-done.1.got_ref
  7.4 0.0 collective-permute-done.m1_ref
  7.4 0.4 %shard_map.119 = (bf16[2,64,1536]{2,1,0:T(8,128)(2,1)S(1)}, bf16[2,64,1536]{2,1,0:T(8,128)(2,1)S(1)}, bf16[64,1536]{1,0:T(8,128)(2,1)S(1)}, f32[8,128]{1,0:T(8,128)S(1)}) custom-call(s32[1]{0:T(128)S(6)} %copy.21.length_ref, bf16[2,32,1536]{2,1,0:T(8,128)(2,1)S(1)} %get-tuple-element.34.own_qg, bf16[2,32,1536]{2,1,0:T(8,128)(2,1)S(1)} %get-tuple-element.35.own_kv, ...), custom_call_target="tpu_custom_call" | custom-call | flops 40000000000 | tf_op jit(solution)/shard_map/pallas_call | solution.py:425
  7.8 1.6 %collective-permute-start.2 = (f32[8,128]{1,0:T(8,128)S(1)}, f32[8,128]{1,0:T(8,128)S(1)}, u32[]{:S(2)}, u32[]{:S(2)}) collective-permute-start(f32[8,128]{1,0:T(8,128)S(1)} %get-tuple-element.40), channel_id=1, source_target_pairs={{0,2},{1,3},{2,0},{3,1},{4,6},{5,7},{6,4},{7,5},{8,10},{9,11},{10,... | collective-permute-start | bytes 12296 | tf_op jit(solution)/shard_map/ppermute | solution.py:407
  9.3 0.5 %collective-permute-start.3 = (bf16[64,1536]{1,0:T(8,128)(2,1)S(1)}, bf16[64,1536]{1,0:T(8,128)(2,1)S(1)}, u32[]{:S(2)}, u32[]{:S(2)}) collective-permute-start(bf16[64,1536]{1,0:T(8,128)(2,1)S(1)} %get-tuple-element.41), channel_id=1, source_target_pairs={{0,2},{1,3},{2,0},{3,1},{4,6},{5,7},{6,4},{7,5},{8,10},{9,11},{10,... | collective-permute-start | bytes 589832 | tf_op jit(solution)/shard_map/ppermute | solution.py:407
  9.9 1.0 %collective-permute-done.4.refs_0_ = bf16[32,1536]{1,0:T(8,128)(2,1)S(1)} collective-permute-done((bf16[32,1536]{1,0:T(8,128)(2,1)S(1)}, bf16[32,1536]{1,0:T(8,128)(2,1)S(1)}, u32[]{:S(2)}, u32[]{:S(2)}) %collective-permute-start.4) | collective-permute-done | bytes 98336 | tf_op jit(solution)/shard_map/ppermute | solution.py:407
  10.8 0.6 %collective-permute-done.5.refs_1_ = bf16[32,1536]{1,0:T(8,128)(2,1)S(1)} collective-permute-done((bf16[32,1536]{1,0:T(8,128)(2,1)S(1)}, bf16[32,1536]{1,0:T(8,128)(2,1)S(1)}, u32[]{:S(2)}, u32[]{:S(2)}) %collective-permute-start.5) | collective-permute-done | bytes 98336 | tf_op jit(solution)/shard_map/ppermute | solution.py:407
  11.4 1.6 %collective-permute-done.2.stats_ref = f32[8,128]{1,0:T(8,128)S(1)} collective-permute-done((f32[8,128]{1,0:T(8,128)S(1)}, f32[8,128]{1,0:T(8,128)S(1)}, u32[]{:S(2)}, u32[]{:S(2)}) %collective-permute-start.2) | collective-permute-done | bytes 4128 | tf_op jit(solution)/shard_map/ppermute | solution.py:407
  13.0 0.9 %shard_map.121 = (bf16[64,3072]{1,0:T(8,128)(2,1)S(1)}, bf16[32,3072]{1,0:T(8,128)(2,1)S(1)}, f32[4,128]{1,0:T(4,128)S(1)}) custom-call(s32[1]{0:T(128)S(6)} %copy.21.length_ref, bf16[2,64,1536]{2,1,0:T(8,128)(2,1)S(1)} %get-tuple-element.38.qg_ref, bf16[2,64,1536]{2,1,0:T(8,128)(2,1)S(1)} %get-tuple-element.39.kv_ref, ...), custom_call_target="tpu_custom_call" | custom-call | flops 40000000000 | tf_op jit(solution)/shard_map/pallas_call | solution.py:437
  14.0 0.1 collective-permute-start.6
  14.0 0.1 collective-permute-start.8
  14.1 2.4 %collective-permute-done.3.refs_0_ = bf16[64,1536]{1,0:T(8,128)(2,1)S(1)} collective-permute-done((bf16[64,1536]{1,0:T(8,128)(2,1)S(1)}, bf16[64,1536]{1,0:T(8,128)(2,1)S(1)}, u32[]{:S(2)}, u32[]{:S(2)}) %collective-permute-start.3) | collective-permute-done | bytes 196640 | tf_op jit(solution)/shard_map/ppermute | solution.py:407
  16.5 0.9 %shard_map.120 = (bf16[64,3072]{1,0:T(8,128)(2,1)S(1)}, bf16[32,3072]{1,0:T(8,128)(2,1)S(1)}, f32[4,128]{1,0:T(4,128)S(1)}) custom-call(s32[1]{0:T(128)S(6)} %copy.21.length_ref, bf16[2,64,1536]{2,1,0:T(8,128)(2,1)S(1)} %get-tuple-element.38.qg_ref, bf16[2,64,1536]{2,1,0:T(8,128)(2,1)S(1)} %get-tuple-element.39.kv_ref, ...), custom_call_target="tpu_custom_call" | custom-call | flops 40000000000 | tf_op jit(solution)/shard_map/pallas_call | solution.py:437
  17.4 0.2 collective-permute-done.6.gates_got
  17.6 0.0 collective-permute-start.7
  17.6 0.0 collective-permute-done.8.got_a
  17.6 1.5 %shard_map.122 = (bf16[32,4096]{1,0:T(8,128)(2,1)}, bf16[32,2048]{1,0:T(8,128)(2,1)}, bf16[32,2048]{1,0:T(8,128)(2,1)}, bf16[32,4096]{1,0:T(8,128)(2,1)}, f32[2,128]{1,0:T(2,128)}, /*index=5*/f32[2,128]{1,0:T(2,128)}) custom-call(bf16[64,3072]{1,0:T(8,128)(2,1)S(1)} %get-tuple-element.47.result_a, bf16[64,3072]{1,0:T(8,128)(2,1)S(1)} %get-tuple-element.48.result_b, ...), custom_call_target="tpu_custom_call" | custom-call | tf_op jit(solution)/shard_map/pallas_call | solution.py:455
  19.1 0.0 collective-permute-done.7.got_b
  19.1 0.7 %shard_map.123 = (bf16[32,4096]{1,0:T(8,128)(2,1)}, bf16[32,2048]{1,0:T(8,128)(2,1)}, bf16[32,2048]{1,0:T(8,128)(2,1)}, bf16[32,4096]{1,0:T(8,128)(2,1)}) custom-call(bf16[32,3072]{1,0:T(8,128)(2,1)S(1)} %collective-permute-done.7.got_b, ...), custom_call_target="tpu_custom_call", output_to_operand_aliasing={{0}: (1, {}), {1}: (2, {}), {2}: (3, {}), {3}: (4, {})} | custom-call | tf_op jit(solution)/shard_map/pallas_call | solution.py:463
Async XLA Ops:
  2.1 5.3 %collective-permute-start = (bf16[32,6144]{1,0:T(8,128)(2,1)S(1)}, bf16[32,6144]{1,0:T(8,128)(2,1)S(1)}, u32[]{:S(2)}, u32[]{:S(2)}) collective-permute-start(bf16[32,6144]{1,0:T(8,128)(2,1)S(1)} %get-tuple-element.36), channel_id=1, source_target_pairs={{0,1},{1,0},{2,3},{3,2},{4,5},{5,4},{6,7},{7,6},{8,9},{9,8},{10,11... | collective-permute-start | bytes 1179656 | tf_op jit(solution)/shard_map/ppermute | solution.py:407
  2.6 4.7 %collective-permute-start.1 = (f32[4,128]{1,0:T(4,128)S(1)}, f32[4,128]{1,0:T(4,128)S(1)}, u32[]{:S(2)}, u32[]{:S(2)}) collective-permute-start(f32[4,128]{1,0:T(4,128)S(1)} %get-tuple-element.37.own_ref), channel_id=1, source_target_pairs={{0,2},{1,3},{2,0},{3,1},{4,6},{5,7},{6,4},{7,5},{8,10},{9,11},{10,... | collective-permute-start | bytes 6152 | tf_op jit(solution)/shard_map/ppermute | solution.py:407
  5.2 5.6 %collective-permute-start.4 = (bf16[32,1536]{1,0:T(8,128)(2,1)S(1)}, bf16[32,1536]{1,0:T(8,128)(2,1)S(1)}, u32[]{:S(2)}, u32[]{:S(2)}) collective-permute-start(bf16[32,1536]{1,0:T(8,128)(2,1)S(1)} %get-tuple-element.43), channel_id=1, source_target_pairs={{0,2},{1,3},{2,0},{3,1},{4,6},{5,7},{6,4},{7,5},{8,10},{9,11},{10,... | collective-permute-start | bytes 294920 | tf_op jit(solution)/shard_map/ppermute | solution.py:407
  5.3 6.1 %collective-permute-start.5 = (bf16[32,1536]{1,0:T(8,128)(2,1)S(1)}, bf16[32,1536]{1,0:T(8,128)(2,1)S(1)}, u32[]{:S(2)}, u32[]{:S(2)}) collective-permute-start(bf16[32,1536]{1,0:T(8,128)(2,1)S(1)} %get-tuple-element.44), channel_id=1, source_target_pairs={{0,3},{1,2},{2,1},{3,0},{4,7},{5,6},{6,5},{7,4},{8,11},{9,10},{10,... | collective-permute-start | bytes 294920 | tf_op jit(solution)/shard_map/ppermute | solution.py:407
  7.8 5.2 %collective-permute-start.2 = (f32[8,128]{1,0:T(8,128)S(1)}, f32[8,128]{1,0:T(8,128)S(1)}, u32[]{:S(2)}, u32[]{:S(2)}) collective-permute-start(f32[8,128]{1,0:T(8,128)S(1)} %get-tuple-element.40), channel_id=1, source_target_pairs={{0,2},{1,3},{2,0},{3,1},{4,6},{5,7},{6,4},{7,5},{8,10},{9,11},{10,... | collective-permute-start | bytes 12296 | tf_op jit(solution)/shard_map/ppermute | solution.py:407
  9.3 7.2 %collective-permute-start.3 = (bf16[64,1536]{1,0:T(8,128)(2,1)S(1)}, bf16[64,1536]{1,0:T(8,128)(2,1)S(1)}, u32[]{:S(2)}, u32[]{:S(2)}) collective-permute-start(bf16[64,1536]{1,0:T(8,128)(2,1)S(1)} %get-tuple-element.41), channel_id=1, source_target_pairs={{0,2},{1,3},{2,0},{3,1},{4,6},{5,7},{6,4},{7,5},{8,10},{9,11},{10,... | collective-permute-start | bytes 589832 | tf_op jit(solution)/shard_map/ppermute | solution.py:407
  14.0 3.7 %collective-permute-start.6 = (f32[4,128]{1,0:T(4,128)S(1)}, f32[4,128]{1,0:T(4,128)S(1)}, u32[]{:S(2)}, u32[]{:S(2)}) collective-permute-start(f32[4,128]{1,0:T(4,128)S(1)} %get-tuple-element.45.gates_a), channel_id=1, source_target_pairs={{0,2},{1,3},{2,0},{3,1},{4,6},{5,7},{6,4},{7,5},{8,10},{9,11},{10,... | collective-permute-start | bytes 6152 | tf_op jit(solution)/shard_map/ppermute | solution.py:407
  14.0 3.6 %collective-permute-start.8 = (bf16[32,3072]{1,0:T(8,128)(2,1)S(1)}, bf16[32,3072]{1,0:T(8,128)(2,1)S(1)}, u32[]{:S(2)}, u32[]{:S(2)}) collective-permute-start(bf16[32,3072]{1,0:T(8,128)(2,1)S(1)} %get-tuple-element.49), channel_id=1, source_target_pairs={{0,1},{1,0},{2,3},{3,2},{4,5},{5,4},{6,7},{7,6},{8,9},{9,8},{10,11... | collective-permute-start | bytes 589832 | tf_op jit(solution)/shard_map/ppermute | solution.py:407
  17.6 1.5 %collective-permute-start.7 = (bf16[32,3072]{1,0:T(8,128)(2,1)S(1)}, bf16[32,3072]{1,0:T(8,128)(2,1)S(1)}, u32[]{:S(2)}, u32[]{:S(2)}) collective-permute-start(bf16[32,3072]{1,0:T(8,128)(2,1)S(1)} %get-tuple-element.46), channel_id=1, source_target_pairs={{0,1},{1,0},{2,3},{3,2},{4,5},{5,4},{6,7},{7,6},{8,9},{9,8},{10,11... | collective-permute-start | bytes 589832 | tf_op jit(solution)/shard_map/ppermute | solution.py:407

commit v4 on v3

--- a/solution.py
+++ b/solution.py
@@ -140,51 +140,63 @@
     return copies
 
 
-def pack_kernel(
-    q_ref, k_ref, v_ref, g_ref, ig_ref, fg_ref, m1_ref, a2_ref, a3_ref, qg_ref, kv_ref, gates_ref, in_ref, out_ref, sems
-):
-    chip, core = place()
-    wq, wv = q_ref.shape[1] // 4, v_ref.shape[1] // 4
-    heads = ig_ref.shape[0]
-
-    def block(ref, owner, width):
-        return ref.at[:, pl.ds(pl.multiple_of(owner * width, width), width)]
-
-    def cross(first, second):
-        pairs = []
-        for target, to in ((a2_ref, core), (a3_ref, 1 - core)):
-            pairs.append((block(first, to, wq), target.at[:, :wq]))
-            pairs.append((block(second, to, wv), target.at[:, wq:]))
-        return pairs
+def block(ref, owner):
+    width = ref.shape[1] // 4
+    return ref.at[:, pl.ds(pl.multiple_of(owner * width, width), width)]
+
+
+def block_copies(refs, owner, target):
+    split = refs[0].shape[1] // 4
+    end = split + refs[1].shape[1] // 4
+    return [(block(refs[0], owner), target.at[:, :split]), (block(refs[1], owner), target.at[:, split:end])]
+
+
+def copy_for_chip(moves, inputs, sems):
+    q_ref, k_ref, v_ref, g_ref = inputs
+    chip = place()[0]
 
     @pl.when(chip == 0)
     def _():
-        run_copies(cross(k_ref, v_ref), sems)
+        run_copies(moves((k_ref, v_ref), (q_ref, g_ref)), sems)
 
     @pl.when(chip != 0)
     def _():
-        run_copies(cross(q_ref, g_ref), sems)
-
-    pairs = [(ig_ref, in_ref), (fg_ref, out_ref)]
-    for chunk in range(2):
-        start = chunk * 2 * (wq + wv)
-        for first, second, own in ((q_ref, g_ref, qg_ref), (k_ref, v_ref, kv_ref)):
-            for ref, width, at in ((first, wq, slice(0, wq)), (second, wv, slice(wq, wq + wv))):
-                pairs.append((block(ref, 2 * chunk + 1 - core, width), m1_ref.at[:, start : start + width]))
-                pairs.append((block(ref, 2 * chunk + core, width), own.at[chunk, :, at]))
-                start += width
-    copies = run_copies(pairs, sems.at[pl.ds(4, 18)])
+        run_copies(moves((q_ref, g_ref), (k_ref, v_ref)), sems)
+
+    pairs = moves((k_ref, v_ref), (q_ref, g_ref))
+    return [pltpu.make_async_copy(source, target, sems.at[i]) for i, (source, target) in enumerate(pairs)]
+
+
+def pack_kernel(
+    q_ref, k_ref, v_ref, g_ref, ig_ref, fg_ref, a2_ref, a3_ref, b2_ref, b3_ref, rest_ref, m1_ref, gates_ref,
+    in_ref, out_ref, sems,
+):
+    core = place()[1]
+    heads = ig_ref.shape[0]
+    width = b2_ref.shape[1]
+
+    def moves(sent, kept):
+        pairs = [(ig_ref, in_ref), (fg_ref, out_ref)]
+        for chunk, (same, other) in enumerate(((a2_ref, a3_ref), (b2_ref, b3_ref))):
+            pairs += block_copies(sent, 2 * chunk + core, same) + block_copies(sent, 2 * chunk + 1 - core, other)
+            pairs += block_copies(kept, 2 * chunk + core, rest_ref.at[chunk])
+            for i, refs in enumerate((sent, kept)):
+                start = (2 * chunk + i) * width
+                pairs += block_copies(refs, 2 * chunk + 1 - core, m1_ref.at[:, start : start + width])
+        return pairs
+
+    copies = copy_for_chip(moves, (q_ref, k_ref, v_ref, g_ref), sems)
     for copy in copies[:2]:
         copy.wait()
     gates_ref[:heads, :] = in_ref[...]
     gates_ref[heads:, :] = out_ref[...]
-    for i, (source, target) in enumerate(cross(k_ref, v_ref)):
-        pltpu.make_async_copy(source, target, sems.at[i]).wait()
     for copy in copies[2:]:
         copy.wait()
 
 
-def local_kernel(qk, vw, length_ref, own_qg, own_kv, m1_ref, own_ref, got_ref, qg_ref, kv_ref, send_ref, stats_ref):
+def local_kernel(
+    qk, vw, length_ref, a2_ref, b2_ref, rest_ref, m1_ref, own_ref, got_ref, qg_ref, kv_ref, stats_ref
+):
     chip, core = place()
     rows = m1_ref.shape[0]
     heads = own_ref.shape[0] // 2
@@ -192,12 +204,15 @@
     width = wq + wv
     mine = pl.ds(pl.multiple_of(core * rows, rows), rows)
     theirs = pl.ds(pl.multiple_of((1 - core) * rows, rows), rows)
-    for chunk in range(2):
-        start = chunk * 2 * width
-        qg_ref[chunk, mine, :] = own_qg[chunk]
-        qg_ref[chunk, theirs, :] = m1_ref[:, start : start + width]
-        kv_ref[chunk, mine, :] = own_kv[chunk]
-        kv_ref[chunk, theirs, :] = m1_ref[:, start + width : start + 2 * width]
+
+    def gather(sent, kept):
+        for chunk, own in enumerate((a2_ref, b2_ref)):
+            start = chunk * 2 * width
+            sent[chunk, mine, :] = own[...]
+            sent[chunk, theirs, :] = m1_ref[:, start : start + width]
+            kept[chunk, mine, :] = rest_ref[chunk]
+            kept[chunk, theirs, :] = m1_ref[:, start + width : start + 2 * width]
+
     stats_ref[...] = jnp.zeros_like(stats_ref)
     length = length_ref[0]
 
@@ -235,21 +250,39 @@
 
     @pl.when(chip == 0)
     def _():
-        send_ref[...] = kv_ref[1]
+        gather(kv_ref, qg_ref)
         part(0, 1)
 
     @pl.when(chip != 0)
     def _():
-        send_ref[...] = qg_ref[1]
+        gather(qg_ref, kv_ref)
         part(1, 0)
         part(1, 1)
 
 
+def placed(source, targets, chunk, by):
+    pairs = []
+    start = 0
+    for target in targets:
+        width = target.shape[1] // 4
+        at = pl.ds(pl.multiple_of((2 * chunk + by) * width, width), width)
+        pairs.append((source.at[:, start : start + width], target.at[:, at]))
+        start += width
+    return pairs
+
+
 def cross_kernel(
-    chunk, qk, vw, length_ref, qg_ref, kv_ref, own_ref, got_ref, stats_ref, *refs
+    chunk, qk, vw, length_ref, qg_ref, kv_ref, own_ref, got_ref, stats_ref, same_ref, other_ref, *refs
 ):
-    *cross_refs, result_ref, theirs_ref, gates_ref, wide_ref = refs
     chip, core = place()
+    writes = []
+    if chunk == 0:
+        result_ref, theirs_ref, gates_ref, wide_ref = refs
+    else:
+        result_a, result_ref, theirs_ref, gates_ref, *outputs, wide_ref, sems = refs
+        rows = theirs_ref.shape[0]
+        mine_a = result_a.at[pl.ds(pl.multiple_of(core * rows, rows), rows), :]
+        writes = run_copies(placed(mine_a, outputs, 0, core), sems)
     rows = theirs_ref.shape[0]
     size = 2 * rows
     heads = own_ref.shape[0] // 2
@@ -258,11 +291,8 @@
     def gather(side, local):
         base = 0 if side else size
         wide_ref[side * size : (side + 1) * size, :] = local[chunk]
-        if len(cross_refs) == 1:
-            wide_ref[base : base + size, :] = cross_refs[0][...]
-        else:
-            for ref, by in zip(cross_refs, (core, 1 - core)):
-                wide_ref[pl.ds(pl.multiple_of(base + by * rows, rows), rows), :] = ref[...]
+        for ref, by in ((same_ref, core), (other_ref, 1 - core)):
+            wide_ref[pl.ds(pl.multiple_of(base + by * rows, rows), rows), :] = ref[...]
 
     length = length_ref[0]
     gates_ref[...] = jnp.zeros_like(gates_ref)
@@ -351,40 +381,28 @@
     def _():
         part(1)
 
-
-def placed(source, targets, chunk, by):
-    pairs = []
-    start = 0
-    for target in targets:
-        width = target.shape[1] // 4
-        at = pl.ds(pl.multiple_of((2 * chunk + by) * width, width), width)
-        pairs.append((source.at[:, start : start + width], target.at[:, at]))
-        start += width
-    return pairs
-
-
-def merge_kernel(
-    result_a, result_b, got_a, gates_a, gates_got, gates_b, hidden_ref, gq_ref, gk_ref, gv_ref, gi_ref, gf_ref, sems
-):
+    for copy in writes:
+        copy.wait()
+
+
+def merge_kernel(result_b, got_a, gates_a, gates_got, gates_b, *refs):
+    *outputs, gi_ref, gf_ref, gates_ref, sems = refs[4:]
     chip, core = place()
     rows = got_a.shape[0]
     heads = gi_ref.shape[0]
-    targets = (gq_ref, gk_ref, gv_ref, hidden_ref)
-    mine = pl.ds(pl.multiple_of(core * rows, rows), rows)
-    pairs = placed(result_a.at[mine, :], targets, 0, core)
-    pairs += placed(result_b.at[mine, :], targets, 1, core)
-    pairs += placed(got_a, targets, 0, 1 - core)
-    copies = run_copies(pairs, sems)
+    mine = result_b.at[pl.ds(pl.multiple_of(core * rows, rows), rows), :]
+    copies = run_copies(placed(mine, outputs, 1, core) + placed(got_a, outputs, 0, 1 - core), sems)
     gates = jnp.where(chip == 0, gates_a[...] + gates_got[...], gates_b[...])
-    gi_ref[...] = gates[:heads]
-    gf_ref[...] = gates[heads:]
+    gates_ref[0] = gates[:heads]
+    gates_ref[1] = gates[heads:]
+    copies += run_copies([(gates_ref.at[0], gi_ref), (gates_ref.at[1], gf_ref)], sems.at[pl.ds(8, 2)])
     for copy in copies:
         copy.wait()
 
 
-def last_kernel(got_b, h_in, q_in, k_in, v_in, hidden_ref, gq_ref, gk_ref, gv_ref, sems):
-    core = place()[1]
-    for copy in run_copies(placed(got_b, (gq_ref, gk_ref, gv_ref, hidden_ref), 1, 1 - core), sems):
+def last_kernel(got_b, *refs):
+    *outputs, sems = refs[4:]
+    for copy in run_copies(placed(got_b, outputs, 1, 1 - place()[1]), sems):
         copy.wait()
 
 
@@ -406,61 +424,63 @@
     def swap(value, mask):
         return lax.ppermute(value, "head", [(s, s ^ mask) for s in range(4)])
 
+    slots = igate.shape[1]
+    gates_shape = shape((2 * heads, slots), f32)
+    arrays = [pltpu.with_memory_space_constraint(a, pltpu.HBM) for a in (queries, keys, values, cotangent, igate, fgate)]
     cross_shape = shape((rows, width), bf16)
-    own_shape = shape((2, rows, width), bf16)
-    slots = igate.shape[1]
-    to_core, a2, a3, own_qg, own_kv, gates = pl.pallas_call(
+    a2_sent, a3, b2_sent, b3, rest, to_core, gates = pl.pallas_call(
         pack_kernel,
-        out_shape=(shape((rows, 4 * width), bf16), cross_shape, cross_shape, own_shape, own_shape)
-        + (shape((2 * heads, slots), f32),),
+        out_shape=(cross_shape,) * 4 + (shape((2, rows, width), bf16), shape((rows, 4 * width), bf16), gates_shape),
         in_specs=[hbm] * 6,
-        out_specs=(vmem,) * 6,
+        out_specs=(vmem,) * 7,
         scratch_shapes=[pltpu.VMEM(igate.shape, f32), pltpu.VMEM(igate.shape, f32), dma((22,))],
         compiler_params=params,
-    )(*(pltpu.with_memory_space_constraint(a, pltpu.HBM) for a in (queries, keys, values, cotangent, igate, fgate)))
+    )(*arrays)
     from_core = swap(to_core, 1)
     gates_got = swap(gates, 2)
-    a2, a3 = swap(a2, 2), swap(a3, 3)
+    a2, a3 = swap(a2_sent, 2), swap(a3, 3)
     both = shape((2, 2 * rows, width), bf16)
-    qg, kv, send, stats = pl.pallas_call(
+    qg, kv, stats = pl.pallas_call(
         functools.partial(local_kernel, qk, vw),
-        out_shape=(both, both, shape((2 * rows, width), bf16), shape((4 * heads, slots), f32)),
-        in_specs=[smem] + [vmem] * 5,
-        out_specs=(vmem,) * 4,
+        out_shape=(both, both, shape((4 * heads, slots), f32)),
+        in_specs=[smem] + [vmem] * 6,
+        out_specs=(vmem,) * 3,
         cost_estimate=costly,
         compiler_params=params,
-    )(lengths, own_qg, own_kv, from_core, gates, gates_got)
+    )(lengths, a2_sent, b2_sent, rest, from_core, gates, gates_got)
     stats = swap(stats, 2)
-    chunk_b = swap(send, 2)
-
-    def cross(chunk, *received):
+    b2, b3 = swap(b2_sent, 2), swap(b3, 3)
+    out_shape = tuple(shape(a.shape, bf16) for a in (queries, keys, values, values))
+
+    def cross(chunk, received, written):
         return pl.pallas_call(
             functools.partial(cross_kernel, chunk, qk, vw),
-            out_shape=(shape((2 * rows, 2 * width), bf16), shape((rows, 2 * width), bf16), shape(gates.shape, f32)),
-            in_specs=[smem] + [vmem] * (5 + len(received)),
-            out_specs=(vmem,) * 3,
+            out_shape=(shape((2 * rows, 2 * width), bf16), shape((rows, 2 * width), bf16), gates_shape)
+            + (out_shape if written else ()),
+            in_specs=[smem] + [vmem] * (7 + len(written)),
+            out_specs=(vmem,) * 3 + ((hbm,) * 4 if written else ()),
+            scratch_shapes=[pltpu.VMEM((4 * rows, width), bf16)] + ([dma((4,))] if written else []),
             cost_estimate=costly,
-            scratch_shapes=[pltpu.VMEM((4 * rows, width), bf16)],
             compiler_params=params,
-        )(lengths, qg, kv, gates, gates_got, stats, *received)
-
-    result_a, theirs_a, gates_a = cross(0, a2, a3)
+        )(lengths, qg, kv, gates, gates_got, stats, *received, *written)
+
+    result_a, theirs_a, gates_a = cross(0, (a2, a3), ())
     gates_back = swap(gates_a, 2)
     got_a = swap(theirs_a, 1)
-    result_b, theirs_b, gates_b = cross(1, chunk_b)
-    theirs_b, gates_back = lax.optimization_barrier((theirs_b, gates_back))
+    result_b, theirs_b, gates_b, *outputs = cross(1, (b2, b3), (result_a,))
     got_b = swap(theirs_b, 1)
-    out_shape = tuple(shape(a.shape, bf16) for a in (values, queries, keys, values))
     gate_shape = shape(igate.shape, f32)
     *outputs, grad_in, grad_forget = pl.pallas_call(
         merge_kernel,
         out_shape=out_shape + (gate_shape, gate_shape),
-        in_specs=[vmem] * 6,
-        out_specs=(hbm,) * 4 + (vmem,) * 2,
-        scratch_shapes=[dma((12,))],
+        in_specs=[vmem] * 5 + [hbm] * 4,
+        out_specs=(hbm,) * 6,
+        scratch_shapes=[pltpu.VMEM((2, *igate.shape), f32), dma((10,))],
+        cost_estimate=costly,
+        input_output_aliases={5: 0, 6: 1, 7: 2, 8: 3},
         compiler_params=params,
-    )(result_a, result_b, got_a, gates_a, gates_back, gates_b)
-    outputs = pl.pallas_call(
+    )(result_b, got_a, gates_a, gates_back, gates_b, *outputs)
+    gq, gk, gv, hidden = pl.pallas_call(
         last_kernel,
         out_shape=out_shape,
         in_specs=[vmem] + [hbm] * 4,
@@ -469,7 +489,7 @@
         input_output_aliases={1: 0, 2: 1, 3: 2, 4: 3},
         compiler_params=params,
     )(got_b, *outputs)
-    return (*outputs, grad_in, grad_forget)
+    return hidden, gq, gk, gv, grad_in, grad_forget
 
 
 def shards(*arrays):

time: 20.1 us -> 19.7 us (0.980)
  starting transfers between devices: 6.85 us -> 7.6 us
  Pallas kernels: 5.91 us -> 5.26 us
  waiting for transfers between devices: 5.72 us -> 5.29 us
    ppermute x9 -> x10, starting transfers between devices: 6.85 us -> 7.6 us  [swap(): return lax.ppermute(value, 'head', [(s, s ^ mask) for s in range(4)])]
    pallas_call x1, Pallas kernels: 1.48 us -> 0.83 us  [split_shards(): pl.pallas_call(merge_kernel, out_shape=out_shape + (gate_shape, gate_shap...]
    ppermute x9 -> x10, waiting for transfers between devices: 5.72 us -> 5.29 us  [swap(): return lax.ppermute(value, 'head', [(s, s ^ mask) for s in range(4)])]
  transfers between devices with their start and end apart: 9 -> 10, of which waited for: 5 -> 4; matrix products, arithmetic and copies ran while one was open for 0% -> 0% of each run, Pallas kernels for 19% -> 16%
where the time goes in v4:
time: 19.7 us; the launch traced here: 19.5 us
  starting transfers between devices  7.6 us (39%)
  waiting for transfers between devices  5.29 us (27%)
  Pallas kernels  5.26 us (27%)
  between operations  1.35 us (7%)
    ppermute x10, starting transfers between devices, swap(): return lax.ppermute(value, 'head', [(s, s ^ mask) for s in range(4)])  7.6 us
    ppermute x10, waiting for transfers between devices, swap(): return lax.ppermute(value, 'head', [(s, s ^ mask) for s in range(4)])  5.29 us
    pallas_call x2, Pallas kernels, cross(): pl.pallas_call(functools.partial(cross_kernel, chunk, qk, vw), out_shape=...  1.91 us
    pallas_call x1, Pallas kernels, split_shards(): pl.pallas_call(pack_kernel, out_shape=(cross_shape,) * 4 + (shape((2, row...  1.47 us
    pallas_call x1, Pallas kernels, split_shards(): pl.pallas_call(merge_kernel, out_shape=out_shape + (gate_shape, gate_shap...  0.83 us
    pallas_call x1, Pallas kernels, split_shards(): pl.pallas_call(last_kernel, out_shape=out_shape, in_specs=[vmem] + [hbm]...  0.71 us
  transfers between devices with their start and end apart: 10, of which 4 were waited for; matrix products, arithmetic and copies ran while one was open for 0% of the time, Pallas kernels for 16%

profile of v4, /device:TPU:0, one launch (start us, length us, event | category | flops | bytes accessed | tf_op | source)
XLA Modules:
  0.0 19.5 jit_solution(845667441568054891)
XLA Ops:
  0.6 1.5 %shard_map.118 = (bf16[32,1536]{1,0:T(8,128)(2,1)S(1)}, bf16[32,1536]{1,0:T(8,128)(2,1)S(1)}, bf16[32,1536]{1,0:T(8,128)(2,1)S(1)}, bf16[32,1536]{1,0:T(8,128)(2...) custom-call(bf16[32,2048]{1,0:T(8,128)(2,1)} %q_ref.1, ...), custom_call_target="tpu_custom_call" | custom-call | tf_op jit(solution)/shard_map/pallas_call | solution.py:431
  2.1 0.5 %collective-permute-start = (bf16[32,6144]{1,0:T(8,128)(2,1)S(1)}, bf16[32,6144]{1,0:T(8,128)(2,1)S(1)}, u32[]{:S(2)}, u32[]{:S(2)}) collective-permute-start(bf16[32,6144]{1,0:T(8,128)(2,1)S(1)} %get-tuple-element.39), channel_id=1, source_target_pairs={{0,1},{1,0},{2,3},{3,2},{4,5},{5,4},{6,7},{7,6},{8,9},{9,8},{10,11... | collective-permute-start | bytes 1179656 | tf_op jit(solution)/shard_map/ppermute | solution.py:425
  2.6 2.6 %collective-permute-start.1 = (f32[4,128]{1,0:T(4,128)S(1)}, f32[4,128]{1,0:T(4,128)S(1)}, u32[]{:S(2)}, u32[]{:S(2)}) collective-permute-start(f32[4,128]{1,0:T(4,128)S(1)} %get-tuple-element.40.own_ref), channel_id=1, source_target_pairs={{0,2},{1,3},{2,0},{3,1},{4,6},{5,7},{6,4},{7,5},{8,10},{9,11},{10,... | collective-permute-start | bytes 6152 | tf_op jit(solution)/shard_map/ppermute | solution.py:425
  5.2 0.1 collective-permute-start.6
  5.3 1.7 %collective-permute-start.5 = (bf16[32,1536]{1,0:T(8,128)(2,1)S(1)}, bf16[32,1536]{1,0:T(8,128)(2,1)S(1)}, u32[]{:S(2)}, u32[]{:S(2)}) collective-permute-start(bf16[32,1536]{1,0:T(8,128)(2,1)S(1)} %get-tuple-element.36.a2_ref), channel_id=1, source_target_pairs={{0,2},{1,3},{2,0},{3,1},{4,6},{5,7},{6,4},{7,5},{8,10},{9,11},{10,... | collective-permute-start | bytes 294920 | tf_op jit(solution)/shard_map/ppermute | solution.py:425
  7.7 0.0 collective-permute-done.1.got_ref
  7.7 0.0 collective-permute-done.m1_ref
  7.7 0.4 %shard_map.119 = (bf16[2,64,1536]{2,1,0:T(8,128)(2,1)S(1)}, bf16[2,64,1536]{2,1,0:T(8,128)(2,1)S(1)}, f32[8,128]{1,0:T(8,128)S(1)}) custom-call(s32[1]{0:T(128)S(6)} %copy.29.length_ref, bf16[32,1536]{1,0:T(8,128)(2,1)S(1)} %get-tuple-element.36.a2_ref, bf16[32,1536]{1,0:T(8,128)(2,1)S(1)} %get-tuple-element.37.b2_ref, ...), custom_call_target="tpu_custom_call" | custom-call | flops 40000000000 | tf_op jit(solution)/shard_map/pallas_call | solution.py:443
  8.1 1.3 %collective-permute-start.2 = (f32[8,128]{1,0:T(8,128)S(1)}, f32[8,128]{1,0:T(8,128)S(1)}, u32[]{:S(2)}, u32[]{:S(2)}) collective-permute-start(f32[8,128]{1,0:T(8,128)S(1)} %get-tuple-element.43), channel_id=1, source_target_pairs={{0,2},{1,3},{2,0},{3,1},{4,6},{5,7},{6,4},{7,5},{8,10},{9,11},{10,... | collective-permute-start | bytes 12296 | tf_op jit(solution)/shard_map/ppermute | solution.py:425
  9.3 0.8 %collective-permute-start.3 = (bf16[32,1536]{1,0:T(8,128)(2,1)S(1)}, bf16[32,1536]{1,0:T(8,128)(2,1)S(1)}, u32[]{:S(2)}, u32[]{:S(2)}) collective-permute-start(bf16[32,1536]{1,0:T(8,128)(2,1)S(1)} %get-tuple-element.37.b2_ref), channel_id=1, source_target_pairs={{0,2},{1,3},{2,0},{3,1},{4,6},{5,7},{6,4},{7,5},{8,10},{9,11},{10,... | collective-permute-start | bytes 294920 | tf_op jit(solution)/shard_map/ppermute | solution.py:425
  10.2 0.0 collective-permute-done.6.other_ref
  10.2 2.6 %collective-permute-done.5.same_ref = bf16[32,1536]{1,0:T(8,128)(2,1)S(1)} collective-permute-done((bf16[32,1536]{1,0:T(8,128)(2,1)S(1)}, bf16[32,1536]{1,0:T(8,128)(2,1)S(1)}, u32[]{:S(2)}, u32[]{:S(2)}) %collective-permute-start.5) | collective-permute-done | bytes 98336 | tf_op jit(solution)/shard_map/ppermute | solution.py:425
  12.8 0.1 collective-permute-done.2.stats_ref
  12.9 0.9 %shard_map.120 = (bf16[64,3072]{1,0:T(8,128)(2,1)S(1)}, bf16[32,3072]{1,0:T(8,128)(2,1)S(1)}, f32[4,128]{1,0:T(4,128)S(1)}) custom-call(s32[1]{0:T(128)S(6)} %copy.29.length_ref, bf16[2,64,1536]{2,1,0:T(8,128)(2,1)S(1)} %get-tuple-element.41.qg_ref, bf16[2,64,1536]{2,1,0:T(8,128)(2,1)S(1)} %get-tuple-element.42.kv_ref, ...), custom_call_target="tpu_custom_call" | custom-call | flops 40000000000 | tf_op jit(solution)/shard_map/pallas_call | solution.py:456
  13.8 0.2 %collective-permute-start.9 = (f32[4,128]{1,0:T(4,128)S(1)}, f32[4,128]{1,0:T(4,128)S(1)}, u32[]{:S(2)}, u32[]{:S(2)}) collective-permute-start(f32[4,128]{1,0:T(4,128)S(1)} %get-tuple-element.50.gates_a), channel_id=1, source_target_pairs={{0,2},{1,3},{2,0},{3,1},{4,6},{5,7},{6,4},{7,5},{8,10},{9,11},{10,... | collective-permute-start | bytes 6152 | tf_op jit(solution)/shard_map/ppermute | solution.py:425
  14.0 0.0 collective-permute-start.8
  14.0 2.3 %collective-permute-done.4.other_ref = bf16[32,1536]{1,0:T(8,128)(2,1)S(1)} collective-permute-done((bf16[32,1536]{1,0:T(8,128)(2,1)S(1)}, bf16[32,1536]{1,0:T(8,128)(2,1)S(1)}, u32[]{:S(2)}, u32[]{:S(2)}) %collective-permute-start.4) | collective-permute-done | bytes 98336 | tf_op jit(solution)/shard_map/ppermute | solution.py:425
  16.3 1.0 %shard_map.121 = (bf16[64,3072]{1,0:T(8,128)(2,1)S(1)}, bf16[32,3072]{1,0:T(8,128)(2,1)S(1)}, f32[4,128]{1,0:T(4,128)S(1)}, bf16[32,2048]{1,0:T(8,128)(2,1)}, bf...) custom-call(s32[1]{0:T(128)S(6)} %copy.29.length_ref, ...), custom_call_target="tpu_custom_call" | custom-call | flops 40000000000 | tf_op jit(solution)/shard_map/pallas_call | solution.py:456
  17.3 0.3 %collective-permute-start.7 = (bf16[32,3072]{1,0:T(8,128)(2,1)S(1)}, bf16[32,3072]{1,0:T(8,128)(2,1)S(1)}, u32[]{:S(2)}, u32[]{:S(2)}) collective-permute-start(bf16[32,3072]{1,0:T(8,128)(2,1)S(1)} %get-tuple-element.47), channel_id=1, source_target_pairs={{0,1},{1,0},{2,3},{3,2},{4,5},{5,4},{6,7},{7,6},{8,9},{9,8},{10,11... | collective-permute-start | bytes 589832 | tf_op jit(solution)/shard_map/ppermute | solution.py:425
  17.6 0.0 collective-permute-done.9.gates_got
  17.6 0.0 collective-permute-done.8.got_a
  17.6 0.8 %shard_map.122 = (bf16[32,2048]{1,0:T(8,128)(2,1)}, bf16[32,2048]{1,0:T(8,128)(2,1)}, bf16[32,4096]{1,0:T(8,128)(2,1)}, bf16[32,4096]{1,0:T(8,128)(2,1)}, f32[2,128]{1,0:T(2,128)}, /*index=5*/f32[2,128]{1,0:T(2,128)}) custom-call(bf16[64,3072]{1,0:T(8,128)(2,1)S(1)} %get-tuple-element.48.resu, ...), custom_call_target="tpu_custom_call", output_to_operand_aliasing={{0}: (5, {}), {1}: (6, {}), {2}: (7, {}), {3}: (8, {})} | custom-call | flops 40000000000 | tf_op jit(solution)/shard_map/pallas_call | solution.py:473
  18.5 0.3 %collective-permute-done.7.got_b = bf16[32,3072]{1,0:T(8,128)(2,1)S(1)} collective-permute-done((bf16[32,3072]{1,0:T(8,128)(2,1)S(1)}, bf16[32,3072]{1,0:T(8,128)(2,1)S(1)}, u32[]{:S(2)}, u32[]{:S(2)}) %collective-permute-start.7) | collective-permute-done | bytes 196640 | tf_op jit(solution)/shard_map/ppermute | solution.py:425
  18.8 0.7 %shard_map.123 = (bf16[32,2048]{1,0:T(8,128)(2,1)}, bf16[32,2048]{1,0:T(8,128)(2,1)}, bf16[32,4096]{1,0:T(8,128)(2,1)}, bf16[32,4096]{1,0:T(8,128)(2,1)}) custom-call(bf16[32,3072]{1,0:T(8,128)(2,1)S(1)} %collective-permute-done.7.got_b, ...), custom_call_target="tpu_custom_call", output_to_operand_aliasing={{0}: (1, {}), {1}: (2, {}), {2}: (3, {}), {3}: (4, {})} | custom-call | tf_op jit(solution)/shard_map/pallas_call | solution.py:483
  (2 shorter events, 0.0 us)
Async XLA Ops:
  2.1 5.6 %collective-permute-start = (bf16[32,6144]{1,0:T(8,128)(2,1)S(1)}, bf16[32,6144]{1,0:T(8,128)(2,1)S(1)}, u32[]{:S(2)}, u32[]{:S(2)}) collective-permute-start(bf16[32,6144]{1,0:T(8,128)(2,1)S(1)} %get-tuple-element.39), channel_id=1, source_target_pairs={{0,1},{1,0},{2,3},{3,2},{4,5},{5,4},{6,7},{7,6},{8,9},{9,8},{10,11... | collective-permute-start | bytes 1179656 | tf_op jit(solution)/shard_map/ppermute | solution.py:425
  2.6 5.1 %collective-permute-start.1 = (f32[4,128]{1,0:T(4,128)S(1)}, f32[4,128]{1,0:T(4,128)S(1)}, u32[]{:S(2)}, u32[]{:S(2)}) collective-permute-start(f32[4,128]{1,0:T(4,128)S(1)} %get-tuple-element.40.own_ref), channel_id=1, source_target_pairs={{0,2},{1,3},{2,0},{3,1},{4,6},{5,7},{6,4},{7,5},{8,10},{9,11},{10,... | collective-permute-start | bytes 6152 | tf_op jit(solution)/shard_map/ppermute | solution.py:425
  5.2 4.9 %collective-permute-start.6 = (bf16[32,1536]{1,0:T(8,128)(2,1)S(1)}, bf16[32,1536]{1,0:T(8,128)(2,1)S(1)}, u32[]{:S(2)}, u32[]{:S(2)}) collective-permute-start(bf16[32,1536]{1,0:T(8,128)(2,1)S(1)} %get-tuple-element.45), channel_id=1, source_target_pairs={{0,3},{1,2},{2,1},{3,0},{4,7},{5,6},{6,5},{7,4},{8,11},{9,10},{10,... | collective-permute-start | bytes 294920 | tf_op jit(solution)/shard_map/ppermute | solution.py:425
  5.3 7.5 %collective-permute-start.5 = (bf16[32,1536]{1,0:T(8,128)(2,1)S(1)}, bf16[32,1536]{1,0:T(8,128)(2,1)S(1)}, u32[]{:S(2)}, u32[]{:S(2)}) collective-permute-start(bf16[32,1536]{1,0:T(8,128)(2,1)S(1)} %get-tuple-element.36.a2_ref), channel_id=1, source_target_pairs={{0,2},{1,3},{2,0},{3,1},{4,6},{5,7},{6,4},{7,5},{8,10},{9,11},{10,... | collective-permute-start | bytes 294920 | tf_op jit(solution)/shard_map/ppermute | solution.py:425
  8.1 4.8 %collective-permute-start.2 = (f32[8,128]{1,0:T(8,128)S(1)}, f32[8,128]{1,0:T(8,128)S(1)}, u32[]{:S(2)}, u32[]{:S(2)}) collective-permute-start(f32[8,128]{1,0:T(8,128)S(1)} %get-tuple-element.43), channel_id=1, source_target_pairs={{0,2},{1,3},{2,0},{3,1},{4,6},{5,7},{6,4},{7,5},{8,10},{9,11},{10,... | collective-permute-start | bytes 12296 | tf_op jit(solution)/shard_map/ppermute | solution.py:425
  9.3 7.0 %collective-permute-start.3 = (bf16[32,1536]{1,0:T(8,128)(2,1)S(1)}, bf16[32,1536]{1,0:T(8,128)(2,1)S(1)}, u32[]{:S(2)}, u32[]{:S(2)}) collective-permute-start(bf16[32,1536]{1,0:T(8,128)(2,1)S(1)} %get-tuple-element.37.b2_ref), channel_id=1, source_target_pairs={{0,2},{1,3},{2,0},{3,1},{4,6},{5,7},{6,4},{7,5},{8,10},{9,11},{10,... | collective-permute-start | bytes 294920 | tf_op jit(solution)/shard_map/ppermute | solution.py:425
  10.2 6.1 %collective-permute-start.4 = (bf16[32,1536]{1,0:T(8,128)(2,1)S(1)}, bf16[32,1536]{1,0:T(8,128)(2,1)S(1)}, u32[]{:S(2)}, u32[]{:S(2)}) collective-permute-start(bf16[32,1536]{1,0:T(8,128)(2,1)S(1)} %get-tuple-element.44), channel_id=1, source_target_pairs={{0,3},{1,2},{2,1},{3,0},{4,7},{5,6},{6,5},{7,4},{8,11},{9,10},{10,... | collective-permute-start | bytes 294920 | tf_op jit(solution)/shard_map/ppermute | solution.py:425
  13.8 3.8 %collective-permute-start.9 = (f32[4,128]{1,0:T(4,128)S(1)}, f32[4,128]{1,0:T(4,128)S(1)}, u32[]{:S(2)}, u32[]{:S(2)}) collective-permute-start(f32[4,128]{1,0:T(4,128)S(1)} %get-tuple-element.50.gates_a), channel_id=1, source_target_pairs={{0,2},{1,3},{2,0},{3,1},{4,6},{5,7},{6,4},{7,5},{8,10},{9,11},{10,... | collective-permute-start | bytes 6152 | tf_op jit(solution)/shard_map/ppermute | solution.py:425
  14.0 3.6 %collective-permute-start.8 = (bf16[32,3072]{1,0:T(8,128)(2,1)S(1)}, bf16[32,3072]{1,0:T(8,128)(2,1)S(1)}, u32[]{:S(2)}, u32[]{:S(2)}) collective-permute-start(bf16[32,3072]{1,0:T(8,128)(2,1)S(1)} %get-tuple-element.49), channel_id=1, source_target_pairs={{0,1},{1,0},{2,3},{3,2},{4,5},{5,4},{6,7},{7,6},{8,9},{9,8},{10,11... | collective-permute-start | bytes 589832 | tf_op jit(solution)/shard_map/ppermute | solution.py:425
  17.3 1.5 %collective-permute-start.7 = (bf16[32,3072]{1,0:T(8,128)(2,1)S(1)}, bf16[32,3072]{1,0:T(8,128)(2,1)S(1)}, u32[]{:S(2)}, u32[]{:S(2)}) collective-permute-start(bf16[32,3072]{1,0:T(8,128)(2,1)S(1)} %get-tuple-element.47), channel_id=1, source_target_pairs={{0,1},{1,0},{2,3},{3,2},{4,5},{5,4},{6,7},{7,6},{8,9},{9,8},{10,11... | collective-permute-start | bytes 589832 | tf_op jit(solution)/shard_map/ppermute | solution.py:425

commit v5 on v4

--- a/solution.py
+++ b/solution.py
@@ -168,18 +168,17 @@
 
 
 def pack_kernel(
-    q_ref, k_ref, v_ref, g_ref, ig_ref, fg_ref, a2_ref, a3_ref, b2_ref, b3_ref, rest_ref, m1_ref, gates_ref,
-    in_ref, out_ref, sems,
+    q_ref, k_ref, v_ref, g_ref, ig_ref, fg_ref, a2_ref, d_ref, m1_ref, gates_ref, in_ref, out_ref, sems
 ):
     core = place()[1]
     heads = ig_ref.shape[0]
-    width = b2_ref.shape[1]
+    width = a2_ref.shape[1]
 
     def moves(sent, kept):
         pairs = [(ig_ref, in_ref), (fg_ref, out_ref)]
-        for chunk, (same, other) in enumerate(((a2_ref, a3_ref), (b2_ref, b3_ref))):
-            pairs += block_copies(sent, 2 * chunk + core, same) + block_copies(sent, 2 * chunk + 1 - core, other)
-            pairs += block_copies(kept, 2 * chunk + core, rest_ref.at[chunk])
+        pairs += block_copies(sent, core, a2_ref)
+        for chunk in range(2):
+            pairs += block_copies(sent, 2 * chunk + 1 - core, d_ref.at[:, chunk * width : (chunk + 1) * width])
             for i, refs in enumerate((sent, kept)):
                 start = (2 * chunk + i) * width
                 pairs += block_copies(refs, 2 * chunk + 1 - core, m1_ref.at[:, start : start + width])
@@ -191,6 +190,17 @@
     gates_ref[:heads, :] = in_ref[...]
     gates_ref[heads:, :] = out_ref[...]
     for copy in copies[2:]:
+        copy.wait()
+
+
+def rest_kernel(q_ref, k_ref, v_ref, g_ref, b2_ref, rest_ref, sems):
+    core = place()[1]
+
+    def moves(sent, kept):
+        pairs = block_copies(sent, 2 + core, b2_ref)
+        return pairs + block_copies(kept, core, rest_ref.at[0]) + block_copies(kept, 2 + core, rest_ref.at[1])
+
+    for copy in copy_for_chip(moves, (q_ref, k_ref, v_ref, g_ref), sems):
         copy.wait()
 
 
@@ -216,48 +226,49 @@
     stats_ref[...] = jnp.zeros_like(stats_ref)
     length = length_ref[0]
 
-    def part(side, chunk):
-        gates = own_ref if side == chunk else got_ref
+    def part(side, chunks):
         size = 2 * rows
         low = side * size
-        for head in range(heads):
-            q = qg_ref[chunk, :, head * qk : (head + 1) * qk]
-            k = kv_ref[chunk, :, head * qk : (head + 1) * qk]
-            g = qg_ref[chunk, :, wq + head * vw : wq + (head + 1) * vw]
-            v = kv_ref[chunk, :, wq + head * vw : wq + (head + 1) * vw]
+        items = [(chunk, head) for chunk in chunks for head in range(heads)]
+        scores, pulled = [], []
+        for chunk, head in items:
+            first = slice(head * qk, (head + 1) * qk)
+            second = slice(wq + head * vw, wq + (head + 1) * vw)
+            scores.append(dot(qg_ref[chunk, :, first], kv_ref[chunk, :, first], NT))
+            pulled.append(dot(qg_ref[chunk, :, second], kv_ref[chunk, :, second], NT))
+        for i, (chunk, head) in enumerate(items):
+            gates = own_ref if side == chunk else got_ref
             weight = decay(gates[head : head + 1, :], gates[heads + head : heads + head + 1, :], length, qk**-0.5)
-            weight = weight[low : low + size, low : low + size]
-            scores = dot(q, k, NT) * weight
-            pulled = dot(g, v, NT)
-            norm = jnp.sum(scores, axis=1, keepdims=True)
-            along = jnp.sum(scores * pulled, axis=1, keepdims=True)
-            on = lax.broadcasted_iota(jnp.int32, (size, 2 * size), 0) + low == lax.broadcasted_iota(
-                jnp.int32, (size, 2 * size), 1
-            )
-
-            def as_row(column):
-                return jnp.sum(jnp.where(on, column, 0.0), axis=0, keepdims=True)
-
+            scores[i] = scores[i] * weight[low : low + size, low : low + size]
+        norms = [jnp.sum(score, axis=1, keepdims=True) for score in scores]
+        alongs = [jnp.sum(score * pull, axis=1, keepdims=True) for score, pull in zip(scores, pulled)]
+        on = lax.broadcasted_iota(jnp.int32, (size, 2 * size), 0) + low == lax.broadcasted_iota(
+            jnp.int32, (size, 2 * size), 1
+        )
+
+        def as_row(column):
+            return jnp.sum(jnp.where(on, column, 0.0), axis=0, keepdims=True)
+
+        for (chunk, head), score, pull, norm, along in zip(items, scores, pulled, norms, alongs):
             if side == 1:
                 at = chunk * heads + head
                 stats_ref[at : at + 1, :] = as_row(norm)
                 stats_ref[2 * heads + at : 2 * heads + at + 1, :] = as_row(along)
             else:
                 inverse, grad_norm, by_row = backward_terms(norm, along)
-                by_column = jnp.sum((pulled * inverse + grad_norm) * scores, axis=0, keepdims=True)
+                by_column = jnp.sum((pull * inverse + grad_norm) * score, axis=0, keepdims=True)
                 stats_ref[head : head + 1, :size] = by_column
                 stats_ref[heads + head : heads + head + 1, :] = as_row(by_row)
 
     @pl.when(chip == 0)
     def _():
         gather(kv_ref, qg_ref)
-        part(0, 1)
+        part(0, (1,))
 
     @pl.when(chip != 0)
     def _():
         gather(qg_ref, kv_ref)
-        part(1, 0)
-        part(1, 1)
+        part(1, (0, 1))
 
 
 def placed(source, targets, chunk, by):
@@ -292,7 +303,8 @@
         base = 0 if side else size
         wide_ref[side * size : (side + 1) * size, :] = local[chunk]
         for ref, by in ((same_ref, core), (other_ref, 1 - core)):
-            wide_ref[pl.ds(pl.multiple_of(base + by * rows, rows), rows), :] = ref[...]
+            start = chunk * (wq + wv) if ref is other_ref else 0
+            wide_ref[pl.ds(pl.multiple_of(base + by * rows, rows), rows), :] = ref[:, start : start + wq + wv]
 
     length = length_ref[0]
     gates_ref[...] = jnp.zeros_like(gates_ref)
@@ -312,42 +324,45 @@
             decay(gates[head : head + 1, :], gates[heads + head : heads + head + 1, :], length, qk**-0.5)
             for head in range(heads)
         ]
-        for head in range(heads):
+        each = range(heads)
+        loaded = []
+        for head in each:
             first = slice(head * qk, (head + 1) * qk)
             second = slice(wq + head * vw, wq + (head + 1) * vw)
-            if side == 0:
-                q, g, k, v = wide_ref[:, first], wide_ref[:, second], thin[:, first], thin[:, second]
-                weight = weights[head][:, :size]
-            else:
-                k, v, q, g = wide_ref[:, first], wide_ref[:, second], thin[:, first], thin[:, second]
-                weight = weights[head][size:, :]
-            scores = dot(q, k, NT) * weight
-            pulled = dot(g, v, NT)
-            norm = jnp.sum(scores, axis=1, keepdims=True)
-            along = jnp.sum(scores * pulled, axis=1, keepdims=True)
-            if side == 0:
-                at = chunk * heads + head
-                norm = norm + as_column(stats_ref[at : at + 1, :])
-                along = along + as_column(stats_ref[2 * heads + at : 2 * heads + at + 1, :])
-            inverse, grad_norm, by_row = backward_terms(norm, along)
-            grad_scores = pulled * inverse + grad_norm
-            scaled = scores * inverse
-            grad_raw = grad_scores * weight
-            if side == 0:
-                hidden = wide_dot(scaled[:size], v, NN)
-                gq = wide_dot(grad_raw[:size], k, NN)
-                gk = wide_dot(grad_raw.T, q, NN)
-                gv = wide_dot(scaled.T, g, NN)
-            else:
-                hidden = wide_dot(scaled, v, NN)
-                gq = wide_dot(grad_raw, k, NN)
-                gk = wide_dot(grad_raw.T[size:], q, NN)
-                gv = wide_dot(scaled.T[size:], g, NN)
-            result_ref[:, head * qk : (head + 1) * qk] = gq.astype(jnp.bfloat16)
-            result_ref[:, wq + head * qk : wq + (head + 1) * qk] = gk.astype(jnp.bfloat16)
-            result_ref[:, 2 * wq + head * vw : 2 * wq + (head + 1) * vw] = gv.astype(jnp.bfloat16)
-            result_ref[:, 2 * wq + wv + head * vw : 2 * wq + wv + (head + 1) * vw] = hidden.astype(jnp.bfloat16)
-            by_column = jnp.sum(grad_scores * scores, axis=0, keepdims=True)
+            of_wide, of_thin = (wide_ref[:, first], wide_ref[:, second]), (thin[:, first], thin[:, second])
+            loaded.append(of_wide + of_thin if side == 0 else of_thin + of_wide)
+        weights = [weight[:, :size] if side == 0 else weight[size:, :] for weight in weights]
+        scores = [dot(q, k, NT) for q, g, k, v in loaded]
+        pulled = [dot(g, v, NT) for q, g, k, v in loaded]
+        scores = [scores[head] * weights[head] for head in each]
+        norms = [jnp.sum(scores[head], axis=1, keepdims=True) for head in each]
+        alongs = [jnp.sum(scores[head] * pulled[head], axis=1, keepdims=True) for head in each]
+        if side == 0:
+            at = chunk * heads
+            norms = [norms[head] + as_column(stats_ref[at + head : at + head + 1, :]) for head in each]
+            at += 2 * heads
+            alongs = [alongs[head] + as_column(stats_ref[at + head : at + head + 1, :]) for head in each]
+        terms = [backward_terms(norms[head], alongs[head]) for head in each]
+        grad_scores = [pulled[head] * terms[head][0] + terms[head][1] for head in each]
+        scaled = [scores[head] * terms[head][0] for head in each]
+        grad_raw = [grad_scores[head] * weights[head] for head in each]
+        turned = [(scaled[head].T, grad_raw[head].T) for head in each]
+        if side == 0:
+            scaled, grad_raw = [value[:size] for value in scaled], [value[:size] for value in grad_raw]
+        else:
+            turned = [(one[size:], other[size:]) for one, other in turned]
+        sections = ((0, qk), (wq, qk), (2 * wq, vw), (2 * wq + wv, vw))
+        for section, (start, step) in enumerate(sections):
+            for head in each:
+                q, g, k, v = loaded[head]
+                left, right = (
+                    (grad_raw[head], k), (turned[head][1], q), (turned[head][0], g), (scaled[head], v)
+                )[section]
+                value = wide_dot(left, right, NN).astype(jnp.bfloat16)
+                result_ref[:, start + head * step : start + (head + 1) * step] = value
+        for head in each:
+            by_column = jnp.sum(grad_scores[head] * scores[head], axis=0, keepdims=True)
+            by_row = terms[head][2]
             forget = gates[heads + head : heads + head + 1, :]
             live = cols_at[:1] < length
             slope = jnp.where(live, 1.0 / (1.0 + jnp.exp(forget)), 0.0)
@@ -428,17 +443,26 @@
     gates_shape = shape((2 * heads, slots), f32)
     arrays = [pltpu.with_memory_space_constraint(a, pltpu.HBM) for a in (queries, keys, values, cotangent, igate, fgate)]
     cross_shape = shape((rows, width), bf16)
-    a2_sent, a3, b2_sent, b3, rest, to_core, gates = pl.pallas_call(
+    a2_sent, d, to_core, gates = pl.pallas_call(
         pack_kernel,
-        out_shape=(cross_shape,) * 4 + (shape((2, rows, width), bf16), shape((rows, 4 * width), bf16), gates_shape),
+        out_shape=(cross_shape, shape((rows, 2 * width), bf16), shape((rows, 4 * width), bf16), gates_shape),
         in_specs=[hbm] * 6,
-        out_specs=(vmem,) * 7,
-        scratch_shapes=[pltpu.VMEM(igate.shape, f32), pltpu.VMEM(igate.shape, f32), dma((22,))],
+        out_specs=(vmem,) * 4,
+        scratch_shapes=[pltpu.VMEM(igate.shape, f32), pltpu.VMEM(igate.shape, f32), dma((16,))],
         compiler_params=params,
     )(*arrays)
+    b2_sent, rest = pl.pallas_call(
+        rest_kernel,
+        out_shape=(cross_shape, shape((2, rows, width), bf16)),
+        in_specs=[hbm] * 4,
+        out_specs=(vmem,) * 2,
+        scratch_shapes=[dma((6,))],
+        compiler_params=params,
+    )(*arrays[:4])
     from_core = swap(to_core, 1)
     gates_got = swap(gates, 2)
-    a2, a3 = swap(a2_sent, 2), swap(a3, 3)
+    a2, d = swap(a2_sent, 2), swap(d, 3)
+    a2, gates_got = lax.optimization_barrier((a2, gates_got))
     both = shape((2, 2 * rows, width), bf16)
     qg, kv, stats = pl.pallas_call(
         functools.partial(local_kernel, qk, vw),
@@ -449,7 +473,7 @@
         compiler_params=params,
     )(lengths, a2_sent, b2_sent, rest, from_core, gates, gates_got)
     stats = swap(stats, 2)
-    b2, b3 = swap(b2_sent, 2), swap(b3, 3)
+    b2 = swap(b2_sent, 2)
     out_shape = tuple(shape(a.shape, bf16) for a in (queries, keys, values, values))
 
     def cross(chunk, received, written):
@@ -464,10 +488,10 @@
             compiler_params=params,
         )(lengths, qg, kv, gates, gates_got, stats, *received, *written)
 
-    result_a, theirs_a, gates_a = cross(0, (a2, a3), ())
+    result_a, theirs_a, gates_a = cross(0, (a2, d), ())
     gates_back = swap(gates_a, 2)
     got_a = swap(theirs_a, 1)
-    result_b, theirs_b, gates_b, *outputs = cross(1, (b2, b3), (result_a,))
+    result_b, theirs_b, gates_b, *outputs = cross(1, (b2, d), (result_a,))
     got_b = swap(theirs_b, 1)
     gate_shape = shape(igate.shape, f32)
     *outputs, grad_in, grad_forget = pl.pallas_call(

time: 19.7 us -> 19 us (0.964)
  waiting for transfers between devices: 5.29 us -> 2.42 us
  starting transfers between devices: 7.6 us -> 9.25 us
  Pallas kernels: 5.26 us -> 5.78 us
    ppermute x10 -> x9, waiting for transfers between devices: 5.29 us -> 2.42 us  [swap(): return lax.ppermute(value, 'head', [(s, s ^ mask) for s in range(4)])]
    ppermute x10 -> x9, starting transfers between devices: 7.6 us -> 9.25 us  [swap(): return lax.ppermute(value, 'head', [(s, s ^ mask) for s in range(4)])]
    pallas_call x1 -> x2, Pallas kernels: 1.47 us -> 2.33 us  [the longest x1 1.32 us: split_shards(): pl.pallas_call(pack_kernel, out_shape=(cross_shape, shape((rows, 2 * widt...]
    pallas_call x2, Pallas kernels: 1.91 us -> 1.55 us  [cross(): pl.pallas_call(functools.partial(cross_kernel, chunk, qk, vw), out_shape=...]
  transfers between devices with their start and end apart: 10 -> 9, of which waited for: 4 -> 4; matrix products, arithmetic and copies ran while one was open for 0% -> 0% of each run, Pallas kernels for 16% -> 20%
where the time goes in v5:
time: 19 us; the launch traced here: 18.8 us
  starting transfers between devices  9.25 us (49%)
  Pallas kernels  5.78 us (30%)
  waiting for transfers between devices  2.42 us (13%)
  between operations  1.34 us (7%)
    ppermute x9, starting transfers between devices, swap(): return lax.ppermute(value, 'head', [(s, s ^ mask) for s in range(4)])  9.25 us
    ppermute x9, waiting for transfers between devices, swap(): return lax.ppermute(value, 'head', [(s, s ^ mask) for s in range(4)])  2.42 us
    pallas_call x2, Pallas kernels, cross(): pl.pallas_call(functools.partial(cross_kernel, chunk, qk, vw), out_shape=...  1.55 us
    pallas_call x1, Pallas kernels, split_shards(): pl.pallas_call(pack_kernel, out_shape=(cross_shape, shape((rows, 2 * widt...  1.32 us
    pallas_call x1, Pallas kernels, split_shards(): pl.pallas_call(rest_kernel, out_shape=(cross_shape, shape((2, rows, width...  1.01 us
    pallas_call x1, Pallas kernels, split_shards(): pl.pallas_call(merge_kernel, out_shape=out_shape + (gate_shape, gate_shap...  0.83 us
    pallas_call x1, Pallas kernels, split_shards(): pl.pallas_call(last_kernel, out_shape=out_shape, in_specs=[vmem] + [hbm]...  0.72 us
  transfers between devices with their start and end apart: 9, of which 4 were waited for; matrix products, arithmetic and copies ran while one was open for 0% of the time, Pallas kernels for 20%

profile of v5, /device:TPU:0, one launch (start us, length us, event | category | flops | bytes accessed | tf_op | source)
XLA Modules:
  0.0 18.8 jit_solution(8945561505697648246)
XLA Ops:
  0.6 1.3 %shard_map.118 = (bf16[32,1536]{1,0:T(8,128)(2,1)S(1)}, bf16[32,3072]{1,0:T(8,128)(2,1)S(1)}, bf16[32,6144]{1,0:T(8,128)(2,1)S(1)}, f32[4,128]{1,0:T(4,128)S(1)}) custom-call(bf16[32,2048]{1,0:T(8,128)(2,1)} %q_ref.3, bf16[32,2048]{1,0:T(8,128)(2,1)} %k_ref.3, bf16[32,4096]{1,0:T(8,128)(2,1)} %v_ref.3, bf16[32,4096]{1,0:T(8,128)(2,1)} %g_ref.3, ...), custom_call_target="tpu_custom_call" | custom-call | tf_op jit(solution)/shard_map/pallas_call | solution.py:446
  2.0 0.5 %collective-permute-start = (bf16[32,6144]{1,0:T(8,128)(2,1)S(1)}, bf16[32,6144]{1,0:T(8,128)(2,1)S(1)}, u32[]{:S(2)}, u32[]{:S(2)}) collective-permute-start(bf16[32,6144]{1,0:T(8,128)(2,1)S(1)} %get-tuple-element.40), channel_id=1, source_target_pairs={{0,1},{1,0},{2,3},{3,2},{4,5},{5,4},{6,7},{7,6},{8,9},{9,8},{10,11... | collective-permute-start | bytes 1179656 | tf_op jit(solution)/shard_map/ppermute | solution.py:440
  2.5 2.6 %collective-permute-start.1 = (bf16[32,1536]{1,0:T(8,128)(2,1)S(1)}, bf16[32,1536]{1,0:T(8,128)(2,1)S(1)}, u32[]{:S(2)}, u32[]{:S(2)}) collective-permute-start(bf16[32,1536]{1,0:T(8,128)(2,1)S(1)} %get-tuple-element.37.a2_ref), channel_id=1, source_target_pairs={{0,2},{1,3},{2,0},{3,1},{4,6},{5,7},{6,4},{7,5},{8,10},{9,11},{10,... | collective-permute-start | bytes 294920 | tf_op jit(solution)/shard_map/ppermute | solution.py:440
  5.1 0.1 collective-permute-start.2
  5.2 1.4 %collective-permute-start.5 = (bf16[32,3072]{1,0:T(8,128)(2,1)S(1)}, bf16[32,3072]{1,0:T(8,128)(2,1)S(1)}, u32[]{:S(2)}, u32[]{:S(2)}) collective-permute-start(bf16[32,3072]{1,0:T(8,128)(2,1)S(1)} %get-tuple-element.46), channel_id=1, source_target_pairs={{0,3},{1,2},{2,1},{3,0},{4,7},{5,6},{6,5},{7,4},{8,11},{9,10},{10,... | collective-permute-start | bytes 589832 | tf_op jit(solution)/shard_map/ppermute | solution.py:440
  6.6 1.0 %shard_map.119 = (bf16[32,1536]{1,0:T(8,128)(2,1)S(1)}, bf16[2,32,1536]{2,1,0:T(8,128)(2,1)S(1)}) custom-call(bf16[32,2048]{1,0:T(8,128)(2,1)} %q_ref.3, bf16[32,2048]{1,0:T(8,128)(2,1)} %k_ref.3, bf16[32,4096]{1,0:T(8,128)(2,1)} %v_ref.3, bf16[32,4096]{1,0:T(8,128)(2,1)} %g_ref.3), custom_call_target="tpu_custom_call" | custom-call | tf_op jit(solution)/shard_map/pallas_call | solution.py:454
  8.3 0.5 %collective-permute-done.2.got_ref = f32[4,128]{1,0:T(4,128)S(1)} collective-permute-done((f32[4,128]{1,0:T(4,128)S(1)}, f32[4,128]{1,0:T(4,128)S(1)}, u32[]{:S(2)}, u32[]{:S(2)}) %collective-permute-start.2) | collective-permute-done | bytes 2080 | tf_op jit(solution)/shard_map/ppermute | solution.py:440
  8.8 0.0 collective-permute-done.1.same_ref
  8.8 0.0 collective-permute-done.m1_ref
  8.8 0.4 %shard_map.120 = (bf16[2,64,1536]{2,1,0:T(8,128)(2,1)S(1)}, bf16[2,64,1536]{2,1,0:T(8,128)(2,1)S(1)}, f32[8,128]{1,0:T(8,128)S(1)}) custom-call(s32[1]{0:T(128)S(6)} %copy.29.length_ref, bf16[32,1536]{1,0:T(8,128)(2,1)S(1)} %get-tuple-element.37.a2_ref, bf16[32,1536]{1,0:T(8,128)(2,1)S(1)} %get-tuple-element.38.b2_ref, ...), custom_call_target="tpu_custom_call" | custom-call | flops 40000000000 | tf_op jit(solution)/shard_map/pallas_call | solution.py:467
  9.1 1.8 %collective-permute-start.3 = (f32[8,128]{1,0:T(8,128)S(1)}, f32[8,128]{1,0:T(8,128)S(1)}, u32[]{:S(2)}, u32[]{:S(2)}) collective-permute-start(f32[8,128]{1,0:T(8,128)S(1)} %get-tuple-element.45), channel_id=1, source_target_pairs={{0,2},{1,3},{2,0},{3,1},{4,6},{5,7},{6,4},{7,5},{8,10},{9,11},{10,... | collective-permute-start | bytes 12296 | tf_op jit(solution)/shard_map/ppermute | solution.py:440
  10.9 0.3 %collective-permute-start.4 = (bf16[32,1536]{1,0:T(8,128)(2,1)S(1)}, bf16[32,1536]{1,0:T(8,128)(2,1)S(1)}, u32[]{:S(2)}, u32[]{:S(2)}) collective-permute-start(bf16[32,1536]{1,0:T(8,128)(2,1)S(1)} %get-tuple-element.38.b2_ref), channel_id=1, source_target_pairs={{0,2},{1,3},{2,0},{3,1},{4,6},{5,7},{6,4},{7,5},{8,10},{9,11},{10,... | collective-permute-start | bytes 294920 | tf_op jit(solution)/shard_map/ppermute | solution.py:440
  11.2 1.2 %collective-permute-done.5.other_ref = bf16[32,3072]{1,0:T(8,128)(2,1)S(1)} collective-permute-done((bf16[32,3072]{1,0:T(8,128)(2,1)S(1)}, bf16[32,3072]{1,0:T(8,128)(2,1)S(1)}, u32[]{:S(2)}, u32[]{:S(2)}) %collective-permute-start.5) | collective-permute-done | bytes 196640 | tf_op jit(solution)/shard_map/ppermute | solution.py:440
  12.5 0.4 %collective-permute-done.3.stats_ref = f32[8,128]{1,0:T(8,128)S(1)} collective-permute-done((f32[8,128]{1,0:T(8,128)S(1)}, f32[8,128]{1,0:T(8,128)S(1)}, u32[]{:S(2)}, u32[]{:S(2)}) %collective-permute-start.3) | collective-permute-done | bytes 4128 | tf_op jit(solution)/shard_map/ppermute | solution.py:440
  12.8 0.8 %shard_map.121 = (bf16[64,3072]{1,0:T(8,128)(2,1)S(1)}, bf16[32,3072]{1,0:T(8,128)(2,1)S(1)}, f32[4,128]{1,0:T(4,128)S(1)}) custom-call(s32[1]{0:T(128)S(6)} %copy.29.length_ref, bf16[2,64,1536]{2,1,0:T(8,128)(2,1)S(1)} %get-tuple-element.43.qg_ref, bf16[2,64,1536]{2,1,0:T(8,128)(2,1)S(1)} %get-tuple-element.44.kv_ref, ...), custom_call_target="tpu_custom_call" | custom-call | flops 40000000000 | tf_op jit(solution)/shard_map/pallas_call | solution.py:480
  13.6 2.0 %collective-permute-start.8 = (f32[4,128]{1,0:T(4,128)S(1)}, f32[4,128]{1,0:T(4,128)S(1)}, u32[]{:S(2)}, u32[]{:S(2)}) collective-permute-start(f32[4,128]{1,0:T(4,128)S(1)} %get-tuple-element.52.gates_a), channel_id=1, source_target_pairs={{0,2},{1,3},{2,0},{3,1},{4,6},{5,7},{6,4},{7,5},{8,10},{9,11},{10,... | collective-permute-start | bytes 6152 | tf_op jit(solution)/shard_map/ppermute | solution.py:440
  15.5 0.0 collective-permute-start.7
  15.5 0.0 collective-permute-done.4.same_ref
  15.6 0.8 %shard_map.122 = (bf16[64,3072]{1,0:T(8,128)(2,1)S(1)}, bf16[32,3072]{1,0:T(8,128)(2,1)S(1)}, f32[4,128]{1,0:T(4,128)S(1)}, bf16[32,2048]{1,0:T(8,128)(2,1)}, bf...) custom-call(s32[1]{0:T(128)S(6)} %copy.29.length_ref, ...), custom_call_target="tpu_custom_call" | custom-call | flops 40000000000 | tf_op jit(solution)/shard_map/pallas_call | solution.py:480
  16.3 0.6 %collective-permute-start.6 = (bf16[32,3072]{1,0:T(8,128)(2,1)S(1)}, bf16[32,3072]{1,0:T(8,128)(2,1)S(1)}, u32[]{:S(2)}, u32[]{:S(2)}) collective-permute-start(bf16[32,3072]{1,0:T(8,128)(2,1)S(1)} %get-tuple-element.49), channel_id=1, source_target_pairs={{0,1},{1,0},{2,3},{3,2},{4,5},{5,4},{6,7},{7,6},{8,9},{9,8},{10,11... | collective-permute-start | bytes 589832 | tf_op jit(solution)/shard_map/ppermute | solution.py:440
  16.9 0.3 %collective-permute-done.8.gates_got = f32[4,128]{1,0:T(4,128)S(1)} collective-permute-done((f32[4,128]{1,0:T(4,128)S(1)}, f32[4,128]{1,0:T(4,128)S(1)}, u32[]{:S(2)}, u32[]{:S(2)}) %collective-permute-start.8) | collective-permute-done | bytes 2080 | tf_op jit(solution)/shard_map/ppermute | solution.py:440
  17.2 0.8 %shard_map.123 = (bf16[32,2048]{1,0:T(8,128)(2,1)}, bf16[32,2048]{1,0:T(8,128)(2,1)}, bf16[32,4096]{1,0:T(8,128)(2,1)}, bf16[32,4096]{1,0:T(8,128)(2,1)}, f32[2,128]{1,0:T(2,128)}, /*index=5*/f32[2,128]{1,0:T(2,128)}) custom-call(bf16[64,3072]{1,0:T(8,128)(2,1)S(1)} %get-tuple-element.50.resu, ...), custom_call_target="tpu_custom_call", output_to_operand_aliasing={{0}: (5, {}), {1}: (6, {}), {2}: (7, {}), {3}: (8, {})} | custom-call | flops 40000000000 | tf_op jit(solution)/shard_map/pallas_call | solution.py:497
  18.1 0.0 collective-permute-done.6.got_b
  18.1 0.7 %shard_map.124 = (bf16[32,2048]{1,0:T(8,128)(2,1)}, bf16[32,2048]{1,0:T(8,128)(2,1)}, bf16[32,4096]{1,0:T(8,128)(2,1)}, bf16[32,4096]{1,0:T(8,128)(2,1)}) custom-call(bf16[32,3072]{1,0:T(8,128)(2,1)S(1)} %collective-permute-done.6.got_b, ...), custom_call_target="tpu_custom_call", output_to_operand_aliasing={{0}: (1, {}), {1}: (2, {}), {2}: (3, {}), {3}: (4, {})} | custom-call | tf_op jit(solution)/shard_map/pallas_call | solution.py:507
  (1 shorter events, 0.0 us)
Async XLA Ops:
  2.0 6.8 %collective-permute-start = (bf16[32,6144]{1,0:T(8,128)(2,1)S(1)}, bf16[32,6144]{1,0:T(8,128)(2,1)S(1)}, u32[]{:S(2)}, u32[]{:S(2)}) collective-permute-start(bf16[32,6144]{1,0:T(8,128)(2,1)S(1)} %get-tuple-element.40), channel_id=1, source_target_pairs={{0,1},{1,0},{2,3},{3,2},{4,5},{5,4},{6,7},{7,6},{8,9},{9,8},{10,11... | collective-permute-start | bytes 1179656 | tf_op jit(solution)/shard_map/ppermute | solution.py:440
  2.5 6.3 %collective-permute-start.1 = (bf16[32,1536]{1,0:T(8,128)(2,1)S(1)}, bf16[32,1536]{1,0:T(8,128)(2,1)S(1)}, u32[]{:S(2)}, u32[]{:S(2)}) collective-permute-start(bf16[32,1536]{1,0:T(8,128)(2,1)S(1)} %get-tuple-element.37.a2_ref), channel_id=1, source_target_pairs={{0,2},{1,3},{2,0},{3,1},{4,6},{5,7},{6,4},{7,5},{8,10},{9,11},{10,... | collective-permute-start | bytes 294920 | tf_op jit(solution)/shard_map/ppermute | solution.py:440
  5.1 3.7 %collective-permute-start.2 = (f32[4,128]{1,0:T(4,128)S(1)}, f32[4,128]{1,0:T(4,128)S(1)}, u32[]{:S(2)}, u32[]{:S(2)}) collective-permute-start(f32[4,128]{1,0:T(4,128)S(1)} %get-tuple-element.41.own_ref), channel_id=1, source_target_pairs={{0,2},{1,3},{2,0},{3,1},{4,6},{5,7},{6,4},{7,5},{8,10},{9,11},{10,... | collective-permute-start | bytes 6152 | tf_op jit(solution)/shard_map/ppermute | solution.py:440
  5.2 7.3 %collective-permute-start.5 = (bf16[32,3072]{1,0:T(8,128)(2,1)S(1)}, bf16[32,3072]{1,0:T(8,128)(2,1)S(1)}, u32[]{:S(2)}, u32[]{:S(2)}) collective-permute-start(bf16[32,3072]{1,0:T(8,128)(2,1)S(1)} %get-tuple-element.46), channel_id=1, source_target_pairs={{0,3},{1,2},{2,1},{3,0},{4,7},{5,6},{6,5},{7,4},{8,11},{9,10},{10,... | collective-permute-start | bytes 589832 | tf_op jit(solution)/shard_map/ppermute | solution.py:440
  9.1 3.7 %collective-permute-start.3 = (f32[8,128]{1,0:T(8,128)S(1)}, f32[8,128]{1,0:T(8,128)S(1)}, u32[]{:S(2)}, u32[]{:S(2)}) collective-permute-start(f32[8,128]{1,0:T(8,128)S(1)} %get-tuple-element.45), channel_id=1, source_target_pairs={{0,2},{1,3},{2,0},{3,1},{4,6},{5,7},{6,4},{7,5},{8,10},{9,11},{10,... | collective-permute-start | bytes 12296 | tf_op jit(solution)/shard_map/ppermute | solution.py:440
  10.9 4.6 %collective-permute-start.4 = (bf16[32,1536]{1,0:T(8,128)(2,1)S(1)}, bf16[32,1536]{1,0:T(8,128)(2,1)S(1)}, u32[]{:S(2)}, u32[]{:S(2)}) collective-permute-start(bf16[32,1536]{1,0:T(8,128)(2,1)S(1)} %get-tuple-element.38.b2_ref), channel_id=1, source_target_pairs={{0,2},{1,3},{2,0},{3,1},{4,6},{5,7},{6,4},{7,5},{8,10},{9,11},{10,... | collective-permute-start | bytes 294920 | tf_op jit(solution)/shard_map/ppermute | solution.py:440
  13.6 3.7 %collective-permute-start.8 = (f32[4,128]{1,0:T(4,128)S(1)}, f32[4,128]{1,0:T(4,128)S(1)}, u32[]{:S(2)}, u32[]{:S(2)}) collective-permute-start(f32[4,128]{1,0:T(4,128)S(1)} %get-tuple-element.52.gates_a), channel_id=1, source_target_pairs={{0,2},{1,3},{2,0},{3,1},{4,6},{5,7},{6,4},{7,5},{8,10},{9,11},{10,... | collective-permute-start | bytes 6152 | tf_op jit(solution)/shard_map/ppermute | solution.py:440
  15.5 1.7 %collective-permute-start.7 = (bf16[32,3072]{1,0:T(8,128)(2,1)S(1)}, bf16[32,3072]{1,0:T(8,128)(2,1)S(1)}, u32[]{:S(2)}, u32[]{:S(2)}) collective-permute-start(bf16[32,3072]{1,0:T(8,128)(2,1)S(1)} %get-tuple-element.51), channel_id=1, source_target_pairs={{0,1},{1,0},{2,3},{3,2},{4,5},{5,4},{6,7},{7,6},{8,9},{9,8},{10,11... | collective-permute-start | bytes 589832 | tf_op jit(solution)/shard_map/ppermute | solution.py:440
  16.3 1.7 %collective-permute-start.6 = (bf16[32,3072]{1,0:T(8,128)(2,1)S(1)}, bf16[32,3072]{1,0:T(8,128)(2,1)S(1)}, u32[]{:S(2)}, u32[]{:S(2)}) collective-permute-start(bf16[32,3072]{1,0:T(8,128)(2,1)S(1)} %get-tuple-element.49), channel_id=1, source_target_pairs={{0,1},{1,0},{2,3},{3,2},{4,5},{5,4},{6,7},{7,6},{8,9},{9,8},{10,11... | collective-permute-start | bytes 589832 | tf_op jit(solution)/shard_map/ppermute | solution.py:440

commit v6 on v5

--- a/solution.py
+++ b/solution.py
@@ -167,16 +167,36 @@
     return [pltpu.make_async_copy(source, target, sems.at[i]) for i, (source, target) in enumerate(pairs)]
 
 
-def pack_kernel(
-    q_ref, k_ref, v_ref, g_ref, ig_ref, fg_ref, a2_ref, d_ref, m1_ref, gates_ref, in_ref, out_ref, sems
-):
+def pack_kernel(q_ref, k_ref, v_ref, g_ref, ig_ref, fg_ref, a2_ref, gates_ref, in_ref, out_ref, sems):
     core = place()[1]
-    heads = ig_ref.shape[0]
-    width = a2_ref.shape[1]
+    heads, slots = ig_ref.shape
+    width = a2_ref.shape[1] - slots
 
     def moves(sent, kept):
-        pairs = [(ig_ref, in_ref), (fg_ref, out_ref)]
-        pairs += block_copies(sent, core, a2_ref)
+        return [(ig_ref, in_ref), (fg_ref, out_ref)] + block_copies(sent, core, a2_ref)
+
+    copies = copy_for_chip(moves, (q_ref, k_ref, v_ref, g_ref), sems)
+    for copy in copies[:2]:
+        copy.wait()
+    gates_ref[:heads, :] = in_ref[...]
+    gates_ref[heads:, :] = out_ref[...]
+    gates = gates_ref[...]
+    terms = []
+    for _ in range(3):
+        terms.append(gates.astype(jnp.bfloat16).astype(jnp.float32))
+        gates = gates - terms[-1]
+    terms.append(jnp.zeros((a2_ref.shape[0] - 6 * heads, slots), jnp.float32))
+    a2_ref[:, width:] = jnp.concatenate(terms, axis=0).astype(jnp.bfloat16)
+    for copy in copies[2:]:
+        copy.wait()
+
+
+def more_kernel(q_ref, k_ref, v_ref, g_ref, d_ref, m1_ref, sems):
+    core = place()[1]
+    width = m1_ref.shape[1] // 4
+
+    def moves(sent, kept):
+        pairs = []
         for chunk in range(2):
             pairs += block_copies(sent, 2 * chunk + 1 - core, d_ref.at[:, chunk * width : (chunk + 1) * width])
             for i, refs in enumerate((sent, kept)):
@@ -184,12 +204,7 @@
                 pairs += block_copies(refs, 2 * chunk + 1 - core, m1_ref.at[:, start : start + width])
         return pairs
 
-    copies = copy_for_chip(moves, (q_ref, k_ref, v_ref, g_ref), sems)
-    for copy in copies[:2]:
-        copy.wait()
-    gates_ref[:heads, :] = in_ref[...]
-    gates_ref[heads:, :] = out_ref[...]
-    for copy in copies[2:]:
+    for copy in copy_for_chip(moves, (q_ref, k_ref, v_ref, g_ref), sems):
         copy.wait()
 
 
@@ -202,6 +217,12 @@
 
     for copy in copy_for_chip(moves, (q_ref, k_ref, v_ref, g_ref), sems):
         copy.wait()
+
+
+def join_kernel(a2_got, got_ref):
+    count, slots = got_ref.shape
+    terms = a2_got[:, a2_got.shape[1] - slots :].astype(jnp.float32)
+    got_ref[...] = terms[:count] + terms[count : 2 * count] + terms[2 * count : 3 * count]
 
 
 def local_kernel(
@@ -218,7 +239,7 @@
     def gather(sent, kept):
         for chunk, own in enumerate((a2_ref, b2_ref)):
             start = chunk * 2 * width
-            sent[chunk, mine, :] = own[...]
+            sent[chunk, mine, :] = own[:, :width]
             sent[chunk, theirs, :] = m1_ref[:, start : start + width]
             kept[chunk, mine, :] = rest_ref[chunk]
             kept[chunk, theirs, :] = m1_ref[:, start + width : start + 2 * width]
@@ -400,24 +421,32 @@
         copy.wait()
 
 
-def merge_kernel(result_b, got_a, gates_a, gates_got, gates_b, *refs):
-    *outputs, gi_ref, gf_ref, gates_ref, sems = refs[4:]
-    chip, core = place()
+def hold_kernel(in_ref, out_ref):
+    out_ref[...] = in_ref[...]
+
+
+def merge_kernel(result_b, got_a, gates_in, *refs):
+    *outputs, gates_ref, sems = refs[4:]
+    core = place()[1]
     rows = got_a.shape[0]
-    heads = gi_ref.shape[0]
     mine = result_b.at[pl.ds(pl.multiple_of(core * rows, rows), rows), :]
     copies = run_copies(placed(mine, outputs, 1, core) + placed(got_a, outputs, 0, 1 - core), sems)
-    gates = jnp.where(chip == 0, gates_a[...] + gates_got[...], gates_b[...])
-    gates_ref[0] = gates[:heads]
-    gates_ref[1] = gates[heads:]
-    copies += run_copies([(gates_ref.at[0], gi_ref), (gates_ref.at[1], gf_ref)], sems.at[pl.ds(8, 2)])
+    gates_ref[...] = gates_in[...]
     for copy in copies:
         copy.wait()
 
 
-def last_kernel(got_b, *refs):
-    *outputs, sems = refs[4:]
-    for copy in run_copies(placed(got_b, outputs, 1, 1 - place()[1]), sems):
+def gates_kernel(gates_a, gates_got, gates_b, gi_ref, gf_ref):
+    heads = gi_ref.shape[0]
+    gates = jnp.where(place()[0] == 0, gates_a[...] + gates_got[...], gates_b[...])
+    gi_ref[...] = gates[:heads]
+    gf_ref[...] = gates[heads:]
+
+
+def last_kernel(got_b, gi_in, gf_in, *refs):
+    *outputs, gi_ref, gf_ref, sems = refs[4:]
+    pairs = placed(got_b, outputs, 1, 1 - place()[1]) + [(gi_in, gi_ref), (gf_in, gf_ref)]
+    for copy in run_copies(pairs, sems):
         copy.wait()
 
 
@@ -433,7 +462,11 @@
     smem = pl.BlockSpec(memory_space=pltpu.SMEM)
     hbm = pl.BlockSpec(memory_space=pltpu.HBM)
     params = pltpu.CompilerParams(vmem_limit_bytes=32 * 1024 * 1024)
-    costly = pl.CostEstimate(flops=4 * 10**10, bytes_accessed=0, transcendentals=0)
+
+    def flops(count):
+        return pl.CostEstimate(flops=count, bytes_accessed=0, transcendentals=0)
+
+    costly = flops(4 * 10**10)
     dma = pltpu.SemaphoreType.DMA
 
     def swap(value, mask):
@@ -443,14 +476,23 @@
     gates_shape = shape((2 * heads, slots), f32)
     arrays = [pltpu.with_memory_space_constraint(a, pltpu.HBM) for a in (queries, keys, values, cotangent, igate, fgate)]
     cross_shape = shape((rows, width), bf16)
-    a2_sent, d, to_core, gates = pl.pallas_call(
+    a2_sent, gates = pl.pallas_call(
         pack_kernel,
-        out_shape=(cross_shape, shape((rows, 2 * width), bf16), shape((rows, 4 * width), bf16), gates_shape),
+        out_shape=(shape((rows, width + slots), bf16), gates_shape),
         in_specs=[hbm] * 6,
-        out_specs=(vmem,) * 4,
-        scratch_shapes=[pltpu.VMEM(igate.shape, f32), pltpu.VMEM(igate.shape, f32), dma((16,))],
+        out_specs=(vmem,) * 2,
+        scratch_shapes=[pltpu.VMEM(igate.shape, f32), pltpu.VMEM(igate.shape, f32), dma((4,))],
         compiler_params=params,
     )(*arrays)
+    a2 = swap(a2_sent, 2)
+    d, to_core = pl.pallas_call(
+        more_kernel,
+        out_shape=(shape((rows, 2 * width), bf16), shape((rows, 4 * width), bf16)),
+        in_specs=[hbm] * 4,
+        out_specs=(vmem,) * 2,
+        scratch_shapes=[dma((12,))],
+        compiler_params=params,
+    )(*arrays[:4])
     b2_sent, rest = pl.pallas_call(
         rest_kernel,
         out_shape=(cross_shape, shape((2, rows, width), bf16)),
@@ -460,9 +502,15 @@
         compiler_params=params,
     )(*arrays[:4])
     from_core = swap(to_core, 1)
-    gates_got = swap(gates, 2)
-    a2, d = swap(a2_sent, 2), swap(d, 3)
-    a2, gates_got = lax.optimization_barrier((a2, gates_got))
+    d = swap(d, 3)
+    gates_got = pl.pallas_call(
+        join_kernel,
+        out_shape=gates_shape,
+        in_specs=[vmem],
+        out_specs=vmem,
+        cost_estimate=costly,
+        compiler_params=params,
+    )(a2)
     both = shape((2, 2 * rows, width), bf16)
     qg, kv, stats = pl.pallas_call(
         functools.partial(local_kernel, qk, vw),
@@ -484,35 +532,52 @@
             in_specs=[smem] + [vmem] * (7 + len(written)),
             out_specs=(vmem,) * 3 + ((hbm,) * 4 if written else ()),
             scratch_shapes=[pltpu.VMEM((4 * rows, width), bf16)] + ([dma((4,))] if written else []),
-            cost_estimate=costly,
+            cost_estimate=flops(2 * 10**9) if written else costly,
             compiler_params=params,
         )(lengths, qg, kv, gates, gates_got, stats, *received, *written)
 
     result_a, theirs_a, gates_a = cross(0, (a2, d), ())
+    gates_a = pl.pallas_call(
+        hold_kernel,
+        out_shape=gates_shape,
+        in_specs=[vmem],
+        out_specs=vmem,
+        cost_estimate=flops(0),
+        compiler_params=params,
+    )(gates_a)
     gates_back = swap(gates_a, 2)
     got_a = swap(theirs_a, 1)
     result_b, theirs_b, gates_b, *outputs = cross(1, (b2, d), (result_a,))
+    theirs_b, got_a = lax.optimization_barrier((theirs_b, got_a))
     got_b = swap(theirs_b, 1)
+    *outputs, gates_b = pl.pallas_call(
+        merge_kernel,
+        out_shape=out_shape + (gates_shape,),
+        in_specs=[vmem] * 3 + [hbm] * 4,
+        out_specs=(hbm,) * 4 + (vmem,),
+        scratch_shapes=[dma((8,))],
+        input_output_aliases={3: 0, 4: 1, 5: 2, 6: 3},
+        cost_estimate=flops(0),
+        compiler_params=params,
+    )(result_b, got_a, gates_b, *outputs)
     gate_shape = shape(igate.shape, f32)
-    *outputs, grad_in, grad_forget = pl.pallas_call(
-        merge_kernel,
+    gate_grads = pl.pallas_call(
+        gates_kernel,
+        out_shape=(gate_shape, gate_shape),
+        in_specs=[vmem] * 3,
+        out_specs=(vmem,) * 2,
+        cost_estimate=costly,
+        compiler_params=params,
+    )(gates_a, gates_back, gates_b)
+    gq, gk, gv, hidden, grad_in, grad_forget = pl.pallas_call(
+        last_kernel,
         out_shape=out_shape + (gate_shape, gate_shape),
-        in_specs=[vmem] * 5 + [hbm] * 4,
+        in_specs=[vmem] * 3 + [hbm] * 4,
         out_specs=(hbm,) * 6,
-        scratch_shapes=[pltpu.VMEM((2, *igate.shape), f32), dma((10,))],
-        cost_estimate=costly,
-        input_output_aliases={5: 0, 6: 1, 7: 2, 8: 3},
-        compiler_params=params,
-    )(result_b, got_a, gates_a, gates_back, gates_b, *outputs)
-    gq, gk, gv, hidden = pl.pallas_call(
-        last_kernel,
-        out_shape=out_shape,
-        in_specs=[vmem] + [hbm] * 4,
-        out_specs=(hbm,) * 4,
-        scratch_shapes=[dma((4,))],
-        input_output_aliases={1: 0, 2: 1, 3: 2, 4: 3},
-        compiler_params=params,
-    )(got_b, *outputs)
+        scratch_shapes=[dma((6,))],
+        input_output_aliases={3: 0, 4: 1, 5: 2, 6: 3},
+        compiler_params=params,
+    )(got_b, *gate_grads, *outputs)
     return hidden, gq, gk, gv, grad_in, grad_forget
 
 

time: 19 us -> 18.5 us (0.974)
  starting transfers between devices: 9.25 us -> 7.06 us
  Pallas kernels: 5.78 us -> 6.62 us
  waiting for transfers between devices: 2.42 us -> 3.11 us
    ppermute x9 -> x8, starting transfers between devices: 9.25 us -> 7.06 us  [swap(): return lax.ppermute(value, 'head', [(s, s ^ mask) for s in range(4)])]
    pallas_call x3 -> x7, Pallas kernels: 2.87 us -> 3.71 us  [the longest x1 1.2 us: split_shards(): pl.pallas_call(more_kernel, out_shape=(shape((rows, 2 * width), bf16), sh...]
    ppermute x9 -> x8, waiting for transfers between devices: 2.42 us -> 3.11 us  [swap(): return lax.ppermute(value, 'head', [(s, s ^ mask) for s in range(4)])]
  transfers between devices with their start and end apart: 9 -> 8, of which waited for: 4 -> 2; matrix products, arithmetic and copies ran while one was open for 0% -> 0% of each run, Pallas kernels for 20% -> 27%
where the time goes in v6:
time: 18.5 us; the launch traced here: 18.2 us
  starting transfers between devices  7.06 us (38%)
  Pallas kernels  6.62 us (36%)
  waiting for transfers between devices  3.11 us (17%)
  between operations  1.38 us (7%)
    ppermute x8, starting transfers between devices, swap(): return lax.ppermute(value, 'head', [(s, s ^ mask) for s in range(4)])  7.06 us
    ppermute x8, waiting for transfers between devices, swap(): return lax.ppermute(value, 'head', [(s, s ^ mask) for s in range(4)])  3.11 us
    pallas_call x2, Pallas kernels, cross(): pl.pallas_call(functools.partial(cross_kernel, chunk, qk, vw), out_shape=...  1.55 us
    pallas_call x1, Pallas kernels, split_shards(): pl.pallas_call(more_kernel, out_shape=(shape((rows, 2 * width), bf16), sh...  1.2 us
    pallas_call x1, Pallas kernels, split_shards(): pl.pallas_call(rest_kernel, out_shape=(cross_shape, shape((2, rows, width...  1.01 us
    pallas_call x1, Pallas kernels, split_shards(): pl.pallas_call(pack_kernel, out_shape=(shape((rows, width + slots), bf16)...  0.94 us
    pallas_call x1, Pallas kernels, split_shards(): pl.pallas_call(merge_kernel, out_shape=out_shape + (gates_shape,), in_spe...  0.81 us
    pallas_call x1, Pallas kernels, split_shards(): pl.pallas_call(last_kernel, out_shape=out_shape + (gate_shape, gate_shape...  0.74 us
  transfers between devices with their start and end apart: 8, of which 2 were waited for; matrix products, arithmetic and copies ran while one was open for 0% of the time, Pallas kernels for 27%

profile of v6, /device:TPU:0, one launch (start us, length us, event | category | flops | bytes accessed | tf_op | source)
XLA Modules:
  0.0 18.2 jit_solution(5467926689292757267)
XLA Ops:
  0.6 0.9 %shard_map.118 = (bf16[32,1664]{1,0:T(8,128)(2,1)S(1)}, f32[4,128]{1,0:T(4,128)S(1)}) custom-call(bf16[32,2048]{1,0:T(8,128)(2,1)} %q_ref.5, bf16[32,2048]{1,0:T(8,128)(2,1)} %k_ref.5, bf16[32,4096]{1,0:T(8,128)(2,1)} %v_ref.5, bf16[32,4096]{1,0:T(8,128)(2,1)} %g_ref.5, f32[2,128]{1,0:T(2,128)} %ig_ref.1, f32[2,128]{1,0:T(2,128)} %fg_ref.1), custom_call_target="tpu_custom_call" | custom-call | tf_op jit(solution)/shard_map/pallas_call | solution.py:479
  1.6 3.0 %collective-permute-start.1 = (bf16[32,1664]{1,0:T(8,128)(2,1)S(1)}, bf16[32,1664]{1,0:T(8,128)(2,1)S(1)}, u32[]{:S(2)}, u32[]{:S(2)}) collective-permute-start(bf16[32,1664]{1,0:T(8,128)(2,1)S(1)} %get-tuple-element.40.a2_ref), channel_id=1, source_target_pairs={{0,2},{1,3},{2,0},{3,1},{4,6},{5,7},{6,4},{7,5},{8,10},{9,11},{10,... | collective-permute-start | bytes 319496 | tf_op jit(solution)/shard_map/ppermute | solution.py:473
  4.6 1.2 %shard_map.120 = (bf16[32,3072]{1,0:T(8,128)(2,1)S(1)}, bf16[32,6144]{1,0:T(8,128)(2,1)S(1)}) custom-call(bf16[32,2048]{1,0:T(8,128)(2,1)} %q_ref.5, bf16[32,2048]{1,0:T(8,128)(2,1)} %k_ref.5, bf16[32,4096]{1,0:T(8,128)(2,1)} %v_ref.5, bf16[32,4096]{1,0:T(8,128)(2,1)} %g_ref.5), custom_call_target="tpu_custom_call" | custom-call | tf_op jit(solution)/shard_map/pallas_call | solution.py:488
  5.8 0.1 collective-permute-start.4
  5.9 0.2 collective-permute-start
  6.0 1.0 %shard_map.119 = (bf16[32,1536]{1,0:T(8,128)(2,1)S(1)}, bf16[2,32,1536]{2,1,0:T(8,128)(2,1)S(1)}) custom-call(bf16[32,2048]{1,0:T(8,128)(2,1)} %q_ref.5, bf16[32,2048]{1,0:T(8,128)(2,1)} %k_ref.5, bf16[32,4096]{1,0:T(8,128)(2,1)} %v_ref.5, bf16[32,4096]{1,0:T(8,128)(2,1)} %g_ref.5), custom_call_target="tpu_custom_call" | custom-call | tf_op jit(solution)/shard_map/pallas_call | solution.py:496
  7.7 0.0 collective-permute-done.1.a2_got.same_ref
  7.7 0.0 collective-permute-done.m1_ref
  7.7 0.4 %shard_map.122 = (bf16[2,64,1536]{2,1,0:T(8,128)(2,1)S(1)}, bf16[2,64,1536]{2,1,0:T(8,128)(2,1)S(1)}, f32[8,128]{1,0:T(8,128)S(1)}) custom-call(s32[1]{0:T(128)S(6)} %copy.29.length_ref, bf16[32,1664]{1,0:T(8,128)(2,1)S(1)} %get-tuple-element.40.a2_ref, bf16[32,1536]{1,0:T(8,128)(2,1)S(1)} %get-tuple-element.41.b2_ref, ...), custom_call_target="tpu_custom_call" | custom-call | flops 40000000000 | tf_op jit(solution)/shard_map/pallas_call | solution.py:515
  8.1 2.2 %collective-permute-start.2 = (f32[8,128]{1,0:T(8,128)S(1)}, f32[8,128]{1,0:T(8,128)S(1)}, u32[]{:S(2)}, u32[]{:S(2)}) collective-permute-start(f32[8,128]{1,0:T(8,128)S(1)} %get-tuple-element.47), channel_id=1, source_target_pairs={{0,2},{1,3},{2,0},{3,1},{4,6},{5,7},{6,4},{7,5},{8,10},{9,11},{10,... | collective-permute-start | bytes 12296 | tf_op jit(solution)/shard_map/ppermute | solution.py:473
  10.3 0.1 collective-permute-start.3
  10.4 2.5 %collective-permute-done.4.other_ref = bf16[32,3072]{1,0:T(8,128)(2,1)S(1)} collective-permute-done((bf16[32,3072]{1,0:T(8,128)(2,1)S(1)}, bf16[32,3072]{1,0:T(8,128)(2,1)S(1)}, u32[]{:S(2)}, u32[]{:S(2)}) %collective-permute-start.4) | collective-permute-done | bytes 196640 | tf_op jit(solution)/shard_map/ppermute | solution.py:473
  12.8 0.0 collective-permute-done.2.stats_ref
  12.8 0.8 %shard_map.123 = (bf16[64,3072]{1,0:T(8,128)(2,1)S(1)}, bf16[32,3072]{1,0:T(8,128)(2,1)S(1)}, f32[4,128]{1,0:T(4,128)S(1)}) custom-call(s32[1]{0:T(128)S(6)} %copy.29.length_ref, bf16[2,64,1536]{2,1,0:T(8,128)(2,1)S(1)} %get-tuple-element.45.qg_ref, bf16[2,64,1536]{2,1,0:T(8,128)(2,1)S(1)} %get-tuple-element.46.kv_ref, ...), custom_call_target="tpu_custom_call" | custom-call | flops 40000000000 | tf_op jit(solution)/shard_map/pallas_call | solution.py:528
  13.6 0.2 %collective-permute-start.5 = (bf16[32,3072]{1,0:T(8,128)(2,1)S(1)}, bf16[32,3072]{1,0:T(8,128)(2,1)S(1)}, u32[]{:S(2)}, u32[]{:S(2)}) collective-permute-start(bf16[32,3072]{1,0:T(8,128)(2,1)S(1)} %get-tuple-element.51), channel_id=1, source_target_pairs={{0,1},{1,0},{2,3},{3,2},{4,5},{5,4},{6,7},{7,6},{8,9},{9,8},{10,11... | collective-permute-start | bytes 589832 | tf_op jit(solution)/shard_map/ppermute | solution.py:473
  13.8 1.2 %collective-permute-start.7 = (f32[4,128]{1,0:T(4,128)S(1)}, f32[4,128]{1,0:T(4,128)S(1)}, u32[]{:S(2)}, u32[]{:S(2)}) collective-permute-start(f32[4,128]{1,0:T(4,128)S(1)} %shard_map.125.gates_a), channel_id=1, source_target_pairs={{0,2},{1,3},{2,0},{3,1},{4,6},{5,7},{6,4},{7,5},{8,10},{9,11},{10,... | collective-permute-start | bytes 6152 | tf_op jit(solution)/shard_map/ppermute | solution.py:473
  15.0 0.0 collective-permute-done.3.same_ref
  15.0 0.8 %shard_map.124 = (bf16[64,3072]{1,0:T(8,128)(2,1)S(1)}, bf16[32,3072]{1,0:T(8,128)(2,1)S(1)}, f32[4,128]{1,0:T(4,128)S(1)}, bf16[32,2048]{1,0:T(8,128)(2,1)}, bf...) custom-call(s32[1]{0:T(128)S(6)} %copy.29.length_ref, ...), custom_call_target="tpu_custom_call" | custom-call | flops 2000000000 | tf_op jit(solution)/shard_map/pallas_call | solution.py:528
  15.8 0.0 collective-permute-done.5.got_a
  15.8 0.2 %collective-permute-start.6 = (bf16[32,3072]{1,0:T(8,128)(2,1)S(1)}, bf16[32,3072]{1,0:T(8,128)(2,1)S(1)}, u32[]{:S(2)}, u32[]{:S(2)}) collective-permute-start(bf16[32,3072]{1,0:T(8,128)(2,1)S(1)} %get-tuple-element.52), channel_id=1, source_target_pairs={{0,1},{1,0},{2,3},{3,2},{4,5},{5,4},{6,7},{7,6},{8,9},{9,8},{10,11... | collective-permute-start | bytes 589832 | tf_op jit(solution)/shard_map/ppermute | solution.py:473
  16.0 0.8 %shard_map.126 = (bf16[32,2048]{1,0:T(8,128)(2,1)}, bf16[32,2048]{1,0:T(8,128)(2,1)}, bf16[32,4096]{1,0:T(8,128)(2,1)}, bf16[32,4096]{1,0:T(8,128)(2,1)}, f32[4,128]{1,0:T(4,128)S(1)}) custom-call(bf16[64,3072]{1,0:T(8,128)(2,1)S(1)} %get-tuple-element.54.result_b, ...), custom_call_target="tpu_custom_call", output_to_operand_aliasing={{0}: (3, {}), {1}: (4, {}), {2}: (5, {}), {3}: (6, {})} | custom-call | tf_op jit(solution)/shard_map/pallas_call | solution.py:553
  16.8 0.6 %collective-permute-done.7.gates_got = f32[4,128]{1,0:T(4,128)S(1)} collective-permute-done((f32[4,128]{1,0:T(4,128)S(1)}, f32[4,128]{1,0:T(4,128)S(1)}, u32[]{:S(2)}, u32[]{:S(2)}) %collective-permute-start.7) | collective-permute-done | bytes 2080 | tf_op jit(solution)/shard_map/ppermute | solution.py:473
  17.4 0.0 collective-permute-done.6.got_b
  17.4 0.7 %shard_map.128 = (bf16[32,2048]{1,0:T(8,128)(2,1)}, bf16[32,2048]{1,0:T(8,128)(2,1)}, bf16[32,4096]{1,0:T(8,128)(2,1)}, bf16[32,4096]{1,0:T(8,128)(2,1)}, f32[2,128]{1,0:T(2,128)}, /*index=5*/f32[2,128]{1,0:T(2,128)}) custom-call(bf16[32,3072]{1,0:T(8,128)(2,1)S(1)} %collective-permute-done.6, ...), custom_call_target="tpu_custom_call", output_to_operand_aliasing={{0}: (3, {}), {1}: (4, {}), {2}: (5, {}), {3}: (6, {})} | custom-call | tf_op jit(solution)/shard_map/pallas_call | solution.py:572
  (3 shorter events, 0.0 us)
Async XLA Ops:
  1.6 6.1 %collective-permute-start.1 = (bf16[32,1664]{1,0:T(8,128)(2,1)S(1)}, bf16[32,1664]{1,0:T(8,128)(2,1)S(1)}, u32[]{:S(2)}, u32[]{:S(2)}) collective-permute-start(bf16[32,1664]{1,0:T(8,128)(2,1)S(1)} %get-tuple-element.40.a2_ref), channel_id=1, source_target_pairs={{0,2},{1,3},{2,0},{3,1},{4,6},{5,7},{6,4},{7,5},{8,10},{9,11},{10,... | collective-permute-start | bytes 319496 | tf_op jit(solution)/shard_map/ppermute | solution.py:473
  5.8 7.0 %collective-permute-start.4 = (bf16[32,3072]{1,0:T(8,128)(2,1)S(1)}, bf16[32,3072]{1,0:T(8,128)(2,1)S(1)}, u32[]{:S(2)}, u32[]{:S(2)}) collective-permute-start(bf16[32,3072]{1,0:T(8,128)(2,1)S(1)} %get-tuple-element.48), channel_id=1, source_target_pairs={{0,3},{1,2},{2,1},{3,0},{4,7},{5,6},{6,5},{7,4},{8,11},{9,10},{10,... | collective-permute-start | bytes 589832 | tf_op jit(solution)/shard_map/ppermute | solution.py:473
  5.9 1.8 %collective-permute-start = (bf16[32,6144]{1,0:T(8,128)(2,1)S(1)}, bf16[32,6144]{1,0:T(8,128)(2,1)S(1)}, u32[]{:S(2)}, u32[]{:S(2)}) collective-permute-start(bf16[32,6144]{1,0:T(8,128)(2,1)S(1)} %get-tuple-element.43), channel_id=1, source_target_pairs={{0,1},{1,0},{2,3},{3,2},{4,5},{5,4},{6,7},{7,6},{8,9},{9,8},{10,11... | collective-permute-start | bytes 1179656 | tf_op jit(solution)/shard_map/ppermute | solution.py:473
  8.1 4.8 %collective-permute-start.2 = (f32[8,128]{1,0:T(8,128)S(1)}, f32[8,128]{1,0:T(8,128)S(1)}, u32[]{:S(2)}, u32[]{:S(2)}) collective-permute-start(f32[8,128]{1,0:T(8,128)S(1)} %get-tuple-element.47), channel_id=1, source_target_pairs={{0,2},{1,3},{2,0},{3,1},{4,6},{5,7},{6,4},{7,5},{8,10},{9,11},{10,... | collective-permute-start | bytes 12296 | tf_op jit(solution)/shard_map/ppermute | solution.py:473
  10.3 4.7 %collective-permute-start.3 = (bf16[32,1536]{1,0:T(8,128)(2,1)S(1)}, bf16[32,1536]{1,0:T(8,128)(2,1)S(1)}, u32[]{:S(2)}, u32[]{:S(2)}) collective-permute-start(bf16[32,1536]{1,0:T(8,128)(2,1)S(1)} %get-tuple-element.41.b2_ref), channel_id=1, source_target_pairs={{0,2},{1,3},{2,0},{3,1},{4,6},{5,7},{6,4},{7,5},{8,10},{9,11},{10,... | collective-permute-start | bytes 294920 | tf_op jit(solution)/shard_map/ppermute | solution.py:473
  13.6 2.2 %collective-permute-start.5 = (bf16[32,3072]{1,0:T(8,128)(2,1)S(1)}, bf16[32,3072]{1,0:T(8,128)(2,1)S(1)}, u32[]{:S(2)}, u32[]{:S(2)}) collective-permute-start(bf16[32,3072]{1,0:T(8,128)(2,1)S(1)} %get-tuple-element.51), channel_id=1, source_target_pairs={{0,1},{1,0},{2,3},{3,2},{4,5},{5,4},{6,7},{7,6},{8,9},{9,8},{10,11... | collective-permute-start | bytes 589832 | tf_op jit(solution)/shard_map/ppermute | solution.py:473
  13.8 3.6 %collective-permute-start.7 = (f32[4,128]{1,0:T(4,128)S(1)}, f32[4,128]{1,0:T(4,128)S(1)}, u32[]{:S(2)}, u32[]{:S(2)}) collective-permute-start(f32[4,128]{1,0:T(4,128)S(1)} %shard_map.125.gates_a), channel_id=1, source_target_pairs={{0,2},{1,3},{2,0},{3,1},{4,6},{5,7},{6,4},{7,5},{8,10},{9,11},{10,... | collective-permute-start | bytes 6152 | tf_op jit(solution)/shard_map/ppermute | solution.py:473
  15.8 1.6 %collective-permute-start.6 = (bf16[32,3072]{1,0:T(8,128)(2,1)S(1)}, bf16[32,3072]{1,0:T(8,128)(2,1)S(1)}, u32[]{:S(2)}, u32[]{:S(2)}) collective-permute-start(bf16[32,3072]{1,0:T(8,128)(2,1)S(1)} %get-tuple-element.52), channel_id=1, source_target_pairs={{0,1},{1,0},{2,3},{3,2},{4,5},{5,4},{6,7},{7,6},{8,9},{9,8},{10,11... | collective-permute-start | bytes 589832 | tf_op jit(solution)/shard_map/ppermute | solution.py:473

commit v7 on v6

--- a/solution.py
+++ b/solution.py
@@ -304,33 +304,36 @@
 
 
 def cross_kernel(
-    chunk, qk, vw, length_ref, qg_ref, kv_ref, own_ref, got_ref, stats_ref, same_ref, other_ref, *refs
+    chunk, sides, work, qk, vw, length_ref, qg_ref, kv_ref, own_ref, got_ref, same_ref, other_ref, *refs
 ):
     chip, core = place()
-    writes = []
-    if chunk == 0:
-        result_ref, theirs_ref, gates_ref, wide_ref = refs
+    rows_wanted, gates_wanted = work != "gates", work != "rows"
+    if work == "gates":
+        gates_ref, wide_ref = refs
+    elif work == "rows":
+        _, result_ref, theirs_ref, wide_ref = refs
+    elif sides == (0,):
+        stats_ref, *later, result_ref, theirs_ref, gates_ref, wide_ref = refs
     else:
-        result_a, result_ref, theirs_ref, gates_ref, *outputs, wide_ref, sems = refs
-        rows = theirs_ref.shape[0]
-        mine_a = result_a.at[pl.ds(pl.multiple_of(core * rows, rows), rows), :]
-        writes = run_copies(placed(mine_a, outputs, 0, core), sems)
-    rows = theirs_ref.shape[0]
+        stats_ref, near_ref, share_ref, result_ref, theirs_ref, gates_ref, wide_ref = refs
+    rows = other_ref.shape[0]
     size = 2 * rows
     heads = own_ref.shape[0] // 2
     wq, wv = heads * qk, heads * vw
 
     def gather(side, local):
         base = 0 if side else size
-        wide_ref[side * size : (side + 1) * size, :] = local[chunk]
+        if side == 1 or chunk == 0:
+            wide_ref[side * size : (side + 1) * size, :] = local[chunk]
         for ref, by in ((same_ref, core), (other_ref, 1 - core)):
             start = chunk * (wq + wv) if ref is other_ref else 0
             wide_ref[pl.ds(pl.multiple_of(base + by * rows, rows), rows), :] = ref[:, start : start + wq + wv]
 
     length = length_ref[0]
-    gates_ref[...] = jnp.zeros_like(gates_ref)
 
     def part(side):
+        if gates_wanted:
+            gates_ref[...] = jnp.zeros_like(gates_ref)
         gather(side, kv_ref if side else qg_ref)
         thin = (qg_ref if side else kv_ref).at[chunk]
         gates = own_ref if side == chunk else got_ref
@@ -346,13 +349,16 @@
             for head in range(heads)
         ]
         each = range(heads)
+        far = side == 0 and chunk == 1
         loaded = []
         for head in each:
             first = slice(head * qk, (head + 1) * qk)
             second = slice(wq + head * vw, wq + (head + 1) * vw)
-            of_wide, of_thin = (wide_ref[:, first], wide_ref[:, second]), (thin[:, first], thin[:, second])
+            seen = slice(size, 2 * size) if far else slice(None)
+            of_wide, of_thin = (wide_ref[seen, first], wide_ref[seen, second]), (thin[:, first], thin[:, second])
             loaded.append(of_wide + of_thin if side == 0 else of_thin + of_wide)
-        weights = [weight[:, :size] if side == 0 else weight[size:, :] for weight in weights]
+        weights = [weight[:, :size] if side == 0 else weight for weight in weights]
+        weights = [weight[size:] if side == 1 or far else weight for weight in weights]
         scores = [dot(q, k, NT) for q, g, k, v in loaded]
         pulled = [dot(g, v, NT) for q, g, k, v in loaded]
         scores = [scores[head] * weights[head] for head in each]
@@ -360,28 +366,41 @@
         alongs = [jnp.sum(scores[head] * pulled[head], axis=1, keepdims=True) for head in each]
         if side == 0:
             at = chunk * heads
-            norms = [norms[head] + as_column(stats_ref[at + head : at + head + 1, :]) for head in each]
+            sums = [as_column(stats_ref[at + head : at + head + 1, :]) for head in each]
+            norms = [norms[head] + (sums[head][size:] if far else sums[head]) for head in each]
             at += 2 * heads
-            alongs = [alongs[head] + as_column(stats_ref[at + head : at + head + 1, :]) for head in each]
+            sums = [as_column(stats_ref[at + head : at + head + 1, :]) for head in each]
+            alongs = [alongs[head] + (sums[head][size:] if far else sums[head]) for head in each]
         terms = [backward_terms(norms[head], alongs[head]) for head in each]
         grad_scores = [pulled[head] * terms[head][0] + terms[head][1] for head in each]
-        scaled = [scores[head] * terms[head][0] for head in each]
-        grad_raw = [grad_scores[head] * weights[head] for head in each]
-        turned = [(scaled[head].T, grad_raw[head].T) for head in each]
-        if side == 0:
-            scaled, grad_raw = [value[:size] for value in scaled], [value[:size] for value in grad_raw]
-        else:
-            turned = [(one[size:], other[size:]) for one, other in turned]
-        sections = ((0, qk), (wq, qk), (2 * wq, vw), (2 * wq + wv, vw))
-        for section, (start, step) in enumerate(sections):
-            for head in each:
-                q, g, k, v = loaded[head]
-                left, right = (
-                    (grad_raw[head], k), (turned[head][1], q), (turned[head][0], g), (scaled[head], v)
-                )[section]
-                value = wide_dot(left, right, NN).astype(jnp.bfloat16)
-                result_ref[:, start + head * step : start + (head + 1) * step] = value
-        for head in each:
+        if rows_wanted:
+            scaled = [scores[head] * terms[head][0] for head in each]
+            grad_raw = [grad_scores[head] * weights[head] for head in each]
+            turned = [(scaled[head].T, grad_raw[head].T) for head in each]
+            if far:
+                pass
+            elif side == 0:
+                scaled, grad_raw = [value[:size] for value in scaled], [value[:size] for value in grad_raw]
+            else:
+                turned = [(one[size:], other[size:]) for one, other in turned]
+            sections = ((0, qk), (wq, qk), (2 * wq, vw), (2 * wq + wv, vw))
+            for section, (start, step) in enumerate(sections):
+                for head in each:
+                    columns = slice(start + head * step, start + (head + 1) * step)
+                    if far and section in (0, 3):
+                        at = (section // 3) * wq + head * step
+                        result_ref[:, columns] = near_ref[:, at : at + step]
+                        continue
+                    q, g, k, v = loaded[head]
+                    left, right = (
+                        (grad_raw[head], k), (turned[head][1], q), (turned[head][0], g), (scaled[head], v)
+                    )[section]
+                    value = wide_dot(left, right, NN)
+                    if far:
+                        at = (section - 1) * wq + head * step
+                        value = value + share_ref[:, at : at + step]
+                    result_ref[:, columns] = value.astype(jnp.bfloat16)
+        for head in each if gates_wanted else ():
             by_column = jnp.sum(grad_scores[head] * scores[head], axis=0, keepdims=True)
             by_row = terms[head][2]
             forget = gates[heads + head : heads + head + 1, :]
@@ -407,30 +426,66 @@
                 grad_log = jnp.sum(jnp.where(rows_at >= cols_at, moved, 0.0), axis=0, keepdims=True)
                 gates_ref[head : head + 1, :] = by_column
                 gates_ref[heads + head : heads + head + 1, :] = jnp.where(seen, grad_log * slope, 0.0)
-        theirs_ref[...] = result_ref[pl.ds(pl.multiple_of((1 - core) * rows, rows), rows), :]
-
-    @pl.when(chip == 0)
-    def _():
-        part(0)
-
-    @pl.when(chip != 0)
-    def _():
-        part(1)
-
-    for copy in writes:
-        copy.wait()
+        if rows_wanted:
+            theirs_ref[...] = result_ref[pl.ds(pl.multiple_of((1 - core) * rows, rows), rows), :]
+
+    for side in sides:
+        pl.when(chip == side)(functools.partial(part, side))
+
+    if sides == (0,):
+
+        @pl.when(chip != 0)
+        def _():
+            for source, target in zip(later, (result_ref, theirs_ref, gates_ref)):
+                target[...] = source[...]
 
 
 def hold_kernel(in_ref, out_ref):
     out_ref[...] = in_ref[...]
 
 
-def merge_kernel(result_b, got_a, gates_in, *refs):
-    *outputs, gates_ref, sems = refs[4:]
+def near_kernel(qk, vw, length_ref, qg_ref, kv_ref, got_ref, got_out, near_ref, share_ref):
+    got_out[...] = got_ref[...]
+    heads = got_ref.shape[0] // 2
+    size = qg_ref.shape[1]
+    wq = heads * qk
+
+    @pl.when(place()[0] == 0)
+    def _():
+        each = range(heads)
+        length = length_ref[0]
+        loaded, weights = [], []
+        for head in each:
+            first = slice(head * qk, (head + 1) * qk)
+            second = slice(wq + head * vw, wq + (head + 1) * vw)
+            loaded.append((qg_ref[1, :, first], qg_ref[1, :, second], kv_ref[1, :, first], kv_ref[1, :, second]))
+            gates = (got_ref[head : head + 1, :], got_ref[heads + head : heads + head + 1, :])
+            weights.append(decay(*gates, length, qk**-0.5)[:size, :size])
+        scores = [dot(q, k, NT) for q, g, k, v in loaded]
+        pulled = [dot(g, v, NT) for q, g, k, v in loaded]
+        scores = [scores[head] * weights[head] for head in each]
+        norms = [jnp.sum(scores[head], axis=1, keepdims=True) for head in each]
+        alongs = [jnp.sum(scores[head] * pulled[head], axis=1, keepdims=True) for head in each]
+        terms = [backward_terms(norms[head], alongs[head]) for head in each]
+        scaled = [scores[head] * terms[head][0] for head in each]
+        grad_raw = [(pulled[head] * terms[head][0] + terms[head][1]) * weights[head] for head in each]
+        for head in each:
+            q, g, k, v = loaded[head]
+            first = slice(head * qk, (head + 1) * qk)
+            second = slice(wq + head * vw, wq + (head + 1) * vw)
+            near_ref[:, first] = wide_dot(grad_raw[head], k, NN).astype(jnp.bfloat16)
+            near_ref[:, second] = wide_dot(scaled[head], v, NN).astype(jnp.bfloat16)
+            share_ref[:, first] = wide_dot(grad_raw[head].T, q, NN)
+            share_ref[:, second] = wide_dot(scaled[head].T, g, NN)
+
+
+def merge_kernel(result_a, result_b, got_a, gates_in, *refs):
+    *outputs, gates_ref, sems = refs
     core = place()[1]
     rows = got_a.shape[0]
-    mine = result_b.at[pl.ds(pl.multiple_of(core * rows, rows), rows), :]
-    copies = run_copies(placed(mine, outputs, 1, core) + placed(got_a, outputs, 0, 1 - core), sems)
+    mine = pl.ds(pl.multiple_of(core * rows, rows), rows)
+    pairs = placed(result_a.at[mine, :], outputs, 0, core) + placed(result_b.at[mine, :], outputs, 1, core)
+    copies = run_copies(pairs + placed(got_a, outputs, 0, 1 - core), sems)
     gates_ref[...] = gates_in[...]
     for copy in copies:
         copy.wait()
@@ -524,42 +579,52 @@
     b2 = swap(b2_sent, 2)
     out_shape = tuple(shape(a.shape, bf16) for a in (queries, keys, values, values))
 
-    def cross(chunk, received, written):
+    results = (shape((2 * rows, 2 * width), bf16), shape((rows, 2 * width), bf16), gates_shape)
+
+    def cross(chunk, sides, work, *received, cost):
+        kept = {"gates": results[2:], "rows": results[:2], "all": results}[work]
         return pl.pallas_call(
-            functools.partial(cross_kernel, chunk, qk, vw),
-            out_shape=(shape((2 * rows, 2 * width), bf16), shape((rows, 2 * width), bf16), gates_shape)
-            + (out_shape if written else ()),
-            in_specs=[smem] + [vmem] * (7 + len(written)),
-            out_specs=(vmem,) * 3 + ((hbm,) * 4 if written else ()),
-            scratch_shapes=[pltpu.VMEM((4 * rows, width), bf16)] + ([dma((4,))] if written else []),
-            cost_estimate=flops(2 * 10**9) if written else costly,
+            functools.partial(cross_kernel, chunk, sides, work, qk, vw),
+            out_shape=kept,
+            in_specs=[smem] + [vmem] * (4 + len(received)),
+            out_specs=(vmem,) * len(kept),
+            scratch_shapes=[pltpu.VMEM((4 * rows, width), bf16)],
+            cost_estimate=cost,
             compiler_params=params,
-        )(lengths, qg, kv, gates, gates_got, stats, *received, *written)
-
-    result_a, theirs_a, gates_a = cross(0, (a2, d), ())
-    gates_a = pl.pallas_call(
+        )(lengths, qg, kv, gates, gates_got, *received)
+
+    gates_got, near, share = pl.pallas_call(
+        functools.partial(near_kernel, qk, vw),
+        out_shape=(gates_shape, shape((2 * rows, width), bf16), shape((2 * rows, width), f32)),
+        in_specs=[smem] + [vmem] * 3,
+        out_specs=(vmem,) * 3,
+        cost_estimate=flops(0),
+        compiler_params=params,
+    )(lengths, qg, kv, gates_got)
+    (gates_later,) = cross(0, (1,), "gates", a2, d, cost=flops(0))
+    to_owner = pl.pallas_call(
         hold_kernel,
         out_shape=gates_shape,
         in_specs=[vmem],
         out_specs=vmem,
         cost_estimate=flops(0),
         compiler_params=params,
-    )(gates_a)
-    gates_back = swap(gates_a, 2)
+    )(gates_later)
+    gates_back = swap(to_owner, 2)
+    later_a = cross(0, (1,), "rows", a2, d, to_owner, cost=flops(0))
+    result_a, theirs_a, gates_a = cross(0, (0,), "all", a2, d, stats, *later_a, gates_later, cost=flops(40000000000))
     got_a = swap(theirs_a, 1)
-    result_b, theirs_b, gates_b, *outputs = cross(1, (b2, d), (result_a,))
-    theirs_b, got_a = lax.optimization_barrier((theirs_b, got_a))
+    result_b, theirs_b, gates_b = cross(1, (0, 1), "all", b2, d, stats, near, share, cost=flops(4000000000))
     got_b = swap(theirs_b, 1)
     *outputs, gates_b = pl.pallas_call(
         merge_kernel,
         out_shape=out_shape + (gates_shape,),
-        in_specs=[vmem] * 3 + [hbm] * 4,
+        in_specs=[vmem] * 4,
         out_specs=(hbm,) * 4 + (vmem,),
-        scratch_shapes=[dma((8,))],
-        input_output_aliases={3: 0, 4: 1, 5: 2, 6: 3},
+        scratch_shapes=[dma((12,))],
         cost_estimate=flops(0),
         compiler_params=params,
-    )(result_b, got_a, gates_b, *outputs)
+    )(result_a, result_b, got_a, gates_b)
     gate_shape = shape(igate.shape, f32)
     gate_grads = pl.pallas_call(
         gates_kernel,

time: 18.5 us -> 18.2 us (0.984)
  waiting for transfers between devices: 3.11 us -> 2.39 us
  Pallas kernels: 6.62 us -> 7.21 us
  starting transfers between devices: 7.06 us -> 6.86 us
    ppermute x8, waiting for transfers between devices: 3.11 us -> 2.39 us  [swap(): return lax.ppermute(value, 'head', [(s, s ^ mask) for s in range(4)])]
    pallas_call x2 -> x5, Pallas kernels: 1.55 us -> 2.04 us  [the longest x4 1.38 us: cross(): pl.pallas_call(functools.partial(cross_kernel, chunk, sides, work, qk, vw...]
    ppermute x8, starting transfers between devices: 7.06 us -> 6.86 us  [swap(): return lax.ppermute(value, 'head', [(s, s ^ mask) for s in range(4)])]
  transfers between devices with their start and end apart: 8 -> 8, of which waited for: 2 -> 4; matrix products, arithmetic and copies ran while one was open for 0% -> 0% of each run, Pallas kernels for 27% -> 31%
where the time goes in v7:
time: 18.2 us; the launch traced here: 17.9 us
  Pallas kernels  7.21 us (40%)
  starting transfers between devices  6.86 us (38%)
  waiting for transfers between devices  2.39 us (13%)
  between operations  1.4 us (8%)
    ppermute x8, starting transfers between devices, swap(): return lax.ppermute(value, 'head', [(s, s ^ mask) for s in range(4)])  6.86 us
    ppermute x8, waiting for transfers between devices, swap(): return lax.ppermute(value, 'head', [(s, s ^ mask) for s in range(4)])  2.39 us
    pallas_call x4, Pallas kernels, cross(): pl.pallas_call(functools.partial(cross_kernel, chunk, sides, work, qk, vw...  1.38 us
    pallas_call x1, Pallas kernels, split_shards(): pl.pallas_call(more_kernel, out_shape=(shape((rows, 2 * width), bf16), sh...  1.2 us
    pallas_call x1, Pallas kernels, split_shards(): pl.pallas_call(rest_kernel, out_shape=(cross_shape, shape((2, rows, width...  1.01 us
    pallas_call x1, Pallas kernels, split_shards(): pl.pallas_call(pack_kernel, out_shape=(shape((rows, width + slots), bf16)...  0.94 us
    pallas_call x1, Pallas kernels, split_shards(): pl.pallas_call(merge_kernel, out_shape=out_shape + (gates_shape,), in_spe...  0.9 us
    pallas_call x1, Pallas kernels, split_shards(): pl.pallas_call(last_kernel, out_shape=out_shape + (gate_shape, gate_shape...  0.73 us
  transfers between devices with their start and end apart: 8, of which 4 were waited for; matrix products, arithmetic and copies ran while one was open for 0% of the time, Pallas kernels for 31%

profile of v7, /device:TPU:0, one launch (start us, length us, event | category | flops | bytes accessed | tf_op | source)
XLA Modules:
  0.0 17.9 jit_solution(5764743157693326962)
XLA Ops:
  0.6 0.9 %shard_map.118 = (bf16[32,1664]{1,0:T(8,128)(2,1)S(1)}, f32[4,128]{1,0:T(4,128)S(1)}) custom-call(bf16[32,2048]{1,0:T(8,128)(2,1)} %q_ref.5, bf16[32,2048]{1,0:T(8,128)(2,1)} %k_ref.5, bf16[32,4096]{1,0:T(8,128)(2,1)} %v_ref.5, bf16[32,4096]{1,0:T(8,128)(2,1)} %g_ref.5, f32[2,128]{1,0:T(2,128)} %ig_ref.1, f32[2,128]{1,0:T(2,128)} %fg_ref.1), custom_call_target="tpu_custom_call" | custom-call | tf_op jit(solution)/shard_map/pallas_call | solution.py:534
  1.6 3.0 %collective-permute-start.1 = (bf16[32,1664]{1,0:T(8,128)(2,1)S(1)}, bf16[32,1664]{1,0:T(8,128)(2,1)S(1)}, u32[]{:S(2)}, u32[]{:S(2)}) collective-permute-start(bf16[32,1664]{1,0:T(8,128)(2,1)S(1)} %get-tuple-element.39.a2_ref), channel_id=1, source_target_pairs={{0,2},{1,3},{2,0},{3,1},{4,6},{5,7},{6,4},{7,5},{8,10},{9,11},{10,... | collective-permute-start | bytes 319496 | tf_op jit(solution)/shard_map/ppermute | solution.py:528
  4.6 1.2 %shard_map.120 = (bf16[32,3072]{1,0:T(8,128)(2,1)S(1)}, bf16[32,6144]{1,0:T(8,128)(2,1)S(1)}) custom-call(bf16[32,2048]{1,0:T(8,128)(2,1)} %q_ref.5, bf16[32,2048]{1,0:T(8,128)(2,1)} %k_ref.5, bf16[32,4096]{1,0:T(8,128)(2,1)} %v_ref.5, bf16[32,4096]{1,0:T(8,128)(2,1)} %g_ref.5), custom_call_target="tpu_custom_call" | custom-call | tf_op jit(solution)/shard_map/pallas_call | solution.py:543
  5.8 0.1 collective-permute-start.3
  5.9 0.2 collective-permute-start
  6.0 1.0 %shard_map.119 = (bf16[32,1536]{1,0:T(8,128)(2,1)S(1)}, bf16[2,32,1536]{2,1,0:T(8,128)(2,1)S(1)}) custom-call(bf16[32,2048]{1,0:T(8,128)(2,1)} %q_ref.5, bf16[32,2048]{1,0:T(8,128)(2,1)} %k_ref.5, bf16[32,4096]{1,0:T(8,128)(2,1)} %v_ref.5, bf16[32,4096]{1,0:T(8,128)(2,1)} %g_ref.5), custom_call_target="tpu_custom_call" | custom-call | tf_op jit(solution)/shard_map/pallas_call | solution.py:551
  7.7 0.0 collective-permute-done.1.a2_got.same_ref
  7.7 0.0 collective-permute-done.m1_ref
  7.7 0.4 %shard_map.122 = (bf16[2,64,1536]{2,1,0:T(8,128)(2,1)S(1)}, bf16[2,64,1536]{2,1,0:T(8,128)(2,1)S(1)}, f32[8,128]{1,0:T(8,128)S(1)}) custom-call(s32[1]{0:T(128)S(6)} %copy.21.length_ref, bf16[32,1664]{1,0:T(8,128)(2,1)S(1)} %get-tuple-element.39.a2_ref, bf16[32,1536]{1,0:T(8,128)(2,1)S(1)} %get-tuple-element.40.b2_ref, ...), custom_call_target="tpu_custom_call" | custom-call | flops 40000000000 | tf_op jit(solution)/shard_map/pallas_call | solution.py:570
  8.1 2.2 %collective-permute-start.4 = (f32[8,128]{1,0:T(8,128)S(1)}, f32[8,128]{1,0:T(8,128)S(1)}, u32[]{:S(2)}, u32[]{:S(2)}) collective-permute-start(f32[8,128]{1,0:T(8,128)S(1)} %get-tuple-element.48), channel_id=1, source_target_pairs={{0,2},{1,3},{2,0},{3,1},{4,6},{5,7},{6,4},{7,5},{8,10},{9,11},{10,... | collective-permute-start | bytes 12296 | tf_op jit(solution)/shard_map/ppermute | solution.py:528
  10.3 0.1 collective-permute-start.2
  10.4 0.7 %shard_map.123 = (f32[4,128]{1,0:T(4,128)S(1)}, bf16[64,1536]{1,0:T(8,128)(2,1)S(1)}, f32[64,1536]{1,0:T(8,128)S(1)}) custom-call(s32[1]{0:T(128)S(6)} %copy.21.length_ref, bf16[2,64,1536]{2,1,0:T(8,128)(2,1)S(1)} %get-tuple-element.44.qg_ref, bf16[2,64,1536]{2,1,0:T(8,128)(2,1)S(1)} %get-tuple-element.45.kv_ref, f32[4,128]{1,0:T(4,128)S(1)} %shard_map.121.got_ref), custom_call_target="tpu_custom_call" | custom-call | tf_op jit(solution)/shard_map/pallas_call | solution.py:596
  11.0 1.8 %collective-permute-done.3.other_ref = bf16[32,3072]{1,0:T(8,128)(2,1)S(1)} collective-permute-done((bf16[32,3072]{1,0:T(8,128)(2,1)S(1)}, bf16[32,3072]{1,0:T(8,128)(2,1)S(1)}, u32[]{:S(2)}, u32[]{:S(2)}) %collective-permute-start.3) | collective-permute-done | bytes 196640 | tf_op jit(solution)/shard_map/ppermute | solution.py:528
  12.8 0.8 %collective-permute-start.6 = (f32[4,128]{1,0:T(4,128)S(1)}, f32[4,128]{1,0:T(4,128)S(1)}, u32[]{:S(2)}, u32[]{:S(2)}) collective-permute-start(f32[4,128]{1,0:T(4,128)S(1)} %shard_map.126.refs_0_), channel_id=1, source_target_pairs={{0,2},{1,3},{2,0},{3,1},{4,6},{5,7},{6,4},{7,5},{8,10},{9,11},{10,... | collective-permute-start | bytes 6152 | tf_op jit(solution)/shard_map/ppermute | solution.py:528
  13.7 0.8 %shard_map.128 = (bf16[64,3072]{1,0:T(8,128)(2,1)S(1)}, bf16[32,3072]{1,0:T(8,128)(2,1)S(1)}, f32[4,128]{1,0:T(4,128)S(1)}) custom-call(s32[1]{0:T(128)S(6)} %copy.21.length_ref, bf16[2,64,1536]{2,1,0:T(8,128)(2,1)S(1)} %get-tuple-element.44.qg_ref, bf16[2,64,1536]{2,1,0:T(8,128)(2,1)S(1)} %get-tuple-element.45.kv_ref, ...), custom_call_target="tpu_custom_call" | custom-call | flops 40000000000 | tf_op jit(solution)/shard_map/pallas_call | solution.py:586
  14.4 0.5 %collective-permute-start.7 = (bf16[32,3072]{1,0:T(8,128)(2,1)S(1)}, bf16[32,3072]{1,0:T(8,128)(2,1)S(1)}, u32[]{:S(2)}, u32[]{:S(2)}) collective-permute-start(bf16[32,3072]{1,0:T(8,128)(2,1)S(1)} %get-tuple-element.57), channel_id=1, source_target_pairs={{0,1},{1,0},{2,3},{3,2},{4,5},{5,4},{6,7},{7,6},{8,9},{9,8},{10,11... | collective-permute-start | bytes 589832 | tf_op jit(solution)/shard_map/ppermute | solution.py:528
  14.9 0.1 collective-permute-done.2.same_ref
  15.0 0.6 %shard_map.124 = (bf16[64,3072]{1,0:T(8,128)(2,1)S(1)}, bf16[32,3072]{1,0:T(8,128)(2,1)S(1)}, f32[4,128]{1,0:T(4,128)S(1)}) custom-call(s32[1]{0:T(128)S(6)} %copy.21.length_ref, bf16[2,64,1536]{2,1,0:T(8,128)(2,1)S(1)} %get-tuple-element.44.qg_ref, bf16[2,64,1536]{2,1,0:T(8,128)(2,1)S(1)} %get-tuple-element.45.kv_ref, ...), custom_call_target="tpu_custom_call" | custom-call | flops 4000000000 | tf_op jit(solution)/shard_map/pallas_call | solution.py:586
  15.6 0.1 collective-permute-start.5
  15.7 0.3 %collective-permute-done.7.got_a = bf16[32,3072]{1,0:T(8,128)(2,1)S(1)} collective-permute-done((bf16[32,3072]{1,0:T(8,128)(2,1)S(1)}, bf16[32,3072]{1,0:T(8,128)(2,1)S(1)}, u32[]{:S(2)}, u32[]{:S(2)}) %collective-permute-start.7) | collective-permute-done | bytes 196640 | tf_op jit(solution)/shard_map/ppermute | solution.py:528
  16.0 0.9 %shard_map.129 = (bf16[32,2048]{1,0:T(8,128)(2,1)}, bf16[32,2048]{1,0:T(8,128)(2,1)}, bf16[32,4096]{1,0:T(8,128)(2,1)}, bf16[32,4096]{1,0:T(8,128)(2,1)}, f32[4,128]{1,0:T(4,128)S(1)}) custom-call(bf16[64,3072]{1,0:T(8,128)(2,1)S(1)} %get-tuple-element.55.result_a, bf16[64,3072]{1,0:T(8,128)(2,1)S(1)} %get-tuple-element.56.result_b, ...), custom_call_target="tpu_custom_call" | custom-call | tf_op jit(solution)/shard_map/pallas_call | solution.py:619
  16.9 0.0 collective-permute-done.6.gates_got
  16.9 0.2 %collective-permute-done.5.got_b = bf16[32,3072]{1,0:T(8,128)(2,1)S(1)} collective-permute-done((bf16[32,3072]{1,0:T(8,128)(2,1)S(1)}, bf16[32,3072]{1,0:T(8,128)(2,1)S(1)}, u32[]{:S(2)}, u32[]{:S(2)}) %collective-permute-start.5) | collective-permute-done | bytes 196640 | tf_op jit(solution)/shard_map/ppermute | solution.py:528
  17.1 0.7 %shard_map.131 = (bf16[32,2048]{1,0:T(8,128)(2,1)}, bf16[32,2048]{1,0:T(8,128)(2,1)}, bf16[32,4096]{1,0:T(8,128)(2,1)}, bf16[32,4096]{1,0:T(8,128)(2,1)}, f32[2,128]{1,0:T(2,128)}, /*index=5*/f32[2,128]{1,0:T(2,128)}) custom-call(bf16[32,3072]{1,0:T(8,128)(2,1)S(1)} %collective-permute-done.5, ...), custom_call_target="tpu_custom_call", output_to_operand_aliasing={{0}: (3, {}), {1}: (4, {}), {2}: (5, {}), {3}: (6, {})} | custom-call | tf_op jit(solution)/shard_map/pallas_call | solution.py:637
  (6 shorter events, 0.0 us)
Async XLA Ops:
  1.6 6.1 %collective-permute-start.1 = (bf16[32,1664]{1,0:T(8,128)(2,1)S(1)}, bf16[32,1664]{1,0:T(8,128)(2,1)S(1)}, u32[]{:S(2)}, u32[]{:S(2)}) collective-permute-start(bf16[32,1664]{1,0:T(8,128)(2,1)S(1)} %get-tuple-element.39.a2_ref), channel_id=1, source_target_pairs={{0,2},{1,3},{2,0},{3,1},{4,6},{5,7},{6,4},{7,5},{8,10},{9,11},{10,... | collective-permute-start | bytes 319496 | tf_op jit(solution)/shard_map/ppermute | solution.py:528
  5.8 7.0 %collective-permute-start.3 = (bf16[32,3072]{1,0:T(8,128)(2,1)S(1)}, bf16[32,3072]{1,0:T(8,128)(2,1)S(1)}, u32[]{:S(2)}, u32[]{:S(2)}) collective-permute-start(bf16[32,3072]{1,0:T(8,128)(2,1)S(1)} %get-tuple-element.47), channel_id=1, source_target_pairs={{0,3},{1,2},{2,1},{3,0},{4,7},{5,6},{6,5},{7,4},{8,11},{9,10},{10,... | collective-permute-start | bytes 589832 | tf_op jit(solution)/shard_map/ppermute | solution.py:528
  5.9 1.8 %collective-permute-start = (bf16[32,6144]{1,0:T(8,128)(2,1)S(1)}, bf16[32,6144]{1,0:T(8,128)(2,1)S(1)}, u32[]{:S(2)}, u32[]{:S(2)}) collective-permute-start(bf16[32,6144]{1,0:T(8,128)(2,1)S(1)} %get-tuple-element.42), channel_id=1, source_target_pairs={{0,1},{1,0},{2,3},{3,2},{4,5},{5,4},{6,7},{7,6},{8,9},{9,8},{10,11... | collective-permute-start | bytes 1179656 | tf_op jit(solution)/shard_map/ppermute | solution.py:528
  8.1 5.6 %collective-permute-start.4 = (f32[8,128]{1,0:T(8,128)S(1)}, f32[8,128]{1,0:T(8,128)S(1)}, u32[]{:S(2)}, u32[]{:S(2)}) collective-permute-start(f32[8,128]{1,0:T(8,128)S(1)} %get-tuple-element.48), channel_id=1, source_target_pairs={{0,2},{1,3},{2,0},{3,1},{4,6},{5,7},{6,4},{7,5},{8,10},{9,11},{10,... | collective-permute-start | bytes 12296 | tf_op jit(solution)/shard_map/ppermute | solution.py:528
  10.3 4.7 %collective-permute-start.2 = (bf16[32,1536]{1,0:T(8,128)(2,1)S(1)}, bf16[32,1536]{1,0:T(8,128)(2,1)S(1)}, u32[]{:S(2)}, u32[]{:S(2)}) collective-permute-start(bf16[32,1536]{1,0:T(8,128)(2,1)S(1)} %get-tuple-element.40.b2_ref), channel_id=1, source_target_pairs={{0,2},{1,3},{2,0},{3,1},{4,6},{5,7},{6,4},{7,5},{8,10},{9,11},{10,... | collective-permute-start | bytes 294920 | tf_op jit(solution)/shard_map/ppermute | solution.py:528
  12.8 4.0 %collective-permute-start.6 = (f32[4,128]{1,0:T(4,128)S(1)}, f32[4,128]{1,0:T(4,128)S(1)}, u32[]{:S(2)}, u32[]{:S(2)}) collective-permute-start(f32[4,128]{1,0:T(4,128)S(1)} %shard_map.126.refs_0_), channel_id=1, source_target_pairs={{0,2},{1,3},{2,0},{3,1},{4,6},{5,7},{6,4},{7,5},{8,10},{9,11},{10,... | collective-permute-start | bytes 6152 | tf_op jit(solution)/shard_map/ppermute | solution.py:528
  14.4 1.6 %collective-permute-start.7 = (bf16[32,3072]{1,0:T(8,128)(2,1)S(1)}, bf16[32,3072]{1,0:T(8,128)(2,1)S(1)}, u32[]{:S(2)}, u32[]{:S(2)}) collective-permute-start(bf16[32,3072]{1,0:T(8,128)(2,1)S(1)} %get-tuple-element.57), channel_id=1, source_target_pairs={{0,1},{1,0},{2,3},{3,2},{4,5},{5,4},{6,7},{7,6},{8,9},{9,8},{10,11... | collective-permute-start | bytes 589832 | tf_op jit(solution)/shard_map/ppermute | solution.py:528
  15.6 1.5 %collective-permute-start.5 = (bf16[32,3072]{1,0:T(8,128)(2,1)S(1)}, bf16[32,3072]{1,0:T(8,128)(2,1)S(1)}, u32[]{:S(2)}, u32[]{:S(2)}) collective-permute-start(bf16[32,3072]{1,0:T(8,128)(2,1)S(1)} %get-tuple-element.51), channel_id=1, source_target_pairs={{0,1},{1,0},{2,3},{3,2},{4,5},{5,4},{6,7},{7,6},{8,9},{9,8},{10,11... | collective-permute-start | bytes 589832 | tf_op jit(solution)/shard_map/ppermute | solution.py:528

commit v8 on v7

--- a/solution.py
+++ b/solution.py
@@ -191,7 +191,7 @@
         copy.wait()
 
 
-def more_kernel(q_ref, k_ref, v_ref, g_ref, d_ref, m1_ref, sems):
+def more_kernel(q_ref, k_ref, v_ref, g_ref, d_ref, m1_ref, b2_ref, sems):
     core = place()[1]
     width = m1_ref.shape[1] // 4
 
@@ -202,18 +202,17 @@
             for i, refs in enumerate((sent, kept)):
                 start = (2 * chunk + i) * width
                 pairs += block_copies(refs, 2 * chunk + 1 - core, m1_ref.at[:, start : start + width])
-        return pairs
+        return pairs + block_copies(sent, 2 + core, b2_ref)
 
     for copy in copy_for_chip(moves, (q_ref, k_ref, v_ref, g_ref), sems):
         copy.wait()
 
 
-def rest_kernel(q_ref, k_ref, v_ref, g_ref, b2_ref, rest_ref, sems):
+def rest_kernel(q_ref, k_ref, v_ref, g_ref, rest_ref, sems):
     core = place()[1]
 
     def moves(sent, kept):
-        pairs = block_copies(sent, 2 + core, b2_ref)
-        return pairs + block_copies(kept, core, rest_ref.at[0]) + block_copies(kept, 2 + core, rest_ref.at[1])
+        return block_copies(kept, core, rest_ref.at[0]) + block_copies(kept, 2 + core, rest_ref.at[1])
 
     for copy in copy_for_chip(moves, (q_ref, k_ref, v_ref, g_ref), sems):
         copy.wait()
@@ -540,20 +539,20 @@
         compiler_params=params,
     )(*arrays)
     a2 = swap(a2_sent, 2)
-    d, to_core = pl.pallas_call(
+    d, to_core, b2_sent = pl.pallas_call(
         more_kernel,
-        out_shape=(shape((rows, 2 * width), bf16), shape((rows, 4 * width), bf16)),
+        out_shape=(shape((rows, 2 * width), bf16), shape((rows, 4 * width), bf16), cross_shape),
         in_specs=[hbm] * 4,
-        out_specs=(vmem,) * 2,
-        scratch_shapes=[dma((12,))],
+        out_specs=(vmem,) * 3,
+        scratch_shapes=[dma((14,))],
         compiler_params=params,
     )(*arrays[:4])
-    b2_sent, rest = pl.pallas_call(
+    rest = pl.pallas_call(
         rest_kernel,
-        out_shape=(cross_shape, shape((2, rows, width), bf16)),
+        out_shape=shape((2, rows, width), bf16),
         in_specs=[hbm] * 4,
-        out_specs=(vmem,) * 2,
-        scratch_shapes=[dma((6,))],
+        out_specs=vmem,
+        scratch_shapes=[dma((4,))],
         compiler_params=params,
     )(*arrays[:4])
     from_core = swap(to_core, 1)

time: 18.2 us -> 18.2 us (level)
  waiting for transfers between devices: 2.39 us -> 2.6 us
    ppermute x8, waiting for transfers between devices: 2.39 us -> 2.6 us  [swap(): return lax.ppermute(value, 'head', [(s, s ^ mask) for s in range(4)])]
where the time goes in v8:
time: 18.2 us; the launch traced here: 17.9 us
  Pallas kernels  7.2 us (40%)
  starting transfers between devices  6.72 us (37%)
  waiting for transfers between devices  2.6 us (14%)
  between operations  1.39 us (8%)
    ppermute x8, starting transfers between devices, swap(): return lax.ppermute(value, 'head', [(s, s ^ mask) for s in range(4)])  6.72 us
    ppermute x8, waiting for transfers between devices, swap(): return lax.ppermute(value, 'head', [(s, s ^ mask) for s in range(4)])  2.6 us
    pallas_call x4, Pallas kernels, cross(): pl.pallas_call(functools.partial(cross_kernel, chunk, sides, work, qk, vw...  1.38 us
    pallas_call x1, Pallas kernels, split_shards(): pl.pallas_call(more_kernel, out_shape=(shape((rows, 2 * width), bf16), sh...  1.25 us
    pallas_call x1, Pallas kernels, split_shards(): pl.pallas_call(rest_kernel, out_shape=shape((2, rows, width), bf16), in_s...  0.94 us
    pallas_call x1, Pallas kernels, split_shards(): pl.pallas_call(pack_kernel, out_shape=(shape((rows, width + slots), bf16)...  0.94 us
    pallas_call x1, Pallas kernels, split_shards(): pl.pallas_call(merge_kernel, out_shape=out_shape + (gates_shape,), in_spe...  0.9 us
    pallas_call x1, Pallas kernels, split_shards(): pl.pallas_call(last_kernel, out_shape=out_shape + (gate_shape, gate_shape...  0.73 us
  transfers between devices with their start and end apart: 8, of which 4 were waited for; matrix products, arithmetic and copies ran while one was open for 0% of the time, Pallas kernels for 31%

profile of v8, /device:TPU:0, one launch (start us, length us, event | category | flops | bytes accessed | tf_op | source)
XLA Modules:
  0.0 17.9 jit_solution(2292030190506405777)
XLA Ops:
  0.6 0.9 %shard_map.118 = (bf16[32,1664]{1,0:T(8,128)(2,1)S(1)}, f32[4,128]{1,0:T(4,128)S(1)}) custom-call(bf16[32,2048]{1,0:T(8,128)(2,1)} %q_ref.5, bf16[32,2048]{1,0:T(8,128)(2,1)} %k_ref.5, bf16[32,4096]{1,0:T(8,128)(2,1)} %v_ref.5, bf16[32,4096]{1,0:T(8,128)(2,1)} %g_ref.5, f32[2,128]{1,0:T(2,128)} %ig_ref.1, f32[2,128]{1,0:T(2,128)} %fg_ref.1), custom_call_target="tpu_custom_call" | custom-call | tf_op jit(solution)/shard_map/pallas_call | solution.py:533
  1.6 3.0 %collective-permute-start.1 = (bf16[32,1664]{1,0:T(8,128)(2,1)S(1)}, bf16[32,1664]{1,0:T(8,128)(2,1)S(1)}, u32[]{:S(2)}, u32[]{:S(2)}) collective-permute-start(bf16[32,1664]{1,0:T(8,128)(2,1)S(1)} %get-tuple-element.38.a2_ref), channel_id=1, source_target_pairs={{0,2},{1,3},{2,0},{3,1},{4,6},{5,7},{6,4},{7,5},{8,10},{9,11},{10,... | collective-permute-start | bytes 319496 | tf_op jit(solution)/shard_map/ppermute | solution.py:527
  4.6 1.3 %shard_map.119 = (bf16[32,3072]{1,0:T(8,128)(2,1)S(1)}, bf16[32,6144]{1,0:T(8,128)(2,1)S(1)}, bf16[32,1536]{1,0:T(8,128)(2,1)S(1)}) custom-call(bf16[32,2048]{1,0:T(8,128)(2,1)} %q_ref.5, bf16[32,2048]{1,0:T(8,128)(2,1)} %k_ref.5, bf16[32,4096]{1,0:T(8,128)(2,1)} %v_ref.5, bf16[32,4096]{1,0:T(8,128)(2,1)} %g_ref.5), custom_call_target="tpu_custom_call" | custom-call | tf_op jit(solution)/shard_map/pallas_call | solution.py:542
  5.8 0.1 collective-permute-start.3
  5.9 0.2 collective-permute-start
  6.1 0.9 %shard_map.120.rest_ref = bf16[2,32,1536]{2,1,0:T(8,128)(2,1)S(1)} custom-call(bf16[32,2048]{1,0:T(8,128)(2,1)} %q_ref.5, bf16[32,2048]{1,0:T(8,128)(2,1)} %k_ref.5, bf16[32,4096]{1,0:T(8,128)(2,1)} %v_ref.5, bf16[32,4096]{1,0:T(8,128)(2,1)} %g_ref.5), custom_call_target="tpu_custom_call" | custom-call | tf_op jit(solution)/shard_map/pallas_call | solution.py:550
  7.7 0.0 collective-permute-done.1.a2_got.same_ref
  7.7 0.0 collective-permute-done.m1_ref
  7.7 0.4 %shard_map.122 = (bf16[2,64,1536]{2,1,0:T(8,128)(2,1)S(1)}, bf16[2,64,1536]{2,1,0:T(8,128)(2,1)S(1)}, f32[8,128]{1,0:T(8,128)S(1)}) custom-call(s32[1]{0:T(128)S(6)} %copy.21.length_ref, bf16[32,1664]{1,0:T(8,128)(2,1)S(1)} %get-tuple-element.38.a2_ref, bf16[32,1536]{1,0:T(8,128)(2,1)S(1)} %get-tuple-element.39.b2_ref, ...), custom_call_target="tpu_custom_call" | custom-call | flops 40000000000 | tf_op jit(solution)/shard_map/pallas_call | solution.py:569
  8.1 2.2 %collective-permute-start.4 = (f32[8,128]{1,0:T(8,128)S(1)}, f32[8,128]{1,0:T(8,128)S(1)}, u32[]{:S(2)}, u32[]{:S(2)}) collective-permute-start(f32[8,128]{1,0:T(8,128)S(1)} %get-tuple-element.46), channel_id=1, source_target_pairs={{0,2},{1,3},{2,0},{3,1},{4,6},{5,7},{6,4},{7,5},{8,10},{9,11},{10,... | collective-permute-start | bytes 12296 | tf_op jit(solution)/shard_map/ppermute | solution.py:527
  10.3 0.1 collective-permute-start.2
  10.3 0.7 %shard_map.123 = (f32[4,128]{1,0:T(4,128)S(1)}, bf16[64,1536]{1,0:T(8,128)(2,1)S(1)}, f32[64,1536]{1,0:T(8,128)S(1)}) custom-call(s32[1]{0:T(128)S(6)} %copy.21.length_ref, bf16[2,64,1536]{2,1,0:T(8,128)(2,1)S(1)} %get-tuple-element.42.qg_ref, bf16[2,64,1536]{2,1,0:T(8,128)(2,1)S(1)} %get-tuple-element.43.kv_ref, f32[4,128]{1,0:T(4,128)S(1)} %shard_map.121.got_ref), custom_call_target="tpu_custom_call" | custom-call | tf_op jit(solution)/shard_map/pallas_call | solution.py:595
  11.0 1.9 %collective-permute-done.3.other_ref = bf16[32,3072]{1,0:T(8,128)(2,1)S(1)} collective-permute-done((bf16[32,3072]{1,0:T(8,128)(2,1)S(1)}, bf16[32,3072]{1,0:T(8,128)(2,1)S(1)}, u32[]{:S(2)}, u32[]{:S(2)}) %collective-permute-start.3) | collective-permute-done | bytes 196640 | tf_op jit(solution)/shard_map/ppermute | solution.py:527
  12.9 0.8 %collective-permute-start.6 = (f32[4,128]{1,0:T(4,128)S(1)}, f32[4,128]{1,0:T(4,128)S(1)}, u32[]{:S(2)}, u32[]{:S(2)}) collective-permute-start(f32[4,128]{1,0:T(4,128)S(1)} %shard_map.126.refs_0_), channel_id=1, source_target_pairs={{0,2},{1,3},{2,0},{3,1},{4,6},{5,7},{6,4},{7,5},{8,10},{9,11},{10,... | collective-permute-start | bytes 6152 | tf_op jit(solution)/shard_map/ppermute | solution.py:527
  13.7 0.8 %shard_map.128 = (bf16[64,3072]{1,0:T(8,128)(2,1)S(1)}, bf16[32,3072]{1,0:T(8,128)(2,1)S(1)}, f32[4,128]{1,0:T(4,128)S(1)}) custom-call(s32[1]{0:T(128)S(6)} %copy.21.length_ref, bf16[2,64,1536]{2,1,0:T(8,128)(2,1)S(1)} %get-tuple-element.42.qg_ref, bf16[2,64,1536]{2,1,0:T(8,128)(2,1)S(1)} %get-tuple-element.43.kv_ref, ...), custom_call_target="tpu_custom_call" | custom-call | flops 40000000000 | tf_op jit(solution)/shard_map/pallas_call | solution.py:585
  14.5 0.3 %collective-permute-start.7 = (bf16[32,3072]{1,0:T(8,128)(2,1)S(1)}, bf16[32,3072]{1,0:T(8,128)(2,1)S(1)}, u32[]{:S(2)}, u32[]{:S(2)}) collective-permute-start(bf16[32,3072]{1,0:T(8,128)(2,1)S(1)} %get-tuple-element.55), channel_id=1, source_target_pairs={{0,1},{1,0},{2,3},{3,2},{4,5},{5,4},{6,7},{7,6},{8,9},{9,8},{10,11... | collective-permute-start | bytes 589832 | tf_op jit(solution)/shard_map/ppermute | solution.py:527
  14.8 0.2 %collective-permute-done.2.same_ref = bf16[32,1536]{1,0:T(8,128)(2,1)S(1)} collective-permute-done((bf16[32,1536]{1,0:T(8,128)(2,1)S(1)}, bf16[32,1536]{1,0:T(8,128)(2,1)S(1)}, u32[]{:S(2)}, u32[]{:S(2)}) %collective-permute-start.2) | collective-permute-done | bytes 98336 | tf_op jit(solution)/shard_map/ppermute | solution.py:527
  15.0 0.6 %shard_map.124 = (bf16[64,3072]{1,0:T(8,128)(2,1)S(1)}, bf16[32,3072]{1,0:T(8,128)(2,1)S(1)}, f32[4,128]{1,0:T(4,128)S(1)}) custom-call(s32[1]{0:T(128)S(6)} %copy.21.length_ref, bf16[2,64,1536]{2,1,0:T(8,128)(2,1)S(1)} %get-tuple-element.42.qg_ref, bf16[2,64,1536]{2,1,0:T(8,128)(2,1)S(1)} %get-tuple-element.43.kv_ref, ...), custom_call_target="tpu_custom_call" | custom-call | flops 4000000000 | tf_op jit(solution)/shard_map/pallas_call | solution.py:585
  15.7 0.1 collective-permute-start.5
  15.8 0.2 %collective-permute-done.7.got_a = bf16[32,3072]{1,0:T(8,128)(2,1)S(1)} collective-permute-done((bf16[32,3072]{1,0:T(8,128)(2,1)S(1)}, bf16[32,3072]{1,0:T(8,128)(2,1)S(1)}, u32[]{:S(2)}, u32[]{:S(2)}) %collective-permute-start.7) | collective-permute-done | bytes 196640 | tf_op jit(solution)/shard_map/ppermute | solution.py:527
  16.0 0.9 %shard_map.129 = (bf16[32,2048]{1,0:T(8,128)(2,1)}, bf16[32,2048]{1,0:T(8,128)(2,1)}, bf16[32,4096]{1,0:T(8,128)(2,1)}, bf16[32,4096]{1,0:T(8,128)(2,1)}, f32[4,128]{1,0:T(4,128)S(1)}) custom-call(bf16[64,3072]{1,0:T(8,128)(2,1)S(1)} %get-tuple-element.53.result_a, bf16[64,3072]{1,0:T(8,128)(2,1)S(1)} %get-tuple-element.54.result_b, ...), custom_call_target="tpu_custom_call" | custom-call | tf_op jit(solution)/shard_map/pallas_call | solution.py:618
  16.9 0.0 collective-permute-done.6.gates_got
  16.9 0.2 %collective-permute-done.5.got_b = bf16[32,3072]{1,0:T(8,128)(2,1)S(1)} collective-permute-done((bf16[32,3072]{1,0:T(8,128)(2,1)S(1)}, bf16[32,3072]{1,0:T(8,128)(2,1)S(1)}, u32[]{:S(2)}, u32[]{:S(2)}) %collective-permute-start.5) | collective-permute-done | bytes 196640 | tf_op jit(solution)/shard_map/ppermute | solution.py:527
  17.2 0.7 %shard_map.131 = (bf16[32,2048]{1,0:T(8,128)(2,1)}, bf16[32,2048]{1,0:T(8,128)(2,1)}, bf16[32,4096]{1,0:T(8,128)(2,1)}, bf16[32,4096]{1,0:T(8,128)(2,1)}, f32[2,128]{1,0:T(2,128)}, /*index=5*/f32[2,128]{1,0:T(2,128)}) custom-call(bf16[32,3072]{1,0:T(8,128)(2,1)S(1)} %collective-permute-done.5, ...), custom_call_target="tpu_custom_call", output_to_operand_aliasing={{0}: (3, {}), {1}: (4, {}), {2}: (5, {}), {3}: (6, {})} | custom-call | tf_op jit(solution)/shard_map/pallas_call | solution.py:636
  (6 shorter events, 0.0 us)
Async XLA Ops:
  1.6 6.1 %collective-permute-start.1 = (bf16[32,1664]{1,0:T(8,128)(2,1)S(1)}, bf16[32,1664]{1,0:T(8,128)(2,1)S(1)}, u32[]{:S(2)}, u32[]{:S(2)}) collective-permute-start(bf16[32,1664]{1,0:T(8,128)(2,1)S(1)} %get-tuple-element.38.a2_ref), channel_id=1, source_target_pairs={{0,2},{1,3},{2,0},{3,1},{4,6},{5,7},{6,4},{7,5},{8,10},{9,11},{10,... | collective-permute-start | bytes 319496 | tf_op jit(solution)/shard_map/ppermute | solution.py:527
  5.8 7.0 %collective-permute-start.3 = (bf16[32,3072]{1,0:T(8,128)(2,1)S(1)}, bf16[32,3072]{1,0:T(8,128)(2,1)S(1)}, u32[]{:S(2)}, u32[]{:S(2)}) collective-permute-start(bf16[32,3072]{1,0:T(8,128)(2,1)S(1)} %get-tuple-element.45), channel_id=1, source_target_pairs={{0,3},{1,2},{2,1},{3,0},{4,7},{5,6},{6,5},{7,4},{8,11},{9,10},{10,... | collective-permute-start | bytes 589832 | tf_op jit(solution)/shard_map/ppermute | solution.py:527
  5.9 1.8 %collective-permute-start = (bf16[32,6144]{1,0:T(8,128)(2,1)S(1)}, bf16[32,6144]{1,0:T(8,128)(2,1)S(1)}, u32[]{:S(2)}, u32[]{:S(2)}) collective-permute-start(bf16[32,6144]{1,0:T(8,128)(2,1)S(1)} %get-tuple-element.40), channel_id=1, source_target_pairs={{0,1},{1,0},{2,3},{3,2},{4,5},{5,4},{6,7},{7,6},{8,9},{9,8},{10,11... | collective-permute-start | bytes 1179656 | tf_op jit(solution)/shard_map/ppermute | solution.py:527
  8.1 5.6 %collective-permute-start.4 = (f32[8,128]{1,0:T(8,128)S(1)}, f32[8,128]{1,0:T(8,128)S(1)}, u32[]{:S(2)}, u32[]{:S(2)}) collective-permute-start(f32[8,128]{1,0:T(8,128)S(1)} %get-tuple-element.46), channel_id=1, source_target_pairs={{0,2},{1,3},{2,0},{3,1},{4,6},{5,7},{6,4},{7,5},{8,10},{9,11},{10,... | collective-permute-start | bytes 12296 | tf_op jit(solution)/shard_map/ppermute | solution.py:527
  10.3 4.8 %collective-permute-start.2 = (bf16[32,1536]{1,0:T(8,128)(2,1)S(1)}, bf16[32,1536]{1,0:T(8,128)(2,1)S(1)}, u32[]{:S(2)}, u32[]{:S(2)}) collective-permute-start(bf16[32,1536]{1,0:T(8,128)(2,1)S(1)} %get-tuple-element.39.b2_ref), channel_id=1, source_target_pairs={{0,2},{1,3},{2,0},{3,1},{4,6},{5,7},{6,4},{7,5},{8,10},{9,11},{10,... | collective-permute-start | bytes 294920 | tf_op jit(solution)/shard_map/ppermute | solution.py:527
  12.9 4.0 %collective-permute-start.6 = (f32[4,128]{1,0:T(4,128)S(1)}, f32[4,128]{1,0:T(4,128)S(1)}, u32[]{:S(2)}, u32[]{:S(2)}) collective-permute-start(f32[4,128]{1,0:T(4,128)S(1)} %shard_map.126.refs_0_), channel_id=1, source_target_pairs={{0,2},{1,3},{2,0},{3,1},{4,6},{5,7},{6,4},{7,5},{8,10},{9,11},{10,... | collective-permute-start | bytes 6152 | tf_op jit(solution)/shard_map/ppermute | solution.py:527
  14.5 1.5 %collective-permute-start.7 = (bf16[32,3072]{1,0:T(8,128)(2,1)S(1)}, bf16[32,3072]{1,0:T(8,128)(2,1)S(1)}, u32[]{:S(2)}, u32[]{:S(2)}) collective-permute-start(bf16[32,3072]{1,0:T(8,128)(2,1)S(1)} %get-tuple-element.55), channel_id=1, source_target_pairs={{0,1},{1,0},{2,3},{3,2},{4,5},{5,4},{6,7},{7,6},{8,9},{9,8},{10,11... | collective-permute-start | bytes 589832 | tf_op jit(solution)/shard_map/ppermute | solution.py:527
  15.7 1.5 %collective-permute-start.5 = (bf16[32,3072]{1,0:T(8,128)(2,1)S(1)}, bf16[32,3072]{1,0:T(8,128)(2,1)S(1)}, u32[]{:S(2)}, u32[]{:S(2)}) collective-permute-start(bf16[32,3072]{1,0:T(8,128)(2,1)S(1)} %get-tuple-element.49), channel_id=1, source_target_pairs={{0,1},{1,0},{2,3},{3,2},{4,5},{5,4},{6,7},{7,6},{8,9},{9,8},{10,11... | collective-permute-start | bytes 589832 | tf_op jit(solution)/shard_map/ppermute | solution.py:527
